TPU v7x, 32 devices: a whole 2x2x4 slice. The times are simulated.
32 devices in a mesh: dp: 16 (over z, x, core), tensor: 2 (over y).
Axes of the slice: x: 2, y: 2, z: 4, core: 2. Of those that a mesh axis runs over, the one named last changes fastest.
Arguments:
- content_in: bfloat16 [32, 512, 768], P('dp'), may hold values from -6 to 6
- query_in: bfloat16 [32, 512, 768], P('dp'), may hold values from -6 to 6
- lengths: int32 [32], P('dp'), may hold values from 1 to 512, 9830 in all
- factor_order: int32 [32, 512], P('dp'), may hold values from 0 to 511, each once within a row
- buckets: int32 [32, 512, 512], P('dp'), may hold values from 0 to 31
- w_qkv: bfloat16 [3, 768, 768], P(None, 'dp', 'tensor'), may hold values from -0.21875 to 0.21875
- b_qv: bfloat16 [2, 768], P(None, 'tensor'), may hold values from -3 to 3
- w_out: bfloat16 [768, 768], P('tensor', 'dp'), may hold values from -1.75 to 1.75
- w_in: bfloat16 [768, 3072], P('dp', 'tensor'), may hold values from -0.21875 to 0.21875
- b_in: bfloat16 [3072], P('tensor'), may hold values from -3 to 3
- w_down: bfloat16 [3072, 768], P('tensor', 'dp'), may hold values from -0.109375 to 0.109375
- b_outs: bfloat16 [2, 768], replicated, may hold values from -2 to 2
- norm_gain: bfloat16 [2, 768], replicated, may hold values from 0.5 to 1.5
- norm_bias: bfloat16 [2, 768], replicated, may hold values from -2 to 2
- rel_table: bfloat16 [32, 12], P(None, 'tensor'), may hold values from -4 to 4
- cot_content: bfloat16 [32, 512, 768], P('dp'), may hold values from -6 to 6
- cot_query: bfloat16 [32, 512, 768], P('dp'), may hold values from -6 to 6
Outputs:
- out_content: bfloat16 [32, 512, 768], P('dp')
- out_query: bfloat16 [32, 512, 768], P('dp')
- grad_content: bfloat16 [32, 512, 768], P('dp', None, 'tensor')
- grad_query: bfloat16 [32, 512, 768], P('dp', None, 'tensor')
- grad_w_qkv: float32 [3, 768, 768], P(None, 'dp', 'tensor')
- grad_b_qv: float32 [2, 768], P(None, 'tensor')
- grad_w_out: float32 [768, 768], P('tensor', 'dp')
- grad_w_in: float32 [768, 3072], P('dp', 'tensor')
- grad_b_in: float32 [3072], P('tensor')
- grad_w_down: float32 [3072, 768], P('tensor', 'dp')
- grad_b_outs: float32 [2, 768], replicated
- grad_norm_gain: float32 [2, 768], replicated
- grad_norm_bias: float32 [2, 768], replicated
- grad_rel_table: float32 [32, 12], P(None, 'tensor')
Inputs may be any that keep to these rules, and one draw needn't show every extreme that they name: `lengths`: positions at or past a sequence's length are padding; some sequence uses all 512 slots. `factor_order`: each row is a permutation of the positions 0 to 511.
All inputs are finite; a program needn't handle non-finite values. No bound on the sum of `lengths` on one device may be relied on, other than what follows from the above.
Results may differ from a plain program's by a relative error of at most 0.019.
Values may be sent and summed in bfloat16 or wider, within the bound.
No kernel may reach another device: no remote copies, remote signals or barrier semaphores. Data moves between devices by JAX's collectives and lax.ppermute only.
A program may use at most 256 MiB of HBM per device.

v0:
```python
import functools

import jax
import jax.numpy as jnp
from jax import lax
from jax.experimental import pallas as pl
from jax.experimental.pallas import tpu as pltpu
from jax.sharding import Mesh, PartitionSpec as P

EPSILON = 1e-05


def cost(us):
    return pl.CostEstimate(flops=int(us * 1e7), bytes_accessed=int(us * 1e4), transcendentals=0)

NEG = -1e30
BF = jnp.bfloat16
F32 = jnp.float32


def dot(a, b, dims):
    return lax.dot_general(a, b, (dims, ((), ())), preferred_element_type=F32)


NN = ((1,), (0,))
NT = ((1,), (1,))
TN = ((0,), (0,))


def bias_kernel(len_ref, buckets_ref, rank_row_ref, rank_col_ref, table_ref, out_ref):
    rows, cols = buckets_ref.shape
    heads = table_ref.shape[0]
    start = pl.program_id(0) * rows
    key = start + lax.broadcasted_iota(jnp.int32, (rows, cols), 0)
    query = lax.broadcasted_iota(jnp.int32, (rows, cols), 1)
    valid = key < len_ref[0]
    rank_key = rank_col_ref[...]
    rank_query = rank_row_ref[...]
    content = (valid & (rank_key <= rank_query)) | (key == query)
    stream = (valid & (rank_key < rank_query)) | (key == 0)
    index = buckets_ref[...]
    for head in range(heads):
        row = jnp.broadcast_to(table_ref[head : head + 1, :], (rows, 128))
        bias = jnp.concatenate(
            [
                jnp.take_along_axis(
                    row, index[:, c : c + 128], axis=1, mode="promise_in_bounds"
                )
                for c in range(0, cols, 128)
            ],
            axis=1,
        )
        out_ref[head, :, :cols] = jnp.where(content, bias, NEG).astype(BF)
        out_ref[head, :, cols:] = jnp.where(stream, bias, NEG).astype(BF)


def masked_bias(length, buckets_t, rank, table, after=()):
    seq = buckets_t.shape[0]
    heads = table.shape[0]
    step = 128
    return call(
        bias_kernel,
        after,
        [length, buckets_t, rank.reshape(1, seq), rank.reshape(seq, 1), table],
        grid=(seq // step,),
        in_specs=[
            pl.BlockSpec(memory_space=pltpu.SMEM),
            pl.BlockSpec((step, seq), lambda g: (g, 0)),
            pl.BlockSpec((1, seq), lambda g: (0, 0)),
            pl.BlockSpec((step, 1), lambda g: (g, 0)),
            pl.BlockSpec((heads, 128), lambda g: (0, 0)),
        ],
        out_specs=pl.BlockSpec((heads, step, 2 * seq), lambda g: (0, g, 0)),
        out_shape=jax.ShapeDtypeStruct((heads, seq, 2 * seq), BF),
        cost_estimate=cost(9),
    )


def forward_kernel(q_ref, k_ref, v_ref, bias_ref, probs_ref, ctx_ref, inv_ref, *, tile):
    count = bias_ref.shape[0]
    size = q_ref.shape[0] // count
    for head in range(count):
        rows = slice(head * size, (head + 1) * size)
        keys = (k_ref[rows, :].astype(F32) * 0.125).astype(BF)
        for t in range(q_ref.shape[1] // tile):
            at = slice(t * tile, (t + 1) * tile)
            scores = dot(keys, q_ref[rows, at], TN) + bias_ref[head, :, at].astype(F32)
            high = jnp.max(scores, axis=0, keepdims=True)
            weight = jnp.exp(scores - high)
            inverse = 1.0 / jnp.sum(weight, axis=0, keepdims=True)
            low = weight.astype(BF)
            probs_ref[head, :, at] = low
            ctx_ref[rows, at] = (dot(v_ref[rows, :], low, NN) * inverse).astype(BF)
            inv_ref[head, :, at] = inverse


def attention(q_t, k_t, v_t, bias, before, heads, begin, steps, tile=1024, count=2, after=()):
    width, both = q_t.shape
    seq = k_t.shape[1]
    size = width // heads * count
    thin = pl.BlockSpec((size, seq), lambda h: (h + begin, 0))
    wide = pl.BlockSpec((size, both), lambda h: (h + begin, 0))
    square = pl.BlockSpec((count, seq, both), lambda h: (h + begin, 0, 0))

    def kernel(q_ref, k_ref, v_ref, bias_ref, *refs):
        forward_kernel(q_ref, k_ref, v_ref, bias_ref, *refs[-3:], tile=tile)

    return call(
        kernel,
        after,
        [q_t, k_t, v_t, bias, *before],
        grid=(steps,),
        in_specs=[wide, thin, thin, square] + [pl.BlockSpec(memory_space=pl.ANY)] * len(before),
        out_specs=[square, wide, pl.BlockSpec((count, 1, both), lambda h: (h + begin, 0, 0))],
        out_shape=[
            jax.ShapeDtypeStruct((heads, seq, both), BF),
            jax.ShapeDtypeStruct((width, both), BF),
            jax.ShapeDtypeStruct((heads, 1, both), F32),
        ],
        input_output_aliases={4 + i: i for i in range(len(before))},
        compiler_params=pltpu.CompilerParams(vmem_limit_bytes=48 * 1024 * 1024),
        cost_estimate=cost(3 * steps),
    )


def backward_kernel(q_ref, k_ref, v_ref, p_ref, inv_ref, ctx_ref, dctx_ref, *refs, tile):
    dq_ref, dk_ref, dv_ref, held_ref = refs[-4:]
    count = p_ref.shape[0]
    size, seq = k_ref.shape[0] // count, k_ref.shape[1]
    group = held_ref.shape[1] // count
    for head in range(count):
        rows = slice(head * size, (head + 1) * size)
        queries = q_ref[rows, :]
        keys = k_ref[rows, :]
        values = v_ref[rows, :]
        grad = dctx_ref[rows, :].astype(F32) * inv_ref[head]
        inner = jnp.sum(grad * ctx_ref[rows, :].astype(F32), axis=0, keepdims=True)
        grad = grad.astype(BF)
        dk = jnp.zeros(keys.shape, F32)
        dv = jnp.zeros(keys.shape, F32)
        for t in range(seq // tile):
            both = None
            for stream in range(2):
                lo = stream * seq + t * tile
                at = slice(lo, lo + tile)
                weight = p_ref[head, :, at]
                part = dot(values, grad[:, at], TN) - inner[:, at]
                ds = weight.astype(F32) * part
                low = ds.astype(BF)
                dv += dot(grad[:, at], weight, NT)
                dk += dot(queries[:, at], low, NT)
                dq_ref[rows, at] = (dot(keys, low, NN) * 0.125).astype(BF)
                both = ds if both is None else both + ds
            held_ref[:, head * group : (head + 1) * group, t * tile : (t + 1) * tile] = (
                both.astype(BF).reshape(seq // group, group, tile)
            )
        dk_ref[rows, :] = (dk * 0.125).astype(BF)
        dv_ref[rows, :] = dv.astype(BF)


def attention_back(
    q_t, k_t, v_t, probs, inverse, ctx_t, dctx_t, before, heads, begin, steps, count=2, group=16, tile=512, after=()
):
    width, both = q_t.shape
    seq = k_t.shape[1]
    size = width // heads * count
    wide = pl.BlockSpec((size, both), lambda h: (h + begin, 0))
    thin = pl.BlockSpec((size, seq), lambda h: (h + begin, 0))
    operands = [q_t, k_t, v_t, probs, inverse, ctx_t, dctx_t, *before]
    return call(
        functools.partial(backward_kernel, tile=tile),
        after,
        operands,
        grid=(steps,),
        in_specs=[
            wide,
            thin,
            thin,
            pl.BlockSpec((count, seq, both), lambda h: (h + begin, 0, 0)),
            pl.BlockSpec((count, 1, both), lambda h: (h + begin, 0, 0)),
            wide,
            wide,
        ]
        + [pl.BlockSpec(memory_space=pl.ANY)] * len(before),
        out_specs=[
            wide,
            thin,
            thin,
            pl.BlockSpec((seq // group, count * group, seq), lambda h: (0, h + begin, 0)),
        ],
        out_shape=[
            pltpu.HBM((width, both), BF),
            pltpu.HBM((width, seq), BF),
            pltpu.HBM((width, seq), BF),
            pltpu.HBM((seq // group, heads * group, seq), BF),
        ],
        input_output_aliases={7 + i: i for i in range(len(before))},
        compiler_params=pltpu.CompilerParams(vmem_limit_bytes=56 * 1024 * 1024),
        cost_estimate=cost(1e4 * steps),
    )


def table_kernel(buckets_ref, *refs, buckets, group):
    held_ref, out_ref, total = refs
    step, steps = pl.program_id(0), pl.num_programs(0)
    parts = buckets_ref.shape[0] // group
    index = buckets_ref[...].astype(F32).astype(BF)
    hot = jnp.concatenate(
        [
            jnp.concatenate(
                [
                    jnp.where(index[p * group : (p + 1) * group] == jnp.asarray(n, BF), 1.0, 0.0).astype(BF)
                    for n in range(buckets)
                ],
                axis=0,
            )
            for p in range(parts)
        ],
        axis=1,
    )
    held = jnp.concatenate([held_ref[p] for p in range(parts)], axis=1)
    value = dot(hot, held, NT)

    @pl.when(step == 0)
    def _():
        total[...] = value

    @pl.when(step > 0)
    def _():
        total[...] += value

    @pl.when(step == steps - 1)
    def _():
        value = total[...]
        row = lax.broadcasted_iota(jnp.int32, value.shape, 0) % group
        col = lax.broadcasted_iota(jnp.int32, value.shape, 1) % group
        kept = jnp.where(row == col, value, 0.0)
        out_ref[...] = jnp.sum(kept.reshape(buckets, group, value.shape[1]), axis=1)


def table_back(buckets_t, held, buckets, group=16, parts=4, after=()):
    seq = buckets_t.shape[0]
    cols = held.shape[1]
    return call(
        functools.partial(table_kernel, buckets=buckets, group=group),
        after,
        [buckets_t, held],
        grid=(seq // (group * parts),),
        in_specs=[
            pl.BlockSpec((group * parts, seq), lambda g: (g, 0)),
            pl.BlockSpec((parts, cols, seq), lambda g: (g, 0, 0)),
        ],
        out_specs=whole((buckets, cols)),
        out_shape=jax.ShapeDtypeStruct((buckets, cols), F32),
        scratch_shapes=[pltpu.VMEM((buckets * group, cols), F32)],
        compiler_params=pltpu.CompilerParams(vmem_limit_bytes=40 * 1024 * 1024),
        cost_estimate=cost(6),
    )


def call(kernel, after, operands, *, in_specs, **settings):
    count = len(operands)

    def body(*refs):
        kernel(*refs[:count], *refs[count + len(after) :])

    operands = [
        pltpu.with_memory_space_constraint(o, pltpu.HBM) if s.memory_space is None and o.size > 1 << 16 else o
        for o, s in zip(operands, in_specs)
    ]
    anywhere = [pl.BlockSpec(memory_space=pl.ANY)] * len(after)
    return pl.pallas_call(body, in_specs=in_specs + anywhere, **settings)(*operands, *after)


def whole(shape):
    return pl.BlockSpec(shape, lambda *_: (0,) * len(shape))


def once(shape, at):
    return pl.BlockSpec(shape, lambda *_: at, pipeline_mode=pl.Buffered(1))


def unit(value):
    centred = value - jnp.mean(value, axis=-1, keepdims=True)
    inverse = lax.rsqrt(jnp.mean(centred * centred, axis=-1, keepdims=True) + EPSILON)
    return centred * inverse, inverse


def unit_back(grad, along, inverse):
    mean = jnp.mean(grad, axis=-1, keepdims=True)
    slope = jnp.mean(grad * along, axis=-1, keepdims=True)
    return (grad - mean - along * slope) * inverse


def column_sum(value):
    rows = value.shape[0]
    return jnp.sum(value.reshape(rows // 8, 8, value.shape[1]), axis=0)


def up_kernel(
    ctx_ref, x_ref, cot_ref, wo_ref, wi_ref, wd_ref, bi_ref, rows_ref,
    out_ref, lowt_ref, act_ref, slope_ref, unit_ref, inv_ref, dres_ref, dlow_ref, dlowt_ref, sums_ref,
    *, chunk, part_rows,
):
    halves, width, part = wo_ref.shape
    ffn = wi_ref.shape[2]
    row = lambda i: rows_ref[i : i + 1, :]
    parts = [slice(r, r + part_rows) for r in range(0, x_ref.shape[0], part_rows)]
    resids, lows = [], []
    for at in parts:
        resid = x_ref[at, :].astype(F32) + row(0)
        for y in range(halves):
            resid += dot(ctx_ref[y * part : (y + 1) * part, at].T, wo_ref[y], NT)
        along, inverse = unit(resid)
        unit_ref[at, :] = along
        inv_ref[at, :] = inverse
        normed = along * row(2) + row(4)
        low = normed.astype(BF)
        lowt_ref[:, at] = low.T
        resids.append(normed + row(1))
        lows.append(low)
    for y in range(halves):
        for n, at in enumerate(parts):
            for c in range(0, ffn, chunk):
                cols = slice(c, c + chunk)
                hidden = dot(lows[n], wi_ref[y, :, cols], NN) + bi_ref[y, :, cols]
                cdf = 0.5 * lax.erf(hidden * 0.7071067811865476) + 0.5
                density = jnp.exp(hidden * hidden * -0.5) * 0.3989422804014327
                act_ref[y, at, cols] = (hidden * cdf).astype(BF)
                slope_ref[y, at, cols] = (cdf + hidden * density).astype(BF)
            resids[n] += dot(act_ref[y, at, :], wd_ref[y], NT)
    sums = [0.0, 0.0, 0.0]
    for n, at in enumerate(parts):
        along, inverse = unit(resids[n])
        out_ref[at, :] = (along * row(3) + row(5)).astype(BF)
        cot = cot_ref[at, :].astype(F32)
        dres = unit_back(cot * row(3), along, inverse)
        dres_ref[at, :] = dres
        dlow = dres.astype(BF)
        dlow_ref[at, :] = dlow
        dlowt_ref[:, at] = dlow.T
        for i, value in enumerate((dres, cot * along, cot)):
            sums[i] += column_sum(value)
    for i in range(3):
        sums_ref[0, i] = sums[i]


def up(ctx_t, stacked, cot, heads_all, rest, hidden_bias, rows, part, tile=256, chunk=512, part_rows=256, after=()):
    tokens, width = stacked.shape
    halves = rest.shape[0]
    ffn = rest.shape[2] // 2
    tall = pl.BlockSpec((width, tile), lambda t: (0, t))
    flat = pl.BlockSpec((tile, width), lambda t: (t, 0))
    wide = pl.BlockSpec((halves, tile, ffn), lambda t: (0, t, 0))
    sds = pltpu.HBM
    return call(
        functools.partial(up_kernel, chunk=chunk, part_rows=part_rows),
        after,
        [ctx_t, stacked, cot, heads_all, rest, rest, hidden_bias, rows],
        grid=(tokens // tile,),
        in_specs=[
            tall,
            flat,
            flat,
            once((halves, width, part), (0, 0, 3)),
            once((halves, width, ffn), (0, 0, 0)),
            once((halves, width, ffn), (0, 0, 1)),
            whole((halves, 1, ffn)),
            whole(rows.shape),
        ],
        out_specs=[
            flat, tall, wide, wide, flat, pl.BlockSpec((tile, 1), lambda t: (t, 0)), flat, flat, tall,
            pl.BlockSpec((1, 3, 8, width), lambda t: (t, 0, 0, 0)),
        ],
        out_shape=[
            sds((tokens, width), BF),
            sds((width, tokens), BF),
            sds((halves, tokens, ffn), BF),
            sds((halves, tokens, ffn), BF),
            sds((tokens, width), F32),
            sds((tokens, 1), F32),
            sds((tokens, width), F32),
            sds((tokens, width), BF),
            sds((width, tokens), BF),
            sds((tokens // tile, 3, 8, width), F32),
        ],
        compiler_params=pltpu.CompilerParams(vmem_limit_bytes=58 * 1024 * 1024),
        cost_estimate=cost(20),
    )


def down_kernel(
    dlow_ref, dres_ref, slope_ref, unit_ref, inv_ref, wo_ref, wi_ref, wd_ref, rows_ref,
    dhid_ref, done_ref, dot_ref, dctx_ref, sums_ref, hsum_ref, *, chunk, part_rows,
):
    halves, width, part = wo_ref.shape
    ffn = wi_ref.shape[2]
    parts = [slice(r, r + part_rows) for r in range(0, dlow_ref.shape[0], part_rows)]
    dnorms = [dres_ref[at, :] for at in parts]
    for y in range(halves):
        for n, at in enumerate(parts):
            for c in range(0, ffn, chunk):
                cols = slice(c, c + chunk)
                dhid = dot(dlow_ref[at, :], wd_ref[y, :, cols], NN) * slope_ref[y, at, cols].astype(F32)
                hsum_ref[0, n, y, :, cols] = column_sum(dhid)
                dhid_ref[y, at, cols] = dhid.astype(BF)
            dnorms[n] += dot(dhid_ref[y, at, :], wi_ref[y], NT)
    sums = [0.0, 0.0, 0.0]
    for n, at in enumerate(parts):
        dnorm = dnorms[n]
        along = unit_ref[at, :]
        done = unit_back(dnorm * rows_ref[2:3, :], along, inv_ref[at, :])
        done_ref[at, :] = done
        low = done.astype(BF)
        dot_ref[:, at] = low.T
        for y in range(halves):
            dctx_ref[y * part : (y + 1) * part, at] = dot(low, wo_ref[y], NN).astype(BF).T
        for i, value in enumerate((done, dnorm * along, dnorm)):
            sums[i] += column_sum(value)
    for i in range(3):
        sums_ref[0, i] = sums[i]


def down(dlow, dres, slope, along, inverse, heads_all, rest, rows, part, tile=256, chunk=512, part_rows=256, after=()):
    tokens, width = dlow.shape
    halves = rest.shape[0]
    ffn = rest.shape[2] // 2
    tall = pl.BlockSpec((width, tile), lambda t: (0, t))
    flat = pl.BlockSpec((tile, width), lambda t: (t, 0))
    wide = pl.BlockSpec((halves, tile, ffn), lambda t: (0, t, 0))
    sds = pltpu.HBM
    return call(
        functools.partial(down_kernel, chunk=chunk, part_rows=part_rows),
        after,
        [dlow, dres, slope, along, inverse, heads_all, rest, rest, rows],
        grid=(tokens // tile,),
        in_specs=[
            flat,
            flat,
            wide,
            flat,
            pl.BlockSpec((tile, 1), lambda t: (t, 0)),
            once((halves, width, part), (0, 0, 3)),
            once((halves, width, ffn), (0, 0, 0)),
            once((halves, width, ffn), (0, 0, 1)),
            whole(rows.shape),
        ],
        out_specs=[
            wide, flat, tall, tall,
            pl.BlockSpec((1, 3, 8, width), lambda t: (t, 0, 0, 0)),
            pl.BlockSpec((1, tile // part_rows, halves, 8, ffn), lambda t: (t, 0, 0, 0, 0)),
        ],
        out_shape=[
            sds((halves, tokens, ffn), BF),
            sds((tokens, width), F32),
            sds((width, tokens), BF),
            sds((width, tokens), BF),
            sds((tokens // tile, 3, 8, width), F32),
            sds((tokens // tile, tile // part_rows, halves, 8, ffn), F32),
        ],
        compiler_params=pltpu.CompilerParams(vmem_limit_bytes=58 * 1024 * 1024),
        cost_estimate=cost(18),
    )


def put_rows(core, value, keep_ref, send_ref, at):
    chips, rows = keep_ref.shape[1], keep_ref.shape[2]
    value = value.reshape(chips, 2, rows, value.shape[1])

    @pl.when(core == 0)
    def _():
        keep_ref[at] = value[:, 0]
        send_ref[at] = value[:, 1]

    @pl.when(core != 0)
    def _():
        keep_ref[at] = value[:, 1]
        send_ref[at] = value[:, 0]


def outer_kernel(core_ref, left_ref, right_ref, keep_ref, send_ref):
    value = dot(left_ref[...], right_ref[0], NN).astype(BF)
    put_rows(core_ref[0], value, keep_ref, send_ref, 0)


def outer(core, left_t, right, rows, tile=768, after=()):
    width, tokens = left_t.shape
    halves, _, cols = right.shape
    block = pl.BlockSpec((1, width // (2 * rows), rows, tile), lambda y, c: (y, 0, 0, c))
    shape = jax.ShapeDtypeStruct((halves, width // (2 * rows), rows, cols), BF)
    return call(
        outer_kernel,
        after,
        [core, left_t, right],
        grid=(halves, cols // tile),
        in_specs=[
            pl.BlockSpec(memory_space=pltpu.SMEM),
            whole(left_t.shape),
            pl.BlockSpec((1, tokens, tile), lambda y, c: (y, 0, c)),
        ],
        out_specs=[block, block],
        out_shape=[shape, shape],
        cost_estimate=cost(5),
    )


def outer_in_kernel(low_ref, dhid_ref, dot_ref, ctx_ref, out_ref):
    owners, _, rows, _ = out_ref.shape
    ffn = dhid_ref.shape[2]
    half = ffn // 2
    for c in (0, half):
        value = dot(low_ref[...], dhid_ref[0, :, c : c + half], NN).astype(BF)
        out_ref[:, 0, :, c : c + half] = value.reshape(owners, rows, half)
    value = dot(dot_ref[...], ctx_ref[...], NT).astype(BF)
    out_ref[:, 0, :, ffn:] = value.reshape(owners, rows, value.shape[1])


def outer_in(low_t, dhid, do_t, ctx_t, rows, after=()):
    width, tokens = low_t.shape
    halves, _, ffn = dhid.shape
    part = ctx_t.shape[0] // halves
    owners = width // rows
    return call(
        outer_in_kernel,
        after,
        [low_t, dhid, do_t, ctx_t],
        grid=(halves,),
        in_specs=[
            whole(low_t.shape),
            pl.BlockSpec((1, tokens, ffn), lambda y: (y, 0, 0)),
            whole(do_t.shape),
            pl.BlockSpec((part, tokens), lambda y: (y, 0)),
        ],
        out_specs=pl.BlockSpec((owners, 1, rows, ffn + part), lambda y: (0, y, 0, 0)),
        out_shape=jax.ShapeDtypeStruct((owners, halves, rows, ffn + part), BF),
        compiler_params=pltpu.CompilerParams(vmem_limit_bytes=48 * 1024 * 1024),
        cost_estimate=cost(6),
    )


def project_kernel(core_ref, own_a, own_b, other_a, other_b, x_ref, bias_ref, q_ref, k_ref, v_ref, w_ref):
    core = core_ref[0]
    cut = own_a.shape[3]
    width = x_ref.shape[1]
    part, seq = k_ref.shape
    w_ref[0, :, core, :, :cut] = own_a[0]
    w_ref[0, :, core, :, cut:] = own_b[0]
    w_ref[0, :, 1 - core, :, :cut] = other_a[0]
    w_ref[0, :, 1 - core, :, cut:] = other_b[0]
    weights = w_ref[0, :, :, :, : 3 * part].reshape(width, 3 * part)
    q = dot(x_ref[...], weights[:, :part], NN) + bias_ref[0, 0:1, :]
    q_ref[...] = q.astype(BF).T
    kv = dot(x_ref[:seq, :], weights[:, part:], NN)
    k_ref[...] = kv[:, :part].astype(BF).T
    v_ref[...] = (kv[:, part:] + bias_ref[0, 1:2, :]).astype(BF).T


def project(core, pieces, stacked, bias, part, after=()):
    tokens, width = stacked.shape
    halves, chips, rows, cut = pieces[0].shape
    cols = cut + pieces[1].shape[3]
    seq = tokens // 2
    sds = pltpu.HBM
    one = pl.BlockSpec((1, chips, rows, cut), lambda y: (y, 0, 0, 0))
    two = pl.BlockSpec((1, chips, rows, cols - cut), lambda y: (y, 0, 0, 0))
    return call(
        project_kernel,
        after,
        [core, *pieces, stacked, bias],
        grid=(halves,),
        in_specs=[
            pl.BlockSpec(memory_space=pltpu.SMEM), one, two, one, two,
            whole(stacked.shape),
            pl.BlockSpec((1, 2, part), lambda y: (y, 0, 0)),
        ],
        out_specs=[
            pl.BlockSpec((part, tokens), lambda y: (y, 0)),
            pl.BlockSpec((part, seq), lambda y: (y, 0)),
            pl.BlockSpec((part, seq), lambda y: (y, 0)),
            pl.BlockSpec((1, chips, 2, rows, cols), lambda y: (y, 0, 0, 0, 0)),
        ],
        out_shape=[
            sds((width, tokens), BF),
            sds((width, seq), BF),
            sds((width, seq), BF),
            sds((halves, chips, 2, rows, cols), BF),
        ],
        compiler_params=pltpu.CompilerParams(vmem_limit_bytes=40 * 1024 * 1024),
        cost_estimate=cost(6),
    )


def project_back_kernel(core_ref, x_ref, dq_ref, dk_ref, dv_ref, ka_ref, sa_ref, kb_ref, sb_ref, xt_ref):
    core = core_ref[0]
    part = dq_ref.shape[0]
    cut = ka_ref.shape[3]

    @pl.when(pl.program_id(0) == 0)
    def _():
        xt_ref[...] = x_ref[...].T

    values = []
    for ref in (dq_ref, dk_ref, dv_ref):
        tokens = ref.shape[1]
        values.append(dot(xt_ref[:, :tokens], ref[...], NT).astype(BF))
    value = jnp.concatenate(values, axis=1)
    put_rows(core, value[:, :cut], ka_ref, sa_ref, 0)
    put_rows(core, value[:, cut:], kb_ref, sb_ref, 0)


def project_back(core, stacked, dq_t, dk_t, dv_t, halves, rows, cut, after=()):
    tokens, width = stacked.shape
    chips = width // (2 * rows)
    part = width // halves
    one = pl.BlockSpec((1, chips, rows, cut), lambda y: (y, 0, 0, 0))
    two = pl.BlockSpec((1, chips, rows, 3 * part - cut), lambda y: (y, 0, 0, 0))
    first = jax.ShapeDtypeStruct((halves, chips, rows, cut), BF)
    second = jax.ShapeDtypeStruct((halves, chips, rows, 3 * part - cut), BF)
    return call(
        project_back_kernel,
        after,
        [core, stacked, dq_t, dk_t, dv_t],
        grid=(halves,),
        in_specs=[pl.BlockSpec(memory_space=pltpu.SMEM), whole(stacked.shape)]
        + [pl.BlockSpec((part, g.shape[1]), lambda y: (y, 0)) for g in (dq_t, dk_t, dv_t)],
        out_specs=[one, one, two, two],
        out_shape=[first, first, second, second],
        scratch_shapes=[pltpu.VMEM((width, tokens), BF)],
        compiler_params=pltpu.CompilerParams(vmem_limit_bytes=40 * 1024 * 1024),
        cost_estimate=cost(5),
    )


def inputs_kernel(half_ref, w_ref, done_ref, dq_ref, dk_ref, dv_ref, keep_ref, send_ref, sum_ref):
    step, steps = pl.program_id(0), pl.num_programs(0)
    halves, width, cols = w_ref.shape
    part = cols // 3
    total = done_ref[...]
    for y in range(halves):
        total += dot(dq_ref[y * part : (y + 1) * part, :].T, w_ref[y, :, :part], NT)
    sum_ref[...] = total

    @pl.when(step < steps // 2)
    def _():
        extra = 0.0
        for y in range(halves):
            at = slice(y * part, (y + 1) * part)
            extra += dot(dk_ref[at, :].T, w_ref[y, :, part : 2 * part], NT)
            extra += dot(dv_ref[at, :].T, w_ref[y, :, 2 * part :], NT)
        sum_ref[...] += extra

    half = width // 2

    @pl.when(half_ref[0] == 0)
    def _():
        keep_ref[...] = sum_ref[:, :half].astype(BF)
        send_ref[...] = sum_ref[:, half:].astype(BF)

    @pl.when(half_ref[0] != 0)
    def _():
        keep_ref[...] = sum_ref[:, half:].astype(BF)
        send_ref[...] = sum_ref[:, :half].astype(BF)


def inputs_back(half, weights, done, dq_t, dk_t, dv_t, tile=256, after=()):
    tokens, width = done.shape
    last = tokens // (2 * tile) - 1
    thin = pl.BlockSpec((width, tile), lambda t: (0, jnp.minimum(t, last)))
    out = pl.BlockSpec((tile, width // 2), lambda t: (t, 0))
    return call(
        inputs_kernel,
        after,
        [half, weights, done, dq_t, dk_t, dv_t],
        grid=(tokens // tile,),
        in_specs=[
            pl.BlockSpec(memory_space=pltpu.SMEM),
            once((weights.shape[0], width, 3 * width // weights.shape[0]), (0, 0, 0)),
            pl.BlockSpec((tile, width), lambda t: (t, 0)),
            pl.BlockSpec((width, tile), lambda t: (0, t)),
            thin,
            thin,
        ],
        out_specs=[out, out],
        out_shape=[jax.ShapeDtypeStruct((tokens, width // 2), BF)] * 2,
        scratch_shapes=[pltpu.VMEM((tile, width), F32)],
        compiler_params=pltpu.CompilerParams(vmem_limit_bytes=40 * 1024 * 1024),
        cost_estimate=cost(5),
    )


def shifted(value, axis, step):
    size = lax.axis_size(axis)
    return lax.ppermute(value, axis, [(i, (i + step) % size) for i in range(size)])


def gather_start(value, axis):
    return [value] + [shifted(value, axis, k) for k in range(1, lax.axis_size(axis))]


def gather_finish(pieces, axis, where):
    size = len(pieces)
    me = lax.axis_index(axis)
    slots = []
    for j in range(size):
        which = lax.rem(me - j + size, size)
        chosen = pieces[0]
        for k in range(1, size):
            chosen = jnp.where(which == k, pieces[k], chosen)
        slots.append(chosen)
    return jnp.stack(slots, axis=where)


def total(parts):
    return sum(part.astype(F32) for part in parts)


def start(parts, axis, where):
    size = lax.axis_size(axis)
    me = lax.axis_index(axis)

    def at(index):
        return [lax.dynamic_index_in_dim(part, index, where, keepdims=False) for part in parts]

    out = [total(at(lax.rem(me + k, size))).astype(BF) for k in range(1, size)]
    return at(me), [shifted(part, axis, k) for k, part in enumerate(out, 1)], out


def start_joined(sums, axis):
    size = lax.axis_size(axis)
    me = lax.axis_index(axis)

    def at(index):
        values = [total([lax.dynamic_index_in_dim(p, index, 0, keepdims=False) for p in parts]) for parts in sums]
        return jnp.concatenate(values, axis=-1)

    return [at(me)] + [shifted(at(lax.rem(me + k, size)).astype(BF), axis, k) for k in range(1, size)]


def start_core(keep, send):
    halves, _, rows, cols = keep.shape
    shape = (halves, lax.axis_size("z"), lax.axis_size("x"), rows, cols)
    return [keep.reshape(shape)], [shifted(send, "core", 1).reshape(shape)]


def tie_sums(pending, *others):
    arrived, *others = tie([p[1] for p in pending], *others)
    return [p[0] + list(a) for p, a in zip(pending, arrived)], *others


def tie(*groups):
    return lax.optimization_barrier(groups)


def sum_pairs(value, axes):
    for axis in axes:
        size = lax.axis_size(axis)
        step = 1
        while step < size:
            value = value + lax.ppermute(value, axis, [(i, i ^ step) for i in range(size)])
            step *= 2
    return value


def shards(
    content_in,
    query_in,
    lengths,
    factor_order,
    buckets,
    w_qkv,
    b_qv,
    w_out,
    w_in,
    b_in,
    w_down,
    b_outs,
    norm_gain,
    norm_bias,
    rel_table,
    cot_content,
    cot_query,
):
    me = lax.axis_index("y")
    halves = lax.axis_size("y")
    each = content_in.shape[0] // halves
    assert each == 1
    seq = content_in.shape[1]
    width = content_in.shape[2]
    bucket_count, heads_here = rel_table.shape
    heads = heads_here * halves
    part = w_qkv.shape[2]
    ffn = w_in.shape[1]
    rows = w_in.shape[0]

    def mine(array):
        return lax.dynamic_index_in_dim(array, me, 0, keepdims=False)

    rest = lax.all_gather(
        jnp.concatenate([w_in, w_down.T], axis=1), ("y", "z", "x", "core"), axis=0
    ).reshape(halves, width, 2 * ffn)
    vectors = jnp.concatenate([b_qv, b_in.reshape(ffn // part, part)], axis=0)
    vectors = jnp.concatenate(
        [vectors, jnp.pad(rel_table, ((0, 0), (0, part - heads_here)))], axis=0
    )
    vectors = gather_finish(gather_start(vectors, "y"), "y", 0).astype(F32)
    qv_bias = vectors[:, :2]
    hidden_bias = vectors[:, 2 : 2 + ffn // part].reshape(halves, 1, ffn)
    table = vectors[:, 2 + ffn // part :, :heads_here]
    table = jnp.transpose(table, (0, 2, 1)).reshape(heads, bucket_count)
    table = jnp.pad(table, ((0, 0), (0, 128 - bucket_count)))
    vector_rows = jnp.concatenate([b_outs, norm_gain, norm_bias], axis=0).astype(F32)
    vector_rows = jnp.pad(vector_rows, ((0, 2), (0, 0)))

    core = lax.axis_index("core").astype(jnp.int32).reshape(1)
    content = mine(content_in)
    stacked = jnp.concatenate([content, mine(query_in)], axis=0)
    buckets_t = mine(buckets).T
    rank = mine(factor_order)
    length = lax.dynamic_slice_in_dim(lengths, me, 1, 0)
    bias = masked_bias(length, buckets_t, rank, table)

    shard = jnp.concatenate([*w_qkv, w_out.T], axis=1)
    wide = shard.shape[1] // 2
    cut = 5 * part // 3
    chips = width // (2 * rows)
    along_z = gather_finish(gather_start(shard, "z"), "z", 0)
    one = gather_start(along_z[:, :, :wide], "x")
    two = gather_start(along_z[:, :, wide:], "y")
    one, two, bias = tie(one, two, bias)
    one = gather_start(gather_finish(one, "x", 1), "y")
    two = gather_start(gather_finish(two, "y", 0), "x")
    one = gather_finish(one, "y", 0).reshape(halves, chips, rows, wide)
    two = gather_finish(two, "x", 2).reshape(halves, chips, rows, wide)
    pieces = (one, two, shifted(one, "core", 1), shifted(two, "core", 1))
    q_t, k_t, v_t, heads_all = project(core, pieces, stacked, qv_bias, part)
    heads_all = heads_all.reshape(halves, width, 2 * wide)
    probs, ctx_t, inverse = attention(q_t, k_t, v_t, bias, (), heads, 0, heads // 2)

    cot = jnp.concatenate([mine(cot_content), mine(cot_query)], axis=0)
    output, low_t, active, slope, unit_one, inv_one, d_two, d_two_low, d_two_low_t, sums_two = up(
        ctx_t, stacked, cot, heads_all, rest, hidden_bias, vector_rows, part
    )
    output_got = shifted(output, "y", 1)
    down_pending = start_core(*outer(core, d_two_low_t, active, rows))
    ((down_sum,),) = tie_sums([down_pending])
    down_pending = start(down_sum, "x", 2)
    below = down(
        d_two_low, d_two, slope, unit_one, inv_one, heads_all, rest, vector_rows, part,
        after=down_pending[2],
    )
    (down_sum,), output_got, below = tie_sums([down_pending], output_got, below)
    d_hidden, d_one, d_one_low_t, dctx_t, sums_one, sums_hidden = below
    down_pending = start(down_sum, "y", 0)
    in_grads = outer_in(low_t, d_hidden, d_one_low_t, ctx_t, rows, after=down_pending[2])
    in_sum = lax.psum_scatter(in_grads, ("z", "x", "core"), scatter_dimension=0)
    (down_sum,), in_grads = tie_sums([down_pending], in_grads)
    down_pending = start(down_sum, "z", 0)
    grads = attention_back(
        q_t, k_t, v_t, probs, inverse, ctx_t, dctx_t, (), heads, 0, heads // 2, after=down_pending[2]
    )
    (down_sum,), grads = tie_sums([down_pending], grads)
    down_share = total(down_sum)
    dq_t, dk_t, dv_t, held = grads
    pairs = project_back(core, stacked, dq_t, dk_t, dv_t, halves, rows, cut)
    pending = [start_core(*pairs[:2]), start_core(*pairs[2:])]
    half = me.astype(jnp.int32).reshape(1)
    grad_in = inputs_back(half, heads_all, d_one, dq_t, dk_t, dv_t, after=pairs)
    sums, grad_in = tie_sums(pending, grad_in)
    pending = [start(sums[0], "x", 2), start(sums[1], "y", 0)]
    table_grad = table_back(buckets_t, held, bucket_count, after=pending[0][2] + pending[1][2])
    sums, table_grad, grad_in = tie_sums(pending, table_grad, grad_in)
    pending = [start(sums[0], "y", 0), start(sums[1], "x", 1)]
    grad_kept, grad_sent = grad_in
    grad_got = shifted(grad_sent, "y", 1)

    table_grad = jnp.sum(table_grad.reshape(bucket_count, heads, -1), axis=2).T
    sums_one = jnp.sum(sums_one, axis=(0, 2))
    sums_two = jnp.sum(sums_two, axis=(0, 2))
    small = jnp.concatenate(
        [jnp.sum(g.astype(F32), axis=1) for g in (dq_t, dv_t)]
        + [table_grad.reshape(-1), jnp.sum(sums_hidden, axis=(0, 1, 3)).reshape(-1)]
        + [s[i] for i in range(3) for s in (sums_one, sums_two)]
    )
    small = sum_pairs(small.reshape(-1, 128), ("core", "x"))
    sums, small = tie_sums(pending, small)
    pending = start_joined(sums, "z")
    in_pending = start([in_sum], "y", 0)
    in_share = total(in_pending[0] + in_pending[1])
    small = sum_pairs(small, ("y", "z")).reshape(-1)
    first_kept = me == 0
    outs = jnp.stack(
        [jnp.where(first_kept, output, output_got), jnp.where(first_kept, output_got, output)]
    ).reshape(halves, 2, seq, width)
    grad_ins = jnp.stack(
        [jnp.where(first_kept, grad_kept, grad_got), jnp.where(first_kept, grad_got, grad_kept)]
    ).reshape(halves, 2, seq, width // halves)
    qkv_share = total(pending)
    ends = [2 * width, 2 * width + heads * bucket_count]
    ends.append(ends[1] + halves * ffn)
    grad_b_qv = mine(jnp.transpose(small[: ends[0]].reshape(2, halves, part), (1, 0, 2)))
    grad_table = mine(small[ends[0] : ends[1]].reshape(halves, heads_here, bucket_count)).T
    grad_b_in = mine(small[ends[1] : ends[2]].reshape(halves, ffn))
    pairs = small[ends[2] :].reshape(3, 2, width)
    return (
        outs[:, 0],
        outs[:, 1],
        grad_ins[:, 0],
        grad_ins[:, 1],
        jnp.transpose(qkv_share.reshape(rows, 3, part), (1, 0, 2)),
        grad_b_qv,
        in_share[:, ffn:].T,
        in_share[:, :ffn],
        grad_b_in,
        down_share.T,
        pairs[0],
        pairs[1],
        pairs[2],
        grad_table,
    )


def solution(mesh):
    count = mesh.shape["dp"] // 2
    depth = 4 if count % 4 == 0 else 1
    while count // depth > depth:
        depth *= 2
    grid = mesh.devices.reshape(depth, count // depth, 2, mesh.shape["tensor"])
    fine = Mesh(grid, ("z", "x", "core", "y"))
    dp = ("z", "x", "core")
    return jax.shard_map(
        shards,
        mesh=fine,
        in_specs=(
            P(dp, None, None),
            P(dp, None, None),
            P(dp),
            P(dp, None),
            P(dp, None, None),
            P(None, dp, "y"),
            P(None, "y"),
            P("y", dp),
            P(dp, "y"),
            P("y"),
            P("y", dp),
            P(),
            P(),
            P(),
            P(None, "y"),
            P(dp, None, None),
            P(dp, None, None),
        ),
        out_specs=(
            P(dp, None, None),
            P(dp, None, None),
            P(dp, None, "y"),
            P(dp, None, "y"),
            P(None, dp, "y"),
            P(None, "y"),
            P("y", dp),
            P(dp, "y"),
            P("y"),
            P("y", dp),
            P(),
            P(),
            P(),
            P(None, "y"),
        ),
        check_vma=False,
    )
```

profile of v0, /device:TPU:0, one launch (start us, length us, event | category | flops | bytes accessed | tf_op | source)
XLA Modules:
  0.0 315.5 jit_solution(13130554663737065619)
XLA Ops:
  7.2 1.9 pad_maximum_fusion.9
  10.0 1.4 pad_maximum_fusion.10
  11.4 5.0 %collective-permute-start = (bf16[48,1536]{1,0:T(8,128)(2,1)}, bf16[48,1536]{1,0:T(8,128)(2,1)S(1)}, u32[]{:S(2)}, u32[]{:S(2)}) collective-permute-start(bf16[48,1536]{1,0:T(8,128)(2,1)} %pad_maximum_fusion.10), channel_id=1, source_target_pairs={{0,24},{8,0},{16,8},{24,16},{1,25},{9,1},{17,9},{25,17},{2,26},{10... | collective-permute-start | bytes 442376 | tf_op jit(solution)/shard_map/ppermute | solution.py:693
  19.0 1.3 fusion.28
  20.3 1.5 collective-permute-start.5
  22.7 1.3 copy.43
  26.0 7.8 %collective-permute-done.1 = bf16[48,1536]{1,0:T(8,128)(2,1)S(1)} collective-permute-done((bf16[48,1536]{1,0:T(8,128)(2,1)}, bf16[48,1536]{1,0:T(8,128)(2,1)S(1)}, u32[]{:S(2)}, u32[]{:S(2)}) %collective-permute-start.1) | collective-permute-done | bytes 147488 | tf_op jit(solution)/shard_map/ppermute | solution.py:693
  36.0 1.6 collective-permute-start.3
  37.6 1.7 collective-permute-start.4
  39.3 1.4 select_bitcast_fusion.11
  42.1 8.6 %shard_map.272.refs_3_ = bf16[12,512,1024]{2,1,0:T(8,128)(2,1)} custom-call(s32[1]{0:T(128)} %dynamic_slice.254.refs_0_, s32[512,512]{1,0:T(8,128)} %bitcast.233, s32[1,512]{1,0:T(1,128)} %constant_dynamic-slice_fusion.3.refs_2_, s32[512,1]{1,0:T(8,128)} %copy.46.refs_3_, f32[12,128]{1,0:T(8,128)} %pad.15.refs_4_), custom_call_target="tpu_custom_call" | custom-call | flops 90000000 | bytes 90000 | tf_op jit(solution)/shard_map/pallas_call | solution.py:272
  52.0 13.7 %collective-permute-done.7 = bf16[2,4,48,768]{3,2,1,0:T(8,128)(2,1)S(1)} collective-permute-done((bf16[2,4,48,768]{3,2,1,0:T(8,128)(2,1)S(1)}, bf16[2,4,48,768]{3,2,1,0:T(8,128)(2,1)S(1)}, u32[]{:S(2)}, u32[]{:S(2)}) %collective-permute-start.7) | collective-permute-done | bytes 589856 | tf_op jit(solution)/shard_map/ppermute | solution.py:693
  68.4 1.5 dynamic-slice_bitcast_fusion.2
  76.9 7.9 %shard_map.273 = (bf16[768,1024]{1,0:T(8,128)(2,1)}, bf16[768,512]{1,0:T(8,128)(2,1)}, bf16[768,512]{1,0:T(8,128)(2,1)}, bf16[2,8,2,48,1536]{4,3,2,1,0:T(8,128)(2,1)}) custom-call(s32[1]{0:T(128)} %bitcast.refs_0_, bf16[2,8,48,768]{3,2,1,0:T(8,128)(2,1)} %copy-done.12, bf16[2,8,48,768]{3,2,1,0:T(8,128)(2,1)} %bitcast.238, ...), custom_call_target="tpu_custom_call" | custom-call | flops 60000000 | bytes 60000 | tf_op jit(solution)/shard_map/pallas_call | solution.py:272
  84.8 16.2 %shard_map.274 = (bf16[12,512,1024]{2,1,0:T(8,128)(2,1)}, bf16[768,1024]{1,0:T(8,128)(2,1)S(1)}, f32[12,1,1024]{2,1,0:T(1,128)S(1)}) custom-call(bf16[768,1024]{1,0:T(8,128)(2,1)} %get-tuple-element.86.refs_0_, bf16[768,512]{1,0:T(8,128)(2,1)} %get-tuple-element.87.refs_1_, bf16[768,512]{1,0:T(8,128)(2,1)} %get-tuple-element.88.refs_2_, ...), custom_call_target="tpu_custom_call" | custom-call | flops 180000000 | bytes 180000 | tf_op jit(solution)/shard_map/pallas_call | solution.py:272
  102.7 2.1 all-gather.3.cloned.1.call-done
  104.8 25.4 %shard_map.275 = (bf16[1024,768]{1,0:T(8,128)(2,1)}, bf16[768,1024]{1,0:T(8,128)(2,1)}, bf16[2,1024,1536]{2,1,0:T(8,128)(2,1)}, bf16[2,1024,1536]{2,1,0:T(8,128)...) custom-call(bf16[768,1024]{1,0:T(8,128)(2,1)} %copy-done.2, ...), custom_call_target="tpu_custom_call" | custom-call | flops 200000000 | bytes 200000 | tf_op jit(solution)/shard_map/pallas_call | solution.py:272
  130.2 9.5 %shard_map.276 = (bf16[2,8,48,1536]{3,2,1,0:T(8,128)(2,1)}, bf16[2,8,48,1536]{3,2,1,0:T(8,128)(2,1)}) custom-call(s32[1]{0:T(128)} %bitcast.refs_0_, bf16[768,1024]{1,0:T(8,128)(2,1)} %get-tuple-element.93.refs_1_, bf16[2,1024,1536]{2,1,0:T(8,128)(2,1)} %get-tuple-element.94.refs_2_), custom_call_target="tpu_custom_call" | custom-call | flops 50000000 | bytes 50000 | tf_op jit(solution)/shard_map/pallas_call | solution.py:272
  139.9 1.5 collective-permute-start.12
  141.4 3.0 collective-permute-done.10
  144.4 2.4 fusion.3.refs_9_
  146.8 1.5 collective-permute-start.11
  148.3 22.2 %shard_map.277 = (bf16[2,1024,1536]{2,1,0:T(8,128)(2,1)}, f32[1024,768]{1,0:T(8,128)}, bf16[768,1024]{1,0:T(8,128)(2,1)}, bf16[768,1024]{1,0:T(8,128)(2,1)}, f32...) custom-call(bf16[1024,768]{1,0:T(8,128)(2,1)} %get-tuple-element.97.refs_0_, f32[1024,768]{1,0:T(8,128)} %get-tuple-element.98.refs_1_, ...), custom_call_target="tpu_custom_call" | custom-call | flops 180000000 | bytes 180000 | tf_op jit(solution)/shard_map/pallas_call | solution.py:272
  170.5 6.3 %collective-permute-done.12 = bf16[1024,768]{1,0:T(8,128)(2,1)} collective-permute-done((bf16[1024,768]{1,0:T(8,128)(2,1)}, bf16[1024,768]{1,0:T(8,128)(2,1)}, u32[]{:S(2)}, u32[]{:S(2)}) %collective-permute-start.12) | collective-permute-done | bytes 1572896 | tf_op jit(solution)/shard_map/ppermute | solution.py:693
  176.8 1.5 fusion.4.refs_4_
  178.2 1.5 collective-permute-start.13
  179.8 11.5 %shard_map.278 = bf16[16,2,48,1920]{3,2,1,0:T(8,128)(2,1)} custom-call(bf16[768,1024]{1,0:T(8,128)(2,1)} %get-tuple-element.110.refs_0_, bf16[2,1024,1536]{2,1,0:T(8,128)(2,1)} %get-tuple-element.111.refs_1_, bf16[768,1024]{1,0:T(8,128)(2,1)} %get-tuple-element.112.refs_2_, bf16[768,1024]{1,0:T(8,128)(2,1)} %copy-done.2, bf16[4,48,1536]{2,1,0:T(8,128)(2,1)S(1)} %fusion.4.refs_4_), custom_call_target="tpu_custom_call" | custom-call | flops 60000000 | bytes 60000 | tf_op jit(solution)/shard_map/pallas_call | solution.py:272
  191.3 1.6 collective-permute-done.13
  193.0 2.4 fusion.16
  195.4 1.4 collective-permute-start.14
  197.8 2.4 collective-permute-start.16
  200.2 18.5 %shard_map.279 = (bf16[768,1024]{1,0:T(8,128)(2,1)}, bf16[768,512]{1,0:T(8,128)(2,1)}, bf16[768,512]{1,0:T(8,128)(2,1)}, bf16[32,192,512]{2,1,0:T(8,128)(2,1)}) custom-call(bf16[768,1024]{1,0:T(8,128)(2,1)} %get-tuple-element.86.refs_0_, bf16[768,512]{1,0:T(8,128)(2,1)} %get-tuple-element.87.refs_1_, bf16[768,512]{1,0:T(8,128)(2,1)} %get-tuple-element.88.refs_2_, ...), custom_call_target="tpu_custom_call" | custom-call | flops 599999971328 | bytes 600000000 | tf_op jit(solution)/shard_map/pallas_call | solution.py:272
  218.7 7.1 %shard_map.280 = (bf16[2,8,48,640]{3,2,1,0:T(8,128)(2,1)S(1)}, bf16[2,8,48,640]{3,2,1,0:T(8,128)(2,1)S(1)}, bf16[2,8,48,512]{3,2,1,0:T(8,128)(2,1)S(1)}, bf16[2,8,48,512]{3,2,1,0:T(8,128)(2,1)S(1)}) custom-call(s32[1]{0:T(128)} %bitcast.refs_0_, bf16[1024,768]{1,0:T(8,128)(2,1)} %pad_maximum_fusion.1.refs_5_.refs_1_, ...), custom_call_target="tpu_custom_call" | custom-call | flops 50000000 | bytes 50000 | tf_op jit(solution)/shard_map/pallas_call | solution.py:272
  231.3 2.1 broadcast_select_fusion
  233.5 1.9 fusion.2
  235.4 8.1 %shard_map.281 = (bf16[1024,384]{1,0:T(8,128)(2,1)S(1)}, bf16[1024,384]{1,0:T(8,128)(2,1)S(1)}) custom-call(s32[1]{0:T(128)} %bitcast.54.refs_0_, bf16[2,768,1536]{2,1,0:T(8,128)(2,1)} %bitcast.232, f32[1024,768]{1,0:T(8,128)} %get-tuple-element.127.refs_2_, bf16[768,1024]{1,0:T(8,128)(2,1)} %get-tuple-element.121.refs_2_.refs_3_, ...), custom_call_target="tpu_custom_call" | custom-call | flops 50000000 | bytes 50000 | tf_op jit(solution)/shard_map/pallas_call | solution.py:272
  244.4 1.4 fusion.10.refs_3_
  249.2 9.7 %shard_map.282 = f32[32,192]{1,0:T(8,128)S(1)} custom-call(s32[512,512]{1,0:T(8,128)} %bitcast.234, bf16[32,192,512]{2,1,0:T(8,128)(2,1)} %get-tuple-element.133.refs_1_, bf16[2,4,48,640]{3,2,1,0:T(8,128)(2,1)S(1)} %fusion.8.refs_2_, bf16[4,2,48,512]{3,2,1,0:T(8,128)(2,1)S(1)} %fusion.10.refs_3_), custom_call_target="tpu_custom_call" | custom-call | flops 60000000 | bytes 60000 | tf_op jit(solution)/shard_map/pallas_call | solution.py:272
  259.0 5.9 %collective-permute-done.19 = bf16[2,4,48,640]{3,2,1,0:T(8,128)(2,1)S(1)} collective-permute-done((bf16[2,4,48,640]{3,2,1,0:T(8,128)(2,1)S(1)}, bf16[2,4,48,640]{3,2,1,0:T(8,128)(2,1)S(1)}, u32[]{:S(2)}, u32[]{:S(2)}) %collective-permute-start.19) | collective-permute-done | bytes 491552 | tf_op jit(solution)/shard_map/ppermute | solution.py:693
  266.9 1.3 collective-permute-start.25
  270.9 5.1 %collective-permute-done.23 = bf16[4,48,512]{2,1,0:T(8,128)(2,1)S(1)} collective-permute-done((bf16[4,48,512]{2,1,0:T(8,128)(2,1)S(1)}, bf16[4,48,512]{2,1,0:T(8,128)(2,1)S(1)}, u32[]{:S(2)}, u32[]{:S(2)}) %collective-permute-start.23) | collective-permute-done | bytes 196640 | tf_op jit(solution)/shard_map/ppermute | solution.py:693
  279.3 3.9 %collective-permute-start.28 = (bf16[48,1152]{1,0:T(8,128)(2,1)S(1)}, bf16[48,1152]{1,0:T(8,128)(2,1)S(1)}, u32[]{:S(2)}, u32[]{:S(2)}) collective-permute-start(bf16[48,1152]{1,0:T(8,128)(2,1)S(1)} %pad_maximum_fusion.13), channel_id=1, source_target_pairs={{0,24},{8,0},{16,8},{24,16},{1,25},{9,1},{17,9},{25,17},{2,26},{10... | collective-permute-start | bytes 331784 | tf_op jit(solution)/shard_map/ppermute | solution.py:693
  283.8 2.1 fusion.15
  287.1 2.3 collective-permute-done.30
  289.4 1.5 collective-permute-start.31
  291.8 2.7 collective-permute-done.31
  300.3 4.9 %collective-permute-done.21 = bf16[1024,384]{1,0:T(8,128)(2,1)S(1)} collective-permute-done((bf16[1024,384]{1,0:T(8,128)(2,1)S(1)}, bf16[1024,384]{1,0:T(8,128)(2,1)S(1)}, u32[]{:S(2)}, u32[]{:S(2)}) %collective-permute-start.21) | collective-permute-done | bytes 786464 | tf_op jit(solution)/shard_map/ppermute | solution.py:693
  305.5 1.3 fusion.7
  (208 shorter events, 51.8 us)
Async XLA Ops:
  7.2 14.6 %copy-start = (s32[2,512,512]{2,1,0:T(8,128)S(1)}, s32[2,512,512]{2,1,0:T(8,128)}, u32[]{:S(2)}) copy-start(s32[2,512,512]{2,1,0:T(8,128)} %param.21) | copy-start | bytes 6291460
  7.2 97.6 %all-gather.3.cloned.1.call-start = ((), (), s32[]{:S(2)}) async-start(), calls=%async_computation.2 | async-start | bytes 9732096 | tf_op jit(solution)/shard_map/all_gather | solution.py:798
  9.1 289.1 %reduce-scatter.2.cloned.1.call-start = ((), (), s32[]{:S(2)}) async-start(), calls=%async_computation.1 | async-start | bytes 6266880 | tf_op jit(solution)/shard_map/reduce_scatter | solution.py:855
  11.4 14.6 %collective-permute-start = (bf16[48,1536]{1,0:T(8,128)(2,1)}, bf16[48,1536]{1,0:T(8,128)(2,1)S(1)}, u32[]{:S(2)}, u32[]{:S(2)}) collective-permute-start(bf16[48,1536]{1,0:T(8,128)(2,1)} %pad_maximum_fusion.10), channel_id=1, source_target_pairs={{0,24},{8,0},{16,8},{24,16},{1,25},{9,1},{17,9},{25,17},{2,26},{10... | collective-permute-start | bytes 442376 | tf_op jit(solution)/shard_map/ppermute | solution.py:693
  16.5 17.3 %collective-permute-start.1 = (bf16[48,1536]{1,0:T(8,128)(2,1)}, bf16[48,1536]{1,0:T(8,128)(2,1)S(1)}, u32[]{:S(2)}, u32[]{:S(2)}) collective-permute-start(bf16[48,1536]{1,0:T(8,128)(2,1)} %pad_maximum_fusion.10), channel_id=1, source_target_pairs={{0,16},{8,24},{16,0},{24,8},{1,17},{9,25},{17,1},{25,9},{2,18},{10... | collective-permute-start | bytes 442376 | tf_op jit(solution)/shard_map/ppermute | solution.py:693
  16.5 17.3 %collective-permute-start.2 = (bf16[48,1536]{1,0:T(8,128)(2,1)}, bf16[48,1536]{1,0:T(8,128)(2,1)}, u32[]{:S(2)}, u32[]{:S(2)}) collective-permute-start(bf16[48,1536]{1,0:T(8,128)(2,1)} %pad_maximum_fusion.10), channel_id=1, source_target_pairs={{0,8},{8,16},{16,24},{24,0},{1,9},{9,17},{17,25},{25,1},{2,10},{10... | collective-permute-start | bytes 442376 | tf_op jit(solution)/shard_map/ppermute | solution.py:693
  20.3 19.0 %collective-permute-start.5 = (bf16[38,384]{1,0:T(8,128)(2,1)}, bf16[38,384]{1,0:T(8,128)(2,1)}, u32[]{:S(2)}, u32[]{:S(2)}) collective-permute-start(bf16[38,384]{1,0:T(8,128)(2,1)} %fusion.28), channel_id=1, source_target_pairs={{0,1},{1,0},{2,3},{3,2},{4,5},{5,4},{6,7},{7,6},{8,9},{9,8},{10,11... | collective-permute-start | bytes 87560 | tf_op jit(solution)/shard_map/ppermute | solution.py:693
  21.9 11.9 %copy-start.19 = (bf16[384,48]{0,1:T(8,128)(2,1)S(1)}, bf16[384,48]{0,1:T(8,128)(2,1)}, u32[]{:S(2)}) copy-start(bf16[384,48]{0,1:T(8,128)(2,1)} %param.24) | copy-start | bytes 110596
  36.0 14.7 %collective-permute-start.3 = (bf16[4,48,768]{2,1,0:T(8,128)(2,1)S(1)}, bf16[4,48,768]{2,1,0:T(8,128)(2,1)S(1)}, u32[]{:S(2)}, u32[]{:S(2)}) collective-permute-start(bf16[4,48,768]{2,1,0:T(8,128)(2,1)S(1)} %get-tuple-element.83), channel_id=1, source_target_pairs={{0,4},{4,0},{1,5},{5,1},{2,6},{6,2},{3,7},{7,3},{8,12},{12,8},{9,1... | collective-permute-start | bytes 884744 | tf_op jit(solution)/shard_map/ppermute | solution.py:693
  37.6 13.1 %collective-permute-start.4 = (bf16[4,48,768]{2,1,0:T(8,128)(2,1)S(1)}, bf16[4,48,768]{2,1,0:T(8,128)(2,1)S(1)}, u32[]{:S(2)}, u32[]{:S(2)}) collective-permute-start(bf16[4,48,768]{2,1,0:T(8,128)(2,1)S(1)} %get-tuple-element.85), channel_id=1, source_target_pairs={{0,1},{1,0},{2,3},{3,2},{4,5},{5,4},{6,7},{7,6},{8,9},{9,8},{10,11... | collective-permute-start | bytes 884744 | tf_op jit(solution)/shard_map/ppermute | solution.py:693
  50.9 14.8 %collective-permute-start.7 = (bf16[2,4,48,768]{3,2,1,0:T(8,128)(2,1)S(1)}, bf16[2,4,48,768]{3,2,1,0:T(8,128)(2,1)S(1)}, u32[]{:S(2)}, u32[]{:S(2)}) collective-permute-start(bf16[2,4,48,768]{3,2,1,0:T(8,128)(2,1)S(1)} %pad_maximum_fusion.8), channel_id=1, source_target_pairs={{0,4},{4,0},{1,5},{5,1},{2,6},{6,2},{3,7},{7,3},{8,12},{12,8},{9,1... | collective-permute-start | bytes 1769480 | tf_op jit(solution)/shard_map/ppermute | solution.py:693
  51.4 14.7 %collective-permute-start.6 = (bf16[4,2,48,768]{3,2,0,1:T(8,128)(2,1)S(1)}, bf16[4,2,48,768]{3,2,0,1:T(8,128)(2,1)S(1)}, u32[]{:S(2)}, u32[]{:S(2)}) collective-permute-start(bf16[4,2,48,768]{3,2,0,1:T(8,128)(2,1)S(1)} %pad_maximum_fusion.7), channel_id=1, source_target_pairs={{0,1},{1,0},{2,3},{3,2},{4,5},{5,4},{6,7},{7,6},{8,9},{9,8},{10,11... | collective-permute-start | bytes 1769480 | tf_op jit(solution)/shard_map/ppermute | solution.py:693
  66.0 9.8 %collective-permute-start.9 = (bf16[2,8,48,768]{3,2,1,0:T(8,128)(2,1)S(1)}, bf16[2,8,48,768]{3,2,1,0:T(8,128)(2,1)S(1)}, u32[]{:S(2)}, u32[]{:S(2)}) collective-permute-start(bf16[2,8,48,768]{3,2,1,0:T(8,128)(2,1)S(1)} %bitcast.237), channel_id=1, source_target_pairs={{0,2},{2,0},{1,3},{3,1},{4,6},{6,4},{5,7},{7,5},{8,10},{10,8},{9,1... | collective-permute-start | bytes 3538952 | tf_op jit(solution)/shard_map/ppermute | solution.py:693
  67.2 8.7 %collective-permute-start.8 = (bf16[2,8,48,768]{3,2,1,0:T(8,128)(2,1)S(1)}, bf16[2,8,48,768]{3,2,1,0:T(8,128)(2,1)}, u32[]{:S(2)}, u32[]{:S(2)}) collective-permute-start(bf16[2,8,48,768]{3,2,1,0:T(8,128)(2,1)S(1)} %pad_maximum_fusion.3.refs_1_), channel_id=1, source_target_pairs={{0,2},{2,0},{1,3},{3,1},{4,6},{6,4},{5,7},{7,5},{8,10},{10,8},{9,1... | collective-permute-start | bytes 3538952 | tf_op jit(solution)/shard_map/ppermute | solution.py:693
  139.7 4.7 %collective-permute-start.10 = (bf16[2,8,48,1536]{3,2,1,0:T(8,128)(2,1)}, bf16[2,8,48,1536]{3,2,1,0:T(8,128)(2,1)S(1)}, u32[]{:S(2)}, u32[]{:S(2)}) collective-permute-start(bf16[2,8,48,1536]{3,2,1,0:T(8,128)(2,1)} %get-tuple-element.96), channel_id=1, source_target_pairs={{0,2},{2,0},{1,3},{3,1},{4,6},{6,4},{5,7},{7,5},{8,10},{10,8},{9,1... | collective-permute-start | bytes 7077896 | tf_op jit(solution)/shard_map/ppermute | solution.py:693
  139.9 36.9 %collective-permute-start.12 = (bf16[1024,768]{1,0:T(8,128)(2,1)}, bf16[1024,768]{1,0:T(8,128)(2,1)}, u32[]{:S(2)}, u32[]{:S(2)}) collective-permute-start(bf16[1024,768]{1,0:T(8,128)(2,1)} %get-tuple-element.92), channel_id=1, source_target_pairs={{0,1},{1,0},{2,3},{3,2},{4,5},{5,4},{6,7},{7,6},{8,9},{9,8},{10,11... | collective-permute-start | bytes 4718600 | tf_op jit(solution)/shard_map/ppermute | solution.py:693
  144.4 48.6 %copy-start.13 = (bf16[2,8,48,1536]{3,2,1,0:T(8,128)(2,1)}, bf16[2,8,48,1536]{3,2,1,0:T(8,128)(2,1)S(1)}, u32[]{:S(2)}) copy-start(bf16[2,8,48,1536]{3,2,1,0:T(8,128)(2,1)S(1)} %collective-permute-done.10) | copy-start | bytes 7077892
  146.8 29.9 %collective-permute-start.11 = (bf16[2,4,48,1536]{3,2,1,0:T(8,128)(2,1)S(1)}, bf16[2,4,48,1536]{3,2,1,0:T(8,128)(2,1)}, u32[]{:S(2)}, u32[]{:S(2)}) collective-permute-start(bf16[2,4,48,1536]{3,2,1,0:T(8,128)(2,1)S(1)} %fusion.3.refs_9_), channel_id=1, source_target_pairs={{0,4},{4,0},{1,5},{5,1},{2,6},{6,2},{3,7},{7,3},{8,12},{12,8},{9,1... | collective-permute-start | bytes 3538952 | tf_op jit(solution)/shard_map/ppermute | solution.py:693
  178.2 14.7 %collective-permute-start.13 = (bf16[4,48,1536]{2,1,0:T(8,128)(2,1)S(1)}, bf16[4,48,1536]{2,1,0:T(8,128)(2,1)S(1)}, u32[]{:S(2)}, u32[]{:S(2)}) collective-permute-start(bf16[4,48,1536]{2,1,0:T(8,128)(2,1)S(1)} %fusion.4.refs_4_), channel_id=1, source_target_pairs={{0,1},{1,0},{2,3},{3,2},{4,5},{5,4},{6,7},{7,6},{8,9},{9,8},{10,11... | collective-permute-start | bytes 1769480 | tf_op jit(solution)/shard_map/ppermute | solution.py:693
  193.0 25.7 %copy-start.15 = (bf16[4,48,1536]{2,1,0:T(8,128)(2,1)}, bf16[4,48,1536]{2,1,0:T(8,128)(2,1)S(1)}, u32[]{:S(2)}) copy-start(bf16[4,48,1536]{2,1,0:T(8,128)(2,1)S(1)} %collective-permute-done.13) | copy-start | bytes 1769476
  195.4 23.3 %collective-permute-start.14 = (bf16[48,1536]{1,0:T(8,128)(2,1)}, bf16[48,1536]{1,0:T(8,128)(2,1)}, u32[]{:S(2)}, u32[]{:S(2)}) collective-permute-start(bf16[48,1536]{1,0:T(8,128)(2,1)} %get-tuple-element.172.refs_7_), channel_id=1, source_target_pairs={{0,8},{8,16},{16,24},{24,0},{1,9},{9,17},{17,25},{25,1},{2,10},{10... | collective-permute-start | bytes 442376 | tf_op jit(solution)/shard_map/ppermute | solution.py:693
  196.8 21.9 %collective-permute-start.15 = (bf16[48,1536]{1,0:T(8,128)(2,1)}, bf16[48,1536]{1,0:T(8,128)(2,1)}, u32[]{:S(2)}, u32[]{:S(2)}) collective-permute-start(bf16[48,1536]{1,0:T(8,128)(2,1)} %get-tuple-element.171.refs_8_), channel_id=1, source_target_pairs={{0,16},{8,24},{16,0},{24,8},{1,17},{9,25},{17,1},{25,9},{2,18},{10... | collective-permute-start | bytes 442376 | tf_op jit(solution)/shard_map/ppermute | solution.py:693
  197.8 20.9 %collective-permute-start.16 = (bf16[48,1536]{1,0:T(8,128)(2,1)}, bf16[48,1536]{1,0:T(8,128)(2,1)}, u32[]{:S(2)}, u32[]{:S(2)}) collective-permute-start(bf16[48,1536]{1,0:T(8,128)(2,1)} %get-tuple-element.170.refs_9_), channel_id=1, source_target_pairs={{0,24},{8,0},{16,8},{24,16},{1,25},{9,1},{17,9},{25,17},{2,26},{10... | collective-permute-start | bytes 442376 | tf_op jit(solution)/shard_map/ppermute | solution.py:693
  225.8 18.7 %collective-permute-start.17 = (bf16[2,8,48,640]{3,2,1,0:T(8,128)(2,1)S(1)}, bf16[2,8,48,640]{3,2,1,0:T(8,128)(2,1)}, u32[]{:S(2)}, u32[]{:S(2)}) collective-permute-start(bf16[2,8,48,640]{3,2,1,0:T(8,128)(2,1)S(1)} %get-tuple-element.125.refs_7_), channel_id=1, source_target_pairs={{0,2},{2,0},{1,3},{3,1},{4,6},{6,4},{5,7},{7,5},{8,10},{10,8},{9,1... | collective-permute-start | bytes 2949128 | tf_op jit(solution)/shard_map/ppermute | solution.py:693
  226.9 17.5 %collective-permute-start.18 = (bf16[2,8,48,512]{3,2,1,0:T(8,128)(2,1)S(1)}, bf16[2,8,48,512]{3,2,1,0:T(8,128)(2,1)}, u32[]{:S(2)}, u32[]{:S(2)}) collective-permute-start(bf16[2,8,48,512]{3,2,1,0:T(8,128)(2,1)S(1)} %get-tuple-element.126.refs_9_), channel_id=1, source_target_pairs={{0,2},{2,0},{1,3},{3,1},{4,6},{6,4},{5,7},{7,5},{8,10},{10,8},{9,1... | collective-permute-start | bytes 2359304 | tf_op jit(solution)/shard_map/ppermute | solution.py:693
  244.4 4.5 %copy-start.3 = (bf16[1024,384]{1,0:T(8,128)(2,1)}, bf16[1024,384]{1,0:T(8,128)(2,1)S(1)}, u32[]{:S(2)}) copy-start(bf16[1024,384]{1,0:T(8,128)(2,1)S(1)} %get-tuple-element.136) | copy-start | bytes 2359300
  245.9 13.1 %collective-permute-start.20 = (bf16[4,2,48,512]{3,2,1,0:T(8,128)(2,1)S(1)}, bf16[4,2,48,512]{3,2,1,0:T(8,128)(2,1)S(1)}, u32[]{:S(2)}, u32[]{:S(2)}) collective-permute-start(bf16[4,2,48,512]{3,2,1,0:T(8,128)(2,1)S(1)} %fusion.10.refs_3_), channel_id=1, source_target_pairs={{0,1},{1,0},{2,3},{3,2},{4,5},{5,4},{6,7},{7,6},{8,9},{9,8},{10,11... | collective-permute-start | bytes 1179656 | tf_op jit(solution)/shard_map/ppermute | solution.py:693
  248.2 16.7 %collective-permute-start.19 = (bf16[2,4,48,640]{3,2,1,0:T(8,128)(2,1)S(1)}, bf16[2,4,48,640]{3,2,1,0:T(8,128)(2,1)S(1)}, u32[]{:S(2)}, u32[]{:S(2)}) collective-permute-start(bf16[2,4,48,640]{3,2,1,0:T(8,128)(2,1)S(1)} %fusion.8.refs_2_), channel_id=1, source_target_pairs={{0,4},{4,0},{1,5},{5,1},{2,6},{6,2},{3,7},{7,3},{8,12},{12,8},{9,1... | collective-permute-start | bytes 1474568 | tf_op jit(solution)/shard_map/ppermute | solution.py:693
  249.2 15.9 %copy-start.23 = (f32[3072]{0:T(1024)S(1)}, f32[3072]{0:T(1024)}, u32[]{:S(2)}) copy-start(f32[3072]{0:T(1024)} %reshape.362) | copy-start | bytes 36868
  249.2 15.9 %copy-start.28 = (f32[768]{0:T(1024)S(1)}, f32[768]{0:T(1024)}, u32[]{:S(2)}) copy-start(f32[768]{0:T(1024)} %get-tuple-element.169) | copy-start | bytes 9220
  249.2 15.9 %copy-start.25 = (f32[768]{0:T(1024)S(1)}, f32[768]{0:T(1024)}, u32[]{:S(2)}) copy-start(f32[768]{0:T(1024)} %get-tuple-element.166) | copy-start | bytes 9220
  249.2 15.9 %copy-start.27 = (f32[768]{0:T(1024)S(1)}, f32[768]{0:T(1024)}, u32[]{:S(2)}) copy-start(f32[768]{0:T(1024)} %get-tuple-element.168) | copy-start | bytes 9220
  249.2 15.9 %copy-start.24 = (f32[768]{0:T(1024)S(1)}, f32[768]{0:T(1024)}, u32[]{:S(2)}) copy-start(f32[768]{0:T(1024)} %get-tuple-element.165) | copy-start | bytes 9220
  249.2 16.0 %copy-start.26 = (f32[768]{0:T(1024)S(1)}, f32[768]{0:T(1024)}, u32[]{:S(2)}) copy-start(f32[768]{0:T(1024)} %get-tuple-element.167) | copy-start | bytes 9220
  265.2 1.6 collective-permute-start.24
  266.4 9.7 %collective-permute-start.22 = (bf16[4,48,640]{2,1,0:T(8,128)(2,1)S(1)}, bf16[4,48,640]{2,1,0:T(8,128)(2,1)S(1)}, u32[]{:S(2)}, u32[]{:S(2)}) collective-permute-start(bf16[4,48,640]{2,1,0:T(8,128)(2,1)S(1)} %fusion.9), channel_id=1, source_target_pairs={{0,1},{1,0},{2,3},{3,2},{4,5},{5,4},{6,7},{7,6},{8,9},{9,8},{10,11... | collective-permute-start | bytes 737288 | tf_op jit(solution)/shard_map/ppermute | solution.py:693
  266.9 4.1 %collective-permute-start.25 = (f32[75,128]{1,0:T(8,128)S(1)}, f32[75,128]{1,0:T(8,128)S(1)}, u32[]{:S(2)}, u32[]{:S(2)}) collective-permute-start(f32[75,128]{1,0:T(8,128)S(1)} %bitcast_add_fusion), channel_id=1, source_target_pairs={{0,4},{4,0},{1,5},{5,1},{2,6},{6,2},{3,7},{7,3},{8,12},{12,8},{9,1... | collective-permute-start | bytes 115208 | tf_op jit(solution)/shard_map/ppermute | solution.py:759
  269.2 6.8 %collective-permute-start.23 = (bf16[4,48,512]{2,1,0:T(8,128)(2,1)S(1)}, bf16[4,48,512]{2,1,0:T(8,128)(2,1)S(1)}, u32[]{:S(2)}, u32[]{:S(2)}) collective-permute-start(bf16[4,48,512]{2,1,0:T(8,128)(2,1)S(1)} %fusion.11), channel_id=1, source_target_pairs={{0,4},{4,0},{1,5},{5,1},{2,6},{6,2},{3,7},{7,3},{8,12},{12,8},{9,1... | collective-permute-start | bytes 589832 | tf_op jit(solution)/shard_map/ppermute | solution.py:693
  276.0 7.1 %collective-permute-start.29 = (f32[75,128]{1,0:T(8,128)S(1)}, f32[75,128]{1,0:T(8,128)S(1)}, u32[]{:S(2)}, u32[]{:S(2)}) collective-permute-start(f32[75,128]{1,0:T(8,128)S(1)} %fusion.40), channel_id=1, source_target_pairs={{0,1},{1,0},{2,3},{3,2},{4,5},{5,4},{6,7},{7,6},{8,9},{9,8},{10,11... | collective-permute-start | bytes 115208 | tf_op jit(solution)/shard_map/ppermute | solution.py:759
  277.9 8.0 %copy-start.6 = (bf16[1024,384]{1,0:T(8,128)(2,1)S(1)}, bf16[1024,384]{1,0:T(8,128)(2,1)}, u32[]{:S(2)}) copy-start(bf16[1024,384]{1,0:T(8,128)(2,1)} %copy-done.5) | copy-start | bytes 2359300
  279.1 11.8 %collective-permute-start.26 = (bf16[48,1152]{1,0:T(8,128)(2,1)S(1)}, bf16[48,1152]{1,0:T(8,128)(2,1)S(1)}, u32[]{:S(2)}, u32[]{:S(2)}) collective-permute-start(bf16[48,1152]{1,0:T(8,128)(2,1)S(1)} %pad_maximum_fusion.11), channel_id=1, source_target_pairs={{0,8},{8,16},{16,24},{24,0},{1,9},{9,17},{17,25},{25,1},{2,10},{10... | collective-permute-start | bytes 331784 | tf_op jit(solution)/shard_map/ppermute | solution.py:693
  279.2 11.7 %collective-permute-start.27 = (bf16[48,1152]{1,0:T(8,128)(2,1)S(1)}, bf16[48,1152]{1,0:T(8,128)(2,1)S(1)}, u32[]{:S(2)}, u32[]{:S(2)}) collective-permute-start(bf16[48,1152]{1,0:T(8,128)(2,1)S(1)} %pad_maximum_fusion.12), channel_id=1, source_target_pairs={{0,16},{8,24},{16,0},{24,8},{1,17},{9,25},{17,1},{25,9},{2,18},{10... | collective-permute-start | bytes 331784 | tf_op jit(solution)/shard_map/ppermute | solution.py:693
  279.3 11.7 %collective-permute-start.28 = (bf16[48,1152]{1,0:T(8,128)(2,1)S(1)}, bf16[48,1152]{1,0:T(8,128)(2,1)S(1)}, u32[]{:S(2)}, u32[]{:S(2)}) collective-permute-start(bf16[48,1152]{1,0:T(8,128)(2,1)S(1)} %pad_maximum_fusion.13), channel_id=1, source_target_pairs={{0,24},{8,0},{16,8},{24,16},{1,25},{9,1},{17,9},{25,17},{2,26},{10... | collective-permute-start | bytes 331784 | tf_op jit(solution)/shard_map/ppermute | solution.py:693
  283.1 6.2 %collective-permute-start.30 = (f32[75,128]{1,0:T(8,128)S(1)}, f32[75,128]{1,0:T(8,128)S(1)}, u32[]{:S(2)}, u32[]{:S(2)}) collective-permute-start(f32[75,128]{1,0:T(8,128)S(1)} %add.703), channel_id=1, source_target_pairs={{0,8},{8,0},{16,24},{24,16},{1,9},{9,1},{17,25},{25,17},{2,10},{10... | collective-permute-start | bytes 115208 | tf_op jit(solution)/shard_map/ppermute | solution.py:759
  285.9 19.4 %copy-start.4 = (bf16[1024,384]{1,0:T(8,128)(2,1)S(1)}, bf16[1024,384]{1,0:T(8,128)(2,1)}, u32[]{:S(2)}) copy-start(bf16[1024,384]{1,0:T(8,128)(2,1)} %copy-done.3) | copy-start | bytes 2359300
  285.9 19.4 %collective-permute-start.21 = (bf16[1024,384]{1,0:T(8,128)(2,1)S(1)}, bf16[1024,384]{1,0:T(8,128)(2,1)S(1)}, u32[]{:S(2)}, u32[]{:S(2)}) collective-permute-start(bf16[1024,384]{1,0:T(8,128)(2,1)S(1)} %copy-done.6), channel_id=1, source_target_pairs={{0,1},{1,0},{2,3},{3,2},{4,5},{5,4},{6,7},{7,6},{8,9},{9,8},{10,11... | collective-permute-start | bytes 2359304 | tf_op jit(solution)/shard_map/ppermute | solution.py:693
  289.4 5.1 %collective-permute-start.31 = (f32[75,128]{1,0:T(8,128)S(1)}, f32[75,128]{1,0:T(8,128)S(1)}, u32[]{:S(2)}, u32[]{:S(2)}) collective-permute-start(f32[75,128]{1,0:T(8,128)S(1)} %add.704), channel_id=1, source_target_pairs={{0,16},{8,24},{16,0},{24,8},{1,17},{9,25},{17,1},{25,9},{2,18},{10... | collective-permute-start | bytes 115208 | tf_op jit(solution)/shard_map/ppermute | solution.py:759
  299.2 8.1 %collective-permute-start.32 = (bf16[48,1920]{1,0:T(8,128)(2,1)S(1)}, bf16[48,1920]{1,0:T(8,128)(2,1)S(1)}, u32[]{:S(2)}, u32[]{:S(2)}) collective-permute-start(bf16[48,1920]{1,0:T(8,128)(2,1)S(1)} %dynamic-slice_bitcast_fusion.4), channel_id=1, source_target_pairs={{0,1},{1,0},{2,3},{3,2},{4,5},{5,4},{6,7},{7,6},{8,9},{9,8},{10,11... | collective-permute-start | bytes 552968 | tf_op jit(solution)/shard_map/ppermute | solution.py:693
  (22 other events, 49.8 us)
Sparse Core Ops, SparseCore 0:
  11.5 93.2 all-gather.2
  191.5 82.0 reduce-scatter.1
where the time goes:
time: 317 us; the launch traced here: 316 us
  Pallas kernels  145 us (46%)
  waiting for transfers between devices  56.9 us (18%)
  other arithmetic  38.4 us (12%)
  starting transfers between devices  35.9 us (11%)
  local copies, waits for them, and re-layouts  24.9 us (8%)
  between operations  14.9 us (5%)
    pallas_call x11, Pallas kernels, call(): pl.pallas_call(body, in_specs=in_specs + anywhere, **settings)  145 us
    ppermute x28, waiting for transfers between devices, shifted(): lax.ppermute(value, axis, [(i, (i + step) % size) for i in range(size)])  48.9 us
    ppermute x28, starting transfers between devices, shifted(): lax.ppermute(value, axis, [(i, (i + step) % size) for i in range(size)])  31.4 us
    convert_element_type x7, other arithmetic, start(): out = [total(at(lax.rem(me + k, size))).astype(BF) for k in range(1, size)]  10.9 us
    unnamed x82, local copies, waits for them, and re-layouts  8.53 us
  transfers between devices with their start and end apart: 35, of which 13 were waited for; matrix products, arithmetic and copies ran while one was open for 17% of the time, Pallas kernels for 35%

commit v1 on v0

--- a/solution.py
+++ b/solution.py
@@ -590,11 +590,7 @@
     )
 
 
-def project_back_kernel(core_ref, x_ref, dq_ref, dk_ref, dv_ref, ka_ref, sa_ref, kb_ref, sb_ref, xt_ref):
-    core = core_ref[0]
-    part = dq_ref.shape[0]
-    cut = ka_ref.shape[3]
-
+def project_back_kernel(core_ref, x_ref, dq_ref, dk_ref, dv_ref, keep_ref, send_ref, xt_ref):
     @pl.when(pl.program_id(0) == 0)
     def _():
         xt_ref[...] = x_ref[...].T
@@ -603,19 +599,15 @@
     for ref in (dq_ref, dk_ref, dv_ref):
         tokens = ref.shape[1]
         values.append(dot(xt_ref[:, :tokens], ref[...], NT).astype(BF))
-    value = jnp.concatenate(values, axis=1)
-    put_rows(core, value[:, :cut], ka_ref, sa_ref, 0)
-    put_rows(core, value[:, cut:], kb_ref, sb_ref, 0)
-
-
-def project_back(core, stacked, dq_t, dk_t, dv_t, halves, rows, cut, after=()):
+    put_rows(core_ref[0], jnp.concatenate(values, axis=1), keep_ref, send_ref, 0)
+
+
+def project_back(core, stacked, dq_t, dk_t, dv_t, halves, rows, after=()):
     tokens, width = stacked.shape
     chips = width // (2 * rows)
     part = width // halves
-    one = pl.BlockSpec((1, chips, rows, cut), lambda y: (y, 0, 0, 0))
-    two = pl.BlockSpec((1, chips, rows, 3 * part - cut), lambda y: (y, 0, 0, 0))
-    first = jax.ShapeDtypeStruct((halves, chips, rows, cut), BF)
-    second = jax.ShapeDtypeStruct((halves, chips, rows, 3 * part - cut), BF)
+    block = pl.BlockSpec((1, chips, rows, 3 * part), lambda y: (y, 0, 0, 0))
+    shape = jax.ShapeDtypeStruct((halves, chips, rows, 3 * part), BF)
     return call(
         project_back_kernel,
         after,
@@ -623,8 +615,8 @@
         grid=(halves,),
         in_specs=[pl.BlockSpec(memory_space=pltpu.SMEM), whole(stacked.shape)]
         + [pl.BlockSpec((part, g.shape[1]), lambda y: (y, 0)) for g in (dq_t, dk_t, dv_t)],
-        out_specs=[one, one, two, two],
-        out_shape=[first, first, second, second],
+        out_specs=[block, block],
+        out_shape=[shape, shape],
         scratch_shapes=[pltpu.VMEM((width, tokens), BF)],
         compiler_params=pltpu.CompilerParams(vmem_limit_bytes=40 * 1024 * 1024),
         cost_estimate=cost(5),
@@ -821,7 +813,6 @@
 
     shard = jnp.concatenate([*w_qkv, w_out.T], axis=1)
     wide = shard.shape[1] // 2
-    cut = 5 * part // 3
     chips = width // (2 * rows)
     along_z = gather_finish(gather_start(shard, "z"), "z", 0)
     one = gather_start(along_z[:, :, :wide], "x")
@@ -841,60 +832,62 @@
         ctx_t, stacked, cot, heads_all, rest, hidden_bias, vector_rows, part
     )
     output_got = shifted(output, "y", 1)
-    down_pending = start_core(*outer(core, d_two_low_t, active, rows))
-    ((down_sum,),) = tie_sums([down_pending])
-    down_pending = start(down_sum, "x", 2)
-    below = down(
-        d_two_low, d_two, slope, unit_one, inv_one, heads_all, rest, vector_rows, part,
-        after=down_pending[2],
-    )
-    (down_sum,), output_got, below = tie_sums([down_pending], output_got, below)
-    d_hidden, d_one, d_one_low_t, dctx_t, sums_one, sums_hidden = below
+    d_hidden, d_one, d_one_low_t, dctx_t, sums_one, sums_hidden = down(
+        d_two_low, d_two, slope, unit_one, inv_one, heads_all, rest, vector_rows, part
+    )
+    in_grads = outer_in(low_t, d_hidden, d_one_low_t, ctx_t, rows)
+    in_sum = lax.psum_scatter(in_grads, ("z", "x", "core"), scatter_dimension=0)
+    output_got, in_grads = tie(output_got, in_grads)
+    down_pair = outer(core, d_two_low_t, active, rows, after=(in_grads,))
+    down_pending = start_core(*down_pair)
+    sums_small = jnp.concatenate(
+        [jnp.sum(sums_hidden, axis=(0, 1, 3)).reshape(-1)]
+        + [s[i] for i in range(3) for s in (jnp.sum(sums_one, axis=(0, 2)), jnp.sum(sums_two, axis=(0, 2)))]
+    )
+    half_back = functools.partial(attention_back, q_t, k_t, v_t, probs, inverse, ctx_t, dctx_t)
+    grads = half_back((), heads, 0, 1, after=down_pair)
+    (down_sum,), grads = tie_sums([down_pending], grads)
     down_pending = start(down_sum, "y", 0)
-    in_grads = outer_in(low_t, d_hidden, d_one_low_t, ctx_t, rows, after=down_pending[2])
-    in_sum = lax.psum_scatter(in_grads, ("z", "x", "core"), scatter_dimension=0)
-    (down_sum,), in_grads = tie_sums([down_pending], in_grads)
-    down_pending = start(down_sum, "z", 0)
-    grads = attention_back(
-        q_t, k_t, v_t, probs, inverse, ctx_t, dctx_t, (), heads, 0, heads // 2, after=down_pending[2]
-    )
-    (down_sum,), grads = tie_sums([down_pending], grads)
-    down_share = total(down_sum)
+    grads = half_back(tuple(grads), heads, 1, heads // 2 - 1, after=down_pending[2])
     dq_t, dk_t, dv_t, held = grads
-    pairs = project_back(core, stacked, dq_t, dk_t, dv_t, halves, rows, cut)
-    pending = [start_core(*pairs[:2]), start_core(*pairs[2:])]
+    pair = project_back(core, stacked, dq_t, dk_t, dv_t, halves, rows)
+    (down_sum,), pair = tie_sums([down_pending], pair)
+    down_pending = start(down_sum, "x", 1)
+    pending = start_core(*pair)
+    table_grad = table_back(buckets_t, held, bucket_count, after=tuple(pair) + tuple(down_pending[2]))
+    (qkv_sum, down_sum), table_grad = tie_sums([pending, down_pending], table_grad)
+    pending, down_pending = start(qkv_sum, "y", 0), start(down_sum, "z", 0)
     half = me.astype(jnp.int32).reshape(1)
-    grad_in = inputs_back(half, heads_all, d_one, dq_t, dk_t, dv_t, after=pairs)
-    sums, grad_in = tie_sums(pending, grad_in)
-    pending = [start(sums[0], "x", 2), start(sums[1], "y", 0)]
-    table_grad = table_back(buckets_t, held, bucket_count, after=pending[0][2] + pending[1][2])
-    sums, table_grad, grad_in = tie_sums(pending, table_grad, grad_in)
-    pending = [start(sums[0], "y", 0), start(sums[1], "x", 1)]
+    grad_in = inputs_back(
+        half, heads_all, d_one, dq_t, dk_t, dv_t, after=pending[2] + down_pending[2]
+    )
+    table_grad = jnp.sum(table_grad.reshape(bucket_count, heads, -1), axis=2).T
+    small = jnp.concatenate(
+        [jnp.sum(g.astype(F32), axis=1) for g in (dq_t, dv_t)] + [table_grad.reshape(-1), sums_small]
+    )
+    small = sum_pairs(small.reshape(-1, 128), ("core",))
+    outs = (output, output_got)
+    (qkv_sum,), grad_in, small, outs = tie_sums([pending], grad_in, small, outs)
+    pending = start(qkv_sum, "x", 1)
     grad_kept, grad_sent = grad_in
     grad_got = shifted(grad_sent, "y", 1)
 
-    table_grad = jnp.sum(table_grad.reshape(bucket_count, heads, -1), axis=2).T
-    sums_one = jnp.sum(sums_one, axis=(0, 2))
-    sums_two = jnp.sum(sums_two, axis=(0, 2))
-    small = jnp.concatenate(
-        [jnp.sum(g.astype(F32), axis=1) for g in (dq_t, dv_t)]
-        + [table_grad.reshape(-1), jnp.sum(sums_hidden, axis=(0, 1, 3)).reshape(-1)]
-        + [s[i] for i in range(3) for s in (sums_one, sums_two)]
-    )
-    small = sum_pairs(small.reshape(-1, 128), ("core", "x"))
-    sums, small = tie_sums(pending, small)
-    pending = start_joined(sums, "z")
+    small = sum_pairs(small, ("z",))
+    (qkv_sum,), small = tie_sums([pending], small)
+    pending = start(qkv_sum, "z", 0)
+    down_share = total(down_pending[0] + down_pending[1])
     in_pending = start([in_sum], "y", 0)
     in_share = total(in_pending[0] + in_pending[1])
-    small = sum_pairs(small, ("y", "z")).reshape(-1)
+    small = sum_pairs(small, ("x", "y")).reshape(-1)
     first_kept = me == 0
+    output, output_got = outs
     outs = jnp.stack(
         [jnp.where(first_kept, output, output_got), jnp.where(first_kept, output_got, output)]
     ).reshape(halves, 2, seq, width)
     grad_ins = jnp.stack(
         [jnp.where(first_kept, grad_kept, grad_got), jnp.where(first_kept, grad_got, grad_kept)]
     ).reshape(halves, 2, seq, width // halves)
-    qkv_share = total(pending)
+    qkv_share = total(pending[0] + pending[1])
     ends = [2 * width, 2 * width + heads * bucket_count]
     ends.append(ends[1] + halves * ffn)
     grad_b_qv = mine(jnp.transpose(small[: ends[0]].reshape(2, halves, part), (1, 0, 2)))

time: 317 us -> 306 us (0.965)
  waiting for transfers between devices: 56.9 us -> 44.3 us
  other arithmetic: 38.4 us -> 31.4 us
  starting transfers between devices: 35.9 us -> 41.3 us
    ppermute x28 -> x25, waiting for transfers between devices: 48.9 us -> 35.9 us  [shifted(): lax.ppermute(value, axis, [(i, (i + step) % size) for i in range(size)])]
    ppermute x5, starting transfers between devices: 4.43 us -> 9.12 us  [sum_pairs(): lax.ppermute(value, axis, [(i, i ^ step) for i in range(size)])]
    all_gather x1, waiting for transfers between devices: 2.07 us -> 5.74 us  [shards(): lax.all_gather(jnp.concatenate([w_in, w_down.T], axis=1), ('y', 'z', 'x',...]
    pallas_call x11 -> x12, Pallas kernels: 145 us -> 148 us  [call(): pl.pallas_call(body, in_specs=in_specs + anywhere, **settings)]
    ppermute x5, waiting for transfers between devices: 5.87 us -> 2.58 us  [sum_pairs(): lax.ppermute(value, axis, [(i, i ^ step) for i in range(size)])]
    convert_element_type x7 -> x6, other arithmetic: 10.9 us -> 9.11 us  [start(): out = [total(at(lax.rem(me + k, size))).astype(BF) for k in range(1, size)]]
    unnamed x82 -> x70, local copies, waits for them, and re-layouts: 8.53 us -> 9.33 us
    ppermute x28 -> x25, starting transfers between devices: 31.4 us -> 32.1 us  [shifted(): lax.ppermute(value, axis, [(i, (i + step) % size) for i in range(size)])]
  transfers between devices with their start and end apart: 35 -> 32, of which waited for: 13 -> 13; matrix products, arithmetic and copies ran while one was open for 17% -> 15% of each run, Pallas kernels for 35% -> 40%
where the time goes in v1:
time: 306 us; the launch traced here: 304 us
  Pallas kernels  148 us (48%)
  waiting for transfers between devices  44.3 us (14%)
  starting transfers between devices  41.3 us (13%)
  other arithmetic  31.4 us (10%)
  local copies, waits for them, and re-layouts  23.9 us (8%)
  between operations  14.7 us (5%)
    pallas_call x12, Pallas kernels, call(): pl.pallas_call(body, in_specs=in_specs + anywhere, **settings)  148 us
    ppermute x25, waiting for transfers between devices, shifted(): lax.ppermute(value, axis, [(i, (i + step) % size) for i in range(size)])  35.9 us
    ppermute x25, starting transfers between devices, shifted(): lax.ppermute(value, axis, [(i, (i + step) % size) for i in range(size)])  32.1 us
    unnamed x70, local copies, waits for them, and re-layouts  9.33 us
    ppermute x5, starting transfers between devices, sum_pairs(): lax.ppermute(value, axis, [(i, i ^ step) for i in range(size)])  9.12 us
    convert_element_type x6, other arithmetic, start(): out = [total(at(lax.rem(me + k, size))).astype(BF) for k in range(1, size)]  9.11 us
  transfers between devices with their start and end apart: 32, of which 13 were waited for; matrix products, arithmetic and copies ran while one was open for 15% of the time, Pallas kernels for 40%

profile of v1, /device:TPU:0, one launch (start us, length us, event | category | flops | bytes accessed | tf_op | source)
XLA Modules:
  0.0 303.6 jit_solution(15951604079880548369)
XLA Ops:
  7.2 1.9 pad_maximum_fusion.9
  10.0 1.4 pad_maximum_fusion.10
  11.4 5.0 %collective-permute-start = (bf16[48,1536]{1,0:T(8,128)(2,1)}, bf16[48,1536]{1,0:T(8,128)(2,1)S(1)}, u32[]{:S(2)}, u32[]{:S(2)}) collective-permute-start(bf16[48,1536]{1,0:T(8,128)(2,1)} %pad_maximum_fusion.10), channel_id=1, source_target_pairs={{0,24},{8,0},{16,8},{24,16},{1,25},{9,1},{17,9},{25,17},{2,26},{10... | collective-permute-start | bytes 442376 | tf_op jit(solution)/shard_map/ppermute | solution.py:685
  20.3 1.5 collective-permute-start.5
  26.0 7.8 %collective-permute-done.1 = bf16[48,1536]{1,0:T(8,128)(2,1)S(1)} collective-permute-done((bf16[48,1536]{1,0:T(8,128)(2,1)}, bf16[48,1536]{1,0:T(8,128)(2,1)S(1)}, u32[]{:S(2)}, u32[]{:S(2)}) %collective-permute-start.1) | collective-permute-done | bytes 147488 | tf_op jit(solution)/shard_map/ppermute | solution.py:685
  36.0 1.6 collective-permute-start.3
  37.6 1.7 collective-permute-start.4
  40.8 8.6 %shard_map.272.refs_3_ = bf16[12,512,1024]{2,1,0:T(8,128)(2,1)} custom-call(s32[1]{0:T(128)} %dynamic_slice.183.refs_0_, s32[512,512]{1,0:T(8,128)} %bitcast.188, s32[1,512]{1,0:T(1,128)} %constant_dynamic-slice_fusion.3.refs_2_, s32[512,1]{1,0:T(8,128)} %copy.51.refs_3_, f32[12,128]{1,0:T(8,128)} %pad.15.refs_4_), custom_call_target="tpu_custom_call" | custom-call | flops 90000000 | bytes 90000 | tf_op jit(solution)/shard_map/pallas_call | solution.py:272
  50.7 15.1 %collective-permute-done.7 = bf16[2,4,48,768]{3,2,1,0:T(8,128)(2,1)S(1)} collective-permute-done((bf16[2,4,48,768]{3,2,1,0:T(8,128)(2,1)S(1)}, bf16[2,4,48,768]{3,2,1,0:T(8,128)(2,1)S(1)}, u32[]{:S(2)}, u32[]{:S(2)}) %collective-permute-start.7) | collective-permute-done | bytes 589856 | tf_op jit(solution)/shard_map/ppermute | solution.py:685
  68.4 1.5 dynamic-slice_bitcast_fusion.2
  74.4 7.8 %shard_map.273 = (bf16[768,1024]{1,0:T(8,128)(2,1)}, bf16[768,512]{1,0:T(8,128)(2,1)}, bf16[768,512]{1,0:T(8,128)(2,1)}, bf16[2,8,2,48,1536]{4,3,2,1,0:T(8,128)(2,1)}) custom-call(s32[1]{0:T(128)} %bitcast.refs_0_, bf16[2,8,48,768]{3,2,1,0:T(8,128)(2,1)} %copy-done.8, bf16[2,8,48,768]{3,2,1,0:T(8,128)(2,1)} %bitcast.193, ...), custom_call_target="tpu_custom_call" | custom-call | flops 60000000 | bytes 60000 | tf_op jit(solution)/shard_map/pallas_call | solution.py:272
  82.2 16.2 %shard_map.274 = (bf16[12,512,1024]{2,1,0:T(8,128)(2,1)}, bf16[768,1024]{1,0:T(8,128)(2,1)S(1)}, f32[12,1,1024]{2,1,0:T(1,128)S(1)}) custom-call(bf16[768,1024]{1,0:T(8,128)(2,1)} %get-tuple-element.81.refs_0_, bf16[768,512]{1,0:T(8,128)(2,1)} %get-tuple-element.82.refs_1_, bf16[768,512]{1,0:T(8,128)(2,1)} %get-tuple-element.83.refs_2_, ...), custom_call_target="tpu_custom_call" | custom-call | flops 180000000 | bytes 180000 | tf_op jit(solution)/shard_map/pallas_call | solution.py:272
  99.6 5.7 %all-gather.3.cloned.1.call-done = bf16[1536,3072]{1,0:T(8,128)(2,1)} async-done(((bf16[48,3072]{1,0:T(8,128)(2,1)}), bf16[1536,3072]{1,0:T(8,128)(2,1)}) %all-gather.3.cloned.1.call-update) | async-done | bytes 9437200 | tf_op jit(solution)/shard_map/all_gather | solution.py:790
  105.3 25.4 %shard_map.275 = (bf16[1024,768]{1,0:T(8,128)(2,1)}, bf16[768,1024]{1,0:T(8,128)(2,1)}, bf16[2,1024,1536]{2,1,0:T(8,128)(2,1)}, bf16[2,1024,1536]{2,1,0:T(8,128)...) custom-call(bf16[768,1024]{1,0:T(8,128)(2,1)} %copy-done.4, ...), custom_call_target="tpu_custom_call" | custom-call | flops 200000000 | bytes 200000 | tf_op jit(solution)/shard_map/pallas_call | solution.py:272
  130.7 1.5 collective-permute-start.10
  132.3 22.4 %shard_map.276 = (bf16[2,1024,1536]{2,1,0:T(8,128)(2,1)}, f32[1024,768]{1,0:T(8,128)}, bf16[768,1024]{1,0:T(8,128)(2,1)}, bf16[768,1024]{1,0:T(8,128)(2,1)}, f32...) custom-call(bf16[1024,768]{1,0:T(8,128)(2,1)} %get-tuple-element.91.refs_0_, f32[1024,768]{1,0:T(8,128)} %get-tuple-element.92.refs_1_, ...), custom_call_target="tpu_custom_call" | custom-call | flops 180000000 | bytes 180000 | tf_op jit(solution)/shard_map/pallas_call | solution.py:272
  154.6 10.3 %shard_map.277.refs_3_ = bf16[16,2,48,1920]{3,2,1,0:T(8,128)(2,1)S(1)} custom-call(bf16[768,1024]{1,0:T(8,128)(2,1)} %get-tuple-element.90.refs_0_, bf16[2,1024,1536]{2,1,0:T(8,128)(2,1)} %get-tuple-element.96.refs_1_, bf16[768,1024]{1,0:T(8,128)(2,1)} %get-tuple-element.97.refs_2_, bf16[768,1024]{1,0:T(8,128)(2,1)} %copy-done.4), custom_call_target="tpu_custom_call" | custom-call | flops 60000000 | bytes 60000 | tf_op jit(solution)/shard_map/pallas_call | solution.py:272
  165.0 2.5 copy-done.2
  167.6 10.1 %shard_map.278 = (bf16[2,8,48,1536]{3,2,1,0:T(8,128)(2,1)}, bf16[2,8,48,1536]{3,2,1,0:T(8,128)(2,1)}) custom-call(s32[1]{0:T(128)} %bitcast.refs_0_, bf16[768,1024]{1,0:T(8,128)(2,1)} %get-tuple-element.87.refs_1_, bf16[2,1024,1536]{2,1,0:T(8,128)(2,1)} %get-tuple-element.88.refs_2_, bf16[16,2,48,1920]{3,2,1,0:T(8,128)(2,1)} %copy-done.2), custom_call_target="tpu_custom_call" | custom-call | flops 50000000 | bytes 50000 | tf_op jit(solution)/shard_map/pallas_call | solution.py:272
  177.7 5.9 %shard_map.279 = (bf16[768,1024]{1,0:T(8,128)(2,1)}, bf16[768,512]{1,0:T(8,128)(2,1)}, bf16[768,512]{1,0:T(8,128)(2,1)}, bf16[32,192,512]{2,1,0:T(8,128)(2,1)}) custom-call(bf16[768,1024]{1,0:T(8,128)(2,1)} %get-tuple-element.81.refs_0_, bf16[768,512]{1,0:T(8,128)(2,1)} %get-tuple-element.82.refs_1_, bf16[768,512]{1,0:T(8,128)(2,1)} %get-tuple-element.83.refs_2_, ...), custom_call_target="tpu_custom_call" | custom-call | flops 99999997952 | bytes 100000000 | tf_op jit(solution)/shard_map/pallas_call | solution.py:272
  183.6 1.6 fusion.3.refs_11_
  185.4 1.4 collective-permute-start.12
  186.9 15.9 %shard_map.280 = (bf16[768,1024]{1,0:T(8,128)(2,1)}, bf16[768,512]{1,0:T(8,128)(2,1)}, bf16[768,512]{1,0:T(8,128)(2,1)}, bf16[32,192,512]{2,1,0:T(8,128)(2,1)}) custom-call(bf16[768,1024]{1,0:T(8,128)(2,1)} %get-tuple-element.81.refs_0_, ...), custom_call_target="tpu_custom_call", output_to_operand_aliasing={{0}: (7, {}), {1}: (8, {}), {2}: (9, {}), {3}: (10, {})} | custom-call | flops 499999997952 | bytes 500000000 | tf_op jit(solution)/shard_map/pallas_call | solution.py:272
  202.8 7.7 %shard_map.281 = (bf16[2,8,48,1152]{3,2,1,0:T(8,128)(2,1)S(1)}, bf16[2,8,48,1152]{3,2,1,0:T(8,128)(2,1)}) custom-call(s32[1]{0:T(128)} %bitcast.refs_0_, bf16[1024,768]{1,0:T(8,128)(2,1)} %pad_maximum_fusion.1.refs_5_.refs_1_, bf16[768,1024]{1,0:T(8,128)(2,1)} %get-tuple-element.113.refs_2_.refs_3_, bf16[768,512]{1,0:T(8,128)(2,1)} %get-tuple-element.114.refs_3_.refs_4_, ...), custom_call_target="tpu_custom_call" | custom-call | flops 50000000 | bytes 50000 | tf_op jit(solution)/shard_map/pallas_call | solution.py:272
  210.5 3.6 %collective-permute-done.12 = bf16[4,2,48,1536]{3,2,1,0:T(8,128)(2,1)} collective-permute-done((bf16[4,2,48,1536]{3,2,1,0:T(8,128)(2,1)}, bf16[4,2,48,1536]{3,2,1,0:T(8,128)(2,1)}, u32[]{:S(2)}, u32[]{:S(2)}) %collective-permute-start.12) | collective-permute-done | bytes 1179680 | tf_op jit(solution)/shard_map/ppermute | solution.py:685
  214.2 1.7 fusion.4.refs_4_
  215.9 1.4 collective-permute-start.14
  218.5 1.8 convert_reduce_fusion
  220.5 9.6 %shard_map.282 = f32[32,192]{1,0:T(8,128)S(1)} custom-call(s32[512,512]{1,0:T(8,128)} %bitcast.189, bf16[32,192,512]{2,1,0:T(8,128)(2,1)} %get-tuple-element.121.refs_1_, bf16[2,8,48,1152]{3,2,1,0:T(8,128)(2,1)S(1)} %get-tuple-element.118.refs_2_, bf16[2,8,48,1152]{3,2,1,0:T(8,128)(2,1)} %get-tuple-element.119.refs_3_, bf16[4,48,1536]{2,1,0:T(8,128)(2,1)S(1)} %fusion.4.refs_4_), custom_call_target="tpu_custom_call" | custom-call | flops 60000000 | bytes 60000 | tf_op jit(solution)/shard_map/pallas_call | solution.py:272
  230.1 1.7 collective-permute-done.14
  232.0 1.4 fusion.5.refs_6_
  233.4 1.6 collective-permute-start.15
  235.1 1.8 fusion.14
  236.9 1.7 collective-permute-start.27
  239.3 2.7 collective-permute-start.29
  242.0 8.2 %shard_map.283 = (bf16[1024,384]{1,0:T(8,128)(2,1)S(1)}, bf16[1024,384]{1,0:T(8,128)(2,1)S(1)}) custom-call(s32[1]{0:T(128)} %bitcast.40.refs_0_, bf16[2,768,1536]{2,1,0:T(8,128)(2,1)} %bitcast.187, f32[1024,768]{1,0:T(8,128)} %get-tuple-element.123.refs_2_, bf16[768,1024]{1,0:T(8,128)(2,1)} %get-tuple-element.113.refs_2_.refs_3_, ...), custom_call_target="tpu_custom_call" | custom-call | flops 50000000 | bytes 50000 | tf_op jit(solution)/shard_map/pallas_call | solution.py:272
  250.2 4.5 %collective-permute-done.15 = bf16[4,2,48,1152]{3,2,1,0:T(8,128)(2,1)S(1)} collective-permute-done((bf16[4,2,48,1152]{3,2,1,0:T(8,128)(2,1)S(1)}, bf16[4,2,48,1152]{3,2,1,0:T(8,128)(2,1)S(1)}, u32[]{:S(2)}, u32[]{:S(2)}) %collective-permute-start.15) | collective-permute-done | bytes 884768 | tf_op jit(solution)/shard_map/ppermute | solution.py:685
  254.7 1.5 collective-permute-start.19
  257.5 1.4 collective-permute-start.18
  259.2 2.0 fusion.13
  261.6 4.6 %collective-permute-start.20 = (f32[75,128]{1,0:T(8,128)S(1)}, f32[75,128]{1,0:T(8,128)S(1)}, u32[]{:S(2)}, u32[]{:S(2)}) collective-permute-start(f32[75,128]{1,0:T(8,128)S(1)} %add.498), channel_id=1, source_target_pairs={{0,16},{8,24},{16,0},{24,8},{1,17},{9,25},{17,1},{25,9},{2,18},{10... | collective-permute-start | bytes 115208 | tf_op jit(solution)/shard_map/ppermute | solution.py:751
  266.5 1.8 collective-permute-done.20
  268.3 1.5 collective-permute-start.24
  269.8 1.9 fusion.2
  272.3 1.5 collective-permute-start.25
  275.1 3.2 %collective-permute-start.21 = (bf16[48,1152]{1,0:T(8,128)(2,1)S(1)}, bf16[48,1152]{1,0:T(8,128)(2,1)S(1)}, u32[]{:S(2)}, u32[]{:S(2)}) collective-permute-start(bf16[48,1152]{1,0:T(8,128)(2,1)S(1)} %get-tuple-element.163), channel_id=1, source_target_pairs={{0,8},{8,16},{16,24},{24,0},{1,9},{9,17},{17,25},{25,1},{2,10},{10... | collective-permute-start | bytes 331784 | tf_op jit(solution)/shard_map/ppermute | solution.py:685
  284.7 1.5 collective-permute-done.22
  289.7 1.6 collective-permute-start.26
  (185 shorter events, 44.4 us)
Async XLA Ops:
  7.2 14.6 %copy-start = (s32[2,512,512]{2,1,0:T(8,128)S(1)}, s32[2,512,512]{2,1,0:T(8,128)}, u32[]{:S(2)}) copy-start(s32[2,512,512]{2,1,0:T(8,128)} %param.21) | copy-start | bytes 6291460
  7.2 98.1 %all-gather.3.cloned.1.call-start = ((), (), s32[]{:S(2)}) async-start(), calls=%async_computation.2 | async-start | bytes 9732096 | tf_op jit(solution)/shard_map/all_gather | solution.py:790
  9.1 279.7 %reduce-scatter.2.cloned.1.call-start = ((), (), s32[]{:S(2)}) async-start(), calls=%async_computation.1 | async-start | bytes 6266880 | tf_op jit(solution)/shard_map/reduce_scatter | solution.py:839
  11.4 14.6 %collective-permute-start = (bf16[48,1536]{1,0:T(8,128)(2,1)}, bf16[48,1536]{1,0:T(8,128)(2,1)S(1)}, u32[]{:S(2)}, u32[]{:S(2)}) collective-permute-start(bf16[48,1536]{1,0:T(8,128)(2,1)} %pad_maximum_fusion.10), channel_id=1, source_target_pairs={{0,24},{8,0},{16,8},{24,16},{1,25},{9,1},{17,9},{25,17},{2,26},{10... | collective-permute-start | bytes 442376 | tf_op jit(solution)/shard_map/ppermute | solution.py:685
  16.5 17.3 %collective-permute-start.1 = (bf16[48,1536]{1,0:T(8,128)(2,1)}, bf16[48,1536]{1,0:T(8,128)(2,1)S(1)}, u32[]{:S(2)}, u32[]{:S(2)}) collective-permute-start(bf16[48,1536]{1,0:T(8,128)(2,1)} %pad_maximum_fusion.10), channel_id=1, source_target_pairs={{0,16},{8,24},{16,0},{24,8},{1,17},{9,25},{17,1},{25,9},{2,18},{10... | collective-permute-start | bytes 442376 | tf_op jit(solution)/shard_map/ppermute | solution.py:685
  16.5 17.3 %collective-permute-start.2 = (bf16[48,1536]{1,0:T(8,128)(2,1)}, bf16[48,1536]{1,0:T(8,128)(2,1)}, u32[]{:S(2)}, u32[]{:S(2)}) collective-permute-start(bf16[48,1536]{1,0:T(8,128)(2,1)} %pad_maximum_fusion.10), channel_id=1, source_target_pairs={{0,8},{8,16},{16,24},{24,0},{1,9},{9,17},{17,25},{25,1},{2,10},{10... | collective-permute-start | bytes 442376 | tf_op jit(solution)/shard_map/ppermute | solution.py:685
  18.3 3.5 %copy-start.21 = (bf16[32,6]{1,0:T(8,128)(2,1)}, bf16[32,6]{1,0:T(8,128)(2,1)S(1)}, u32[]{:S(2)}) copy-start(bf16[32,6]{1,0:T(8,128)(2,1)S(1)} %copy.49) | copy-start | bytes 1156
  20.3 19.0 %collective-permute-start.5 = (bf16[38,384]{1,0:T(8,128)(2,1)}, bf16[38,384]{1,0:T(8,128)(2,1)}, u32[]{:S(2)}, u32[]{:S(2)}) collective-permute-start(bf16[38,384]{1,0:T(8,128)(2,1)} %fusion.24), channel_id=1, source_target_pairs={{0,1},{1,0},{2,3},{3,2},{4,5},{5,4},{6,7},{7,6},{8,9},{9,8},{10,11... | collective-permute-start | bytes 87560 | tf_op jit(solution)/shard_map/ppermute | solution.py:685
  21.9 3.5 %copy-start.24 = (s32[2,512]{1,0:T(2,128)S(1)}, s32[2,512]{1,0:T(2,128)}, u32[]{:S(2)}) copy-start(s32[2,512]{1,0:T(2,128)} %param.20) | copy-start | bytes 12292
  21.9 11.9 %copy-start.17 = (bf16[384,48]{0,1:T(8,128)(2,1)S(1)}, bf16[384,48]{0,1:T(8,128)(2,1)}, u32[]{:S(2)}) copy-start(bf16[384,48]{0,1:T(8,128)(2,1)} %param.24) | copy-start | bytes 110596
  34.8 4.4 %copy-start.22 = (bf16[32,6]{1,0:T(8,128)(2,1)S(1)}, bf16[32,6]{1,0:T(8,128)(2,1)}, u32[]{:S(2)}) copy-start(bf16[32,6]{1,0:T(8,128)(2,1)} %copy-done.21) | copy-start | bytes 1156
  34.9 4.4 %copy-start.23 = (bf16[2,384]{1,0:T(2,128)(2,1)S(1)}, bf16[2,384]{1,0:T(2,128)(2,1)}, u32[]{:S(2)}) copy-start(bf16[2,384]{1,0:T(2,128)(2,1)} %param.23) | copy-start | bytes 4612
  36.0 13.4 %collective-permute-start.3 = (bf16[4,48,768]{2,1,0:T(8,128)(2,1)S(1)}, bf16[4,48,768]{2,1,0:T(8,128)(2,1)S(1)}, u32[]{:S(2)}, u32[]{:S(2)}) collective-permute-start(bf16[4,48,768]{2,1,0:T(8,128)(2,1)S(1)} %get-tuple-element.78), channel_id=1, source_target_pairs={{0,4},{4,0},{1,5},{5,1},{2,6},{6,2},{3,7},{7,3},{8,12},{12,8},{9,1... | collective-permute-start | bytes 884744 | tf_op jit(solution)/shard_map/ppermute | solution.py:685
  37.6 11.8 %collective-permute-start.4 = (bf16[4,48,768]{2,1,0:T(8,128)(2,1)S(1)}, bf16[4,48,768]{2,1,0:T(8,128)(2,1)S(1)}, u32[]{:S(2)}, u32[]{:S(2)}) collective-permute-start(bf16[4,48,768]{2,1,0:T(8,128)(2,1)S(1)} %get-tuple-element.80), channel_id=1, source_target_pairs={{0,1},{1,0},{2,3},{3,2},{4,5},{5,4},{6,7},{7,6},{8,9},{9,8},{10,11... | collective-permute-start | bytes 884744 | tf_op jit(solution)/shard_map/ppermute | solution.py:685
  49.6 16.1 %collective-permute-start.7 = (bf16[2,4,48,768]{3,2,1,0:T(8,128)(2,1)S(1)}, bf16[2,4,48,768]{3,2,1,0:T(8,128)(2,1)S(1)}, u32[]{:S(2)}, u32[]{:S(2)}) collective-permute-start(bf16[2,4,48,768]{3,2,1,0:T(8,128)(2,1)S(1)} %pad_maximum_fusion.8), channel_id=1, source_target_pairs={{0,4},{4,0},{1,5},{5,1},{2,6},{6,2},{3,7},{7,3},{8,12},{12,8},{9,1... | collective-permute-start | bytes 1769480 | tf_op jit(solution)/shard_map/ppermute | solution.py:685
  50.1 16.0 %collective-permute-start.6 = (bf16[4,2,48,768]{3,2,0,1:T(8,128)(2,1)S(1)}, bf16[4,2,48,768]{3,2,0,1:T(8,128)(2,1)S(1)}, u32[]{:S(2)}, u32[]{:S(2)}) collective-permute-start(bf16[4,2,48,768]{3,2,0,1:T(8,128)(2,1)S(1)} %pad_maximum_fusion.7), channel_id=1, source_target_pairs={{0,1},{1,0},{2,3},{3,2},{4,5},{5,4},{6,7},{7,6},{8,9},{9,8},{10,11... | collective-permute-start | bytes 1769480 | tf_op jit(solution)/shard_map/ppermute | solution.py:685
  66.0 8.3 %collective-permute-start.9 = (bf16[2,8,48,768]{3,2,1,0:T(8,128)(2,1)S(1)}, bf16[2,8,48,768]{3,2,1,0:T(8,128)(2,1)}, u32[]{:S(2)}, u32[]{:S(2)}) collective-permute-start(bf16[2,8,48,768]{3,2,1,0:T(8,128)(2,1)S(1)} %bitcast.192), channel_id=1, source_target_pairs={{0,2},{2,0},{1,3},{3,1},{4,6},{6,4},{5,7},{7,5},{8,10},{10,8},{9,1... | collective-permute-start | bytes 3538952 | tf_op jit(solution)/shard_map/ppermute | solution.py:685
  67.3 7.1 %collective-permute-start.8 = (bf16[2,8,48,768]{3,2,1,0:T(8,128)(2,1)S(1)}, bf16[2,8,48,768]{3,2,1,0:T(8,128)(2,1)}, u32[]{:S(2)}, u32[]{:S(2)}) collective-permute-start(bf16[2,8,48,768]{3,2,1,0:T(8,128)(2,1)S(1)} %pad_maximum_fusion.3.refs_1_), channel_id=1, source_target_pairs={{0,2},{2,0},{1,3},{3,1},{4,6},{6,4},{5,7},{7,5},{8,10},{10,8},{9,1... | collective-permute-start | bytes 3538952 | tf_op jit(solution)/shard_map/ppermute | solution.py:685
  99.6 31.2 %copy-start.5 = (f32[12,1,1024]{2,1,0:T(1,128)}, f32[12,1,1024]{2,1,0:T(1,128)S(1)}, u32[]{:S(2)}) copy-start(f32[12,1,1024]{2,1,0:T(1,128)S(1)} %get-tuple-element.102.refs_4_) | copy-start | bytes 147460
  130.7 36.8 %collective-permute-start.10 = (bf16[1024,768]{1,0:T(8,128)(2,1)}, bf16[1024,768]{1,0:T(8,128)(2,1)S(1)}, u32[]{:S(2)}, u32[]{:S(2)}) collective-permute-start(bf16[1024,768]{1,0:T(8,128)(2,1)} %get-tuple-element.132), channel_id=1, source_target_pairs={{0,1},{1,0},{2,3},{3,2},{4,5},{5,4},{6,7},{7,6},{8,9},{9,8},{10,11... | collective-permute-start | bytes 4718600 | tf_op jit(solution)/shard_map/ppermute | solution.py:685
  167.6 10.1 %copy-start.12 = (bf16[1024,768]{1,0:T(8,128)(2,1)}, bf16[1024,768]{1,0:T(8,128)(2,1)S(1)}, u32[]{:S(2)}) copy-start(bf16[1024,768]{1,0:T(8,128)(2,1)S(1)} %collective-permute-done.10) | copy-start | bytes 4718596
  177.7 5.9 %collective-permute-start.11 = (bf16[2,8,48,1536]{3,2,1,0:T(8,128)(2,1)}, bf16[2,8,48,1536]{3,2,1,0:T(8,128)(2,1)S(1)}, u32[]{:S(2)}, u32[]{:S(2)}) collective-permute-start(bf16[2,8,48,1536]{3,2,1,0:T(8,128)(2,1)} %get-tuple-element.100.refs_8_), channel_id=1, source_target_pairs={{0,2},{2,0},{1,3},{3,1},{4,6},{6,4},{5,7},{7,5},{8,10},{10,8},{9,1... | collective-permute-start | bytes 7077896 | tf_op jit(solution)/shard_map/ppermute | solution.py:685
  177.7 5.9 %copy-start.9 = (bf16[2,8,48,1536]{3,2,1,0:T(8,128)(2,1)S(1)}, bf16[2,8,48,1536]{3,2,1,0:T(8,128)(2,1)}, u32[]{:S(2)}) copy-start(bf16[2,8,48,1536]{3,2,1,0:T(8,128)(2,1)} %get-tuple-element.99.refs_7_) | copy-start | bytes 7077892
  185.4 28.6 %collective-permute-start.12 = (bf16[4,2,48,1536]{3,2,1,0:T(8,128)(2,1)}, bf16[4,2,48,1536]{3,2,1,0:T(8,128)(2,1)}, u32[]{:S(2)}, u32[]{:S(2)}) collective-permute-start(bf16[4,2,48,1536]{3,2,1,0:T(8,128)(2,1)} %fusion.3.refs_11_), channel_id=1, source_target_pairs={{0,1},{1,0},{2,3},{3,2},{4,5},{5,4},{6,7},{7,6},{8,9},{9,8},{10,11... | collective-permute-start | bytes 3538952 | tf_op jit(solution)/shard_map/ppermute | solution.py:685
  202.8 11.3 %copy-start.19 = (f32[4,3,8,768]{3,2,1,0:T(8,128)S(1)}, f32[4,3,8,768]{3,2,1,0:T(8,128)}, u32[]{:S(2)}) copy-start(f32[4,3,8,768]{3,2,1,0:T(8,128)} %get-tuple-element.129) | copy-start | bytes 884740
  202.8 11.4 %copy-start.18 = (f32[4,3,8,768]{3,2,1,0:T(8,128)S(1)}, f32[4,3,8,768]{3,2,1,0:T(8,128)}, u32[]{:S(2)}) copy-start(f32[4,3,8,768]{3,2,1,0:T(8,128)} %get-tuple-element.130) | copy-start | bytes 884740
  210.5 21.5 %copy-start.3 = (bf16[2,8,48,1152]{3,2,1,0:T(8,128)(2,1)}, bf16[2,8,48,1152]{3,2,1,0:T(8,128)(2,1)S(1)}, u32[]{:S(2)}) copy-start(bf16[2,8,48,1152]{3,2,1,0:T(8,128)(2,1)S(1)} %get-tuple-element.118.refs_2_) | copy-start | bytes 5308420
  214.1 17.7 %collective-permute-start.13 = (bf16[2,8,48,1152]{3,2,1,0:T(8,128)(2,1)}, bf16[2,8,48,1152]{3,2,1,0:T(8,128)(2,1)}, u32[]{:S(2)}, u32[]{:S(2)}) collective-permute-start(bf16[2,8,48,1152]{3,2,1,0:T(8,128)(2,1)} %get-tuple-element.119.refs_3_), channel_id=1, source_target_pairs={{0,2},{2,0},{1,3},{3,1},{4,6},{6,4},{5,7},{7,5},{8,10},{10,8},{9,1... | collective-permute-start | bytes 5308424 | tf_op jit(solution)/shard_map/ppermute | solution.py:685
  215.9 4.3 %copy-start.6 = (bf16[768,512]{1,0:T(8,128)(2,1)S(1)}, bf16[768,512]{1,0:T(8,128)(2,1)}, u32[]{:S(2)}) copy-start(bf16[768,512]{1,0:T(8,128)(2,1)} %get-tuple-element.115.refs_4_.refs_5_) | copy-start | bytes 2359300
  215.9 15.9 %collective-permute-start.14 = (bf16[4,48,1536]{2,1,0:T(8,128)(2,1)S(1)}, bf16[4,48,1536]{2,1,0:T(8,128)(2,1)}, u32[]{:S(2)}, u32[]{:S(2)}) collective-permute-start(bf16[4,48,1536]{2,1,0:T(8,128)(2,1)S(1)} %fusion.4.refs_4_), channel_id=1, source_target_pairs={{0,4},{4,0},{1,5},{5,1},{2,6},{6,2},{3,7},{7,3},{8,12},{12,8},{9,1... | collective-permute-start | bytes 1769480 | tf_op jit(solution)/shard_map/ppermute | solution.py:685
  233.4 21.3 %collective-permute-start.15 = (bf16[4,2,48,1152]{3,2,1,0:T(8,128)(2,1)S(1)}, bf16[4,2,48,1152]{3,2,1,0:T(8,128)(2,1)S(1)}, u32[]{:S(2)}, u32[]{:S(2)}) collective-permute-start(bf16[4,2,48,1152]{3,2,1,0:T(8,128)(2,1)S(1)} %fusion.5.refs_6_), channel_id=1, source_target_pairs={{0,1},{1,0},{2,3},{3,2},{4,5},{5,4},{6,7},{7,6},{8,9},{9,8},{10,11... | collective-permute-start | bytes 2654216 | tf_op jit(solution)/shard_map/ppermute | solution.py:685
  235.1 15.1 %collective-permute-start.16 = (f32[75,128]{1,0:T(8,128)S(1)}, f32[75,128]{1,0:T(8,128)S(1)}, u32[]{:S(2)}, u32[]{:S(2)}) collective-permute-start(f32[75,128]{1,0:T(8,128)S(1)} %bitcast.212), channel_id=1, source_target_pairs={{0,2},{2,0},{1,3},{3,1},{4,6},{6,4},{5,7},{7,5},{8,10},{10,8},{9,1... | collective-permute-start | bytes 115208 | tf_op jit(solution)/shard_map/ppermute | solution.py:751
  236.9 22.0 %collective-permute-start.27 = (bf16[48,1536]{1,0:T(8,128)(2,1)S(1)}, bf16[48,1536]{1,0:T(8,128)(2,1)S(1)}, u32[]{:S(2)}, u32[]{:S(2)}) collective-permute-start(bf16[48,1536]{1,0:T(8,128)(2,1)S(1)} %get-tuple-element.162.refs_7_), channel_id=1, source_target_pairs={{0,8},{8,16},{16,24},{24,0},{1,9},{9,17},{17,25},{25,1},{2,10},{10... | collective-permute-start | bytes 442376 | tf_op jit(solution)/shard_map/ppermute | solution.py:685
  238.6 20.5 %collective-permute-start.28 = (bf16[48,1536]{1,0:T(8,128)(2,1)S(1)}, bf16[48,1536]{1,0:T(8,128)(2,1)S(1)}, u32[]{:S(2)}, u32[]{:S(2)}) collective-permute-start(bf16[48,1536]{1,0:T(8,128)(2,1)S(1)} %get-tuple-element.161.refs_8_), channel_id=1, source_target_pairs={{0,16},{8,24},{16,0},{24,8},{1,17},{9,25},{17,1},{25,9},{2,18},{10... | collective-permute-start | bytes 442376 | tf_op jit(solution)/shard_map/ppermute | solution.py:685
  239.3 19.8 %collective-permute-start.29 = (bf16[48,1536]{1,0:T(8,128)(2,1)S(1)}, bf16[48,1536]{1,0:T(8,128)(2,1)S(1)}, u32[]{:S(2)}, u32[]{:S(2)}) collective-permute-start(bf16[48,1536]{1,0:T(8,128)(2,1)S(1)} %get-tuple-element.160.refs_9_), channel_id=1, source_target_pairs={{0,24},{8,0},{16,8},{24,16},{1,25},{9,1},{17,9},{25,17},{2,26},{10... | collective-permute-start | bytes 442376 | tf_op jit(solution)/shard_map/ppermute | solution.py:685
  254.7 11.5 %copy-start.11 = (bf16[1024,768]{1,0:T(8,128)(2,1)S(1)}, bf16[1024,768]{1,0:T(8,128)(2,1)}, u32[]{:S(2)}) copy-start(bf16[1024,768]{1,0:T(8,128)(2,1)} %get-tuple-element.132) | copy-start | bytes 4718596
  254.7 11.5 %copy-start.13 = (bf16[1024,768]{1,0:T(8,128)(2,1)S(1)}, bf16[1024,768]{1,0:T(8,128)(2,1)}, u32[]{:S(2)}) copy-start(bf16[1024,768]{1,0:T(8,128)(2,1)} %copy-done.12) | copy-start | bytes 4718596
  254.7 6.9 %collective-permute-start.19 = (f32[75,128]{1,0:T(8,128)S(1)}, f32[75,128]{1,0:T(8,128)S(1)}, u32[]{:S(2)}, u32[]{:S(2)}) collective-permute-start(f32[75,128]{1,0:T(8,128)S(1)} %bitcast_add_fusion), channel_id=1, source_target_pairs={{0,8},{8,0},{16,24},{24,16},{1,9},{9,1},{17,25},{25,17},{2,10},{10... | collective-permute-start | bytes 115208 | tf_op jit(solution)/shard_map/ppermute | solution.py:751
  257.5 10.7 %collective-permute-start.18 = (bf16[4,48,1152]{2,1,0:T(8,128)(2,1)S(1)}, bf16[4,48,1152]{2,1,0:T(8,128)(2,1)S(1)}, u32[]{:S(2)}, u32[]{:S(2)}) collective-permute-start(bf16[4,48,1152]{2,1,0:T(8,128)(2,1)S(1)} %fusion.6), channel_id=1, source_target_pairs={{0,4},{4,0},{1,5},{5,1},{2,6},{6,2},{3,7},{7,3},{8,12},{12,8},{9,1... | collective-permute-start | bytes 1327112 | tf_op jit(solution)/shard_map/ppermute | solution.py:685
  261.1 30.2 %collective-permute-start.17 = (bf16[1024,384]{1,0:T(8,128)(2,1)S(1)}, bf16[1024,384]{1,0:T(8,128)(2,1)}, u32[]{:S(2)}, u32[]{:S(2)}) collective-permute-start(bf16[1024,384]{1,0:T(8,128)(2,1)S(1)} %get-tuple-element.135), channel_id=1, source_target_pairs={{0,1},{1,0},{2,3},{3,2},{4,5},{5,4},{6,7},{7,6},{8,9},{9,8},{10,11... | collective-permute-start | bytes 2359304 | tf_op jit(solution)/shard_map/ppermute | solution.py:685
  261.6 6.6 %collective-permute-start.20 = (f32[75,128]{1,0:T(8,128)S(1)}, f32[75,128]{1,0:T(8,128)S(1)}, u32[]{:S(2)}, u32[]{:S(2)}) collective-permute-start(f32[75,128]{1,0:T(8,128)S(1)} %add.498), channel_id=1, source_target_pairs={{0,16},{8,24},{16,0},{24,8},{1,17},{9,25},{17,1},{25,9},{2,18},{10... | collective-permute-start | bytes 115208 | tf_op jit(solution)/shard_map/ppermute | solution.py:751
  268.3 4.0 %collective-permute-start.24 = (f32[75,128]{1,0:T(8,128)S(1)}, f32[75,128]{1,0:T(8,128)S(1)}, u32[]{:S(2)}, u32[]{:S(2)}) collective-permute-start(f32[75,128]{1,0:T(8,128)S(1)} %add.499), channel_id=1, source_target_pairs={{0,4},{4,0},{1,5},{5,1},{2,6},{6,2},{3,7},{7,3},{8,12},{12,8},{9,1... | collective-permute-start | bytes 115208 | tf_op jit(solution)/shard_map/ppermute | solution.py:751
  272.3 8.6 %collective-permute-start.25 = (f32[75,128]{1,0:T(8,128)S(1)}, f32[75,128]{1,0:T(8,128)S(1)}, u32[]{:S(2)}, u32[]{:S(2)}) collective-permute-start(f32[75,128]{1,0:T(8,128)S(1)} %add.516), channel_id=1, source_target_pairs={{0,1},{1,0},{2,3},{3,2},{4,5},{5,4},{6,7},{7,6},{8,9},{9,8},{10,11... | collective-permute-start | bytes 115208 | tf_op jit(solution)/shard_map/ppermute | solution.py:751
  275.1 9.6 %collective-permute-start.21 = (bf16[48,1152]{1,0:T(8,128)(2,1)S(1)}, bf16[48,1152]{1,0:T(8,128)(2,1)S(1)}, u32[]{:S(2)}, u32[]{:S(2)}) collective-permute-start(bf16[48,1152]{1,0:T(8,128)(2,1)S(1)} %get-tuple-element.163), channel_id=1, source_target_pairs={{0,8},{8,16},{16,24},{24,0},{1,9},{9,17},{17,25},{25,1},{2,10},{10... | collective-permute-start | bytes 331784 | tf_op jit(solution)/shard_map/ppermute | solution.py:685
  278.3 7.9 %collective-permute-start.22 = (bf16[48,1152]{1,0:T(8,128)(2,1)S(1)}, bf16[48,1152]{1,0:T(8,128)(2,1)S(1)}, u32[]{:S(2)}, u32[]{:S(2)}) collective-permute-start(bf16[48,1152]{1,0:T(8,128)(2,1)S(1)} %get-tuple-element.165), channel_id=1, source_target_pairs={{0,16},{8,24},{16,0},{24,8},{1,17},{9,25},{17,1},{25,9},{2,18},{10... | collective-permute-start | bytes 331784 | tf_op jit(solution)/shard_map/ppermute | solution.py:685
  279.5 7.4 %collective-permute-start.23 = (bf16[48,1152]{1,0:T(8,128)(2,1)S(1)}, bf16[48,1152]{1,0:T(8,128)(2,1)}, u32[]{:S(2)}, u32[]{:S(2)}) collective-permute-start(bf16[48,1152]{1,0:T(8,128)(2,1)S(1)} %get-tuple-element.164), channel_id=1, source_target_pairs={{0,24},{8,0},{16,8},{24,16},{1,25},{9,1},{17,9},{25,17},{2,26},{10... | collective-permute-start | bytes 331784 | tf_op jit(solution)/shard_map/ppermute | solution.py:685
  289.7 5.6 %collective-permute-start.26 = (bf16[48,1920]{1,0:T(8,128)(2,1)S(1)}, bf16[48,1920]{1,0:T(8,128)(2,1)S(1)}, u32[]{:S(2)}, u32[]{:S(2)}) collective-permute-start(bf16[48,1920]{1,0:T(8,128)(2,1)S(1)} %dynamic-slice_bitcast_fusion.4), channel_id=1, source_target_pairs={{0,1},{1,0},{2,3},{3,2},{4,5},{5,4},{6,7},{7,6},{8,9},{9,8},{10,11... | collective-permute-start | bytes 552968 | tf_op jit(solution)/shard_map/ppermute | solution.py:685
  292.7 4.1 %copy-start.1 = (s32[2,512,512]{2,1,0:T(8,128)S(1)}, s32[2,512,512]{2,1,0:T(8,128)}, u32[]{:S(2)}) copy-start(s32[2,512,512]{2,1,0:T(8,128)} %param.21) | copy-start | bytes 6291460
  (13 other events, 22.1 us)
Sparse Core Ops, SparseCore 0:
  11.5 93.7 all-gather.2
  167.6 94.4 reduce-scatter.1

commit v2 on v1

--- a/solution.py
+++ b/solution.py
@@ -113,9 +113,9 @@
         in_specs=[wide, thin, thin, square] + [pl.BlockSpec(memory_space=pl.ANY)] * len(before),
         out_specs=[square, wide, pl.BlockSpec((count, 1, both), lambda h: (h + begin, 0, 0))],
         out_shape=[
-            jax.ShapeDtypeStruct((heads, seq, both), BF),
-            jax.ShapeDtypeStruct((width, both), BF),
-            jax.ShapeDtypeStruct((heads, 1, both), F32),
+            pltpu.HBM((heads, seq, both), BF),
+            pltpu.HBM((width, both), BF),
+            pltpu.HBM((heads, 1, both), F32),
         ],
         input_output_aliases={4 + i: i for i in range(len(before))},
         compiler_params=pltpu.CompilerParams(vmem_limit_bytes=48 * 1024 * 1024),
@@ -238,7 +238,7 @@
         out_ref[...] = jnp.sum(kept.reshape(buckets, group, value.shape[1]), axis=1)
 
 
-def table_back(buckets_t, held, buckets, group=16, parts=4, after=()):
+def table_back(buckets_t, held, buckets, group=16, parts=8, after=()):
     seq = buckets_t.shape[0]
     cols = held.shape[1]
     return call(
@@ -532,7 +532,7 @@
             pl.BlockSpec((part, tokens), lambda y: (y, 0)),
         ],
         out_specs=pl.BlockSpec((owners, 1, rows, ffn + part), lambda y: (0, y, 0, 0)),
-        out_shape=jax.ShapeDtypeStruct((owners, halves, rows, ffn + part), BF),
+        out_shape=pltpu.HBM((owners, halves, rows, ffn + part), BF),
         compiler_params=pltpu.CompilerParams(vmem_limit_bytes=48 * 1024 * 1024),
         cost_estimate=cost(6),
     )
@@ -607,7 +607,7 @@
     chips = width // (2 * rows)
     part = width // halves
     block = pl.BlockSpec((1, chips, rows, 3 * part), lambda y: (y, 0, 0, 0))
-    shape = jax.ShapeDtypeStruct((halves, chips, rows, 3 * part), BF)
+    shape = pltpu.HBM((halves, chips, rows, 3 * part), BF)
     return call(
         project_back_kernel,
         after,
@@ -673,7 +673,7 @@
             thin,
         ],
         out_specs=[out, out],
-        out_shape=[jax.ShapeDtypeStruct((tokens, width // 2), BF)] * 2,
+        out_shape=[pltpu.HBM((tokens, width // 2), BF)] * 2,
         scratch_shapes=[pltpu.VMEM((tile, width), F32)],
         compiler_params=pltpu.CompilerParams(vmem_limit_bytes=40 * 1024 * 1024),
         cost_estimate=cost(5),
@@ -831,25 +831,23 @@
     output, low_t, active, slope, unit_one, inv_one, d_two, d_two_low, d_two_low_t, sums_two = up(
         ctx_t, stacked, cot, heads_all, rest, hidden_bias, vector_rows, part
     )
-    output_got = shifted(output, "y", 1)
-    d_hidden, d_one, d_one_low_t, dctx_t, sums_one, sums_hidden = down(
-        d_two_low, d_two, slope, unit_one, inv_one, heads_all, rest, vector_rows, part
-    )
-    in_grads = outer_in(low_t, d_hidden, d_one_low_t, ctx_t, rows)
+    content_got, query_got = shifted(output[:seq], "y", 1), shifted(output[seq:], "y", 1)
+    below = down(d_two_low, d_two, slope, unit_one, inv_one, heads_all, rest, vector_rows, part)
+    content_got, below = tie(content_got, below)
+    d_hidden, d_one, d_one_low_t, dctx_t, sums_one, sums_hidden = below
+    down_pair = outer(core, d_two_low_t, active, rows, after=(d_one_low_t,))
+    down_pending = start_core(*down_pair)
+    in_grads = outer_in(low_t, d_hidden, d_one_low_t, ctx_t, rows, after=down_pair)
     in_sum = lax.psum_scatter(in_grads, ("z", "x", "core"), scatter_dimension=0)
-    output_got, in_grads = tie(output_got, in_grads)
-    down_pair = outer(core, d_two_low_t, active, rows, after=(in_grads,))
-    down_pending = start_core(*down_pair)
     sums_small = jnp.concatenate(
         [jnp.sum(sums_hidden, axis=(0, 1, 3)).reshape(-1)]
         + [s[i] for i in range(3) for s in (jnp.sum(sums_one, axis=(0, 2)), jnp.sum(sums_two, axis=(0, 2)))]
     )
-    half_back = functools.partial(attention_back, q_t, k_t, v_t, probs, inverse, ctx_t, dctx_t)
-    grads = half_back((), heads, 0, 1, after=down_pair)
-    (down_sum,), grads = tie_sums([down_pending], grads)
+    (down_sum,), query_got, in_grads = tie_sums([down_pending], query_got, in_grads)
     down_pending = start(down_sum, "y", 0)
-    grads = half_back(tuple(grads), heads, 1, heads // 2 - 1, after=down_pending[2])
-    dq_t, dk_t, dv_t, held = grads
+    dq_t, dk_t, dv_t, held = attention_back(
+        q_t, k_t, v_t, probs, inverse, ctx_t, dctx_t, (), heads, 0, heads // 2, after=down_pending[2]
+    )
     pair = project_back(core, stacked, dq_t, dk_t, dv_t, halves, rows)
     (down_sum,), pair = tie_sums([down_pending], pair)
     down_pending = start(down_sum, "x", 1)
@@ -866,7 +864,7 @@
         [jnp.sum(g.astype(F32), axis=1) for g in (dq_t, dv_t)] + [table_grad.reshape(-1), sums_small]
     )
     small = sum_pairs(small.reshape(-1, 128), ("core",))
-    outs = (output, output_got)
+    outs = (output[:seq], content_got, output[seq:], query_got)
     (qkv_sum,), grad_in, small, outs = tie_sums([pending], grad_in, small, outs)
     pending = start(qkv_sum, "x", 1)
     grad_kept, grad_sent = grad_in
@@ -880,10 +878,10 @@
     in_share = total(in_pending[0] + in_pending[1])
     small = sum_pairs(small, ("x", "y")).reshape(-1)
     first_kept = me == 0
-    output, output_got = outs
-    outs = jnp.stack(
-        [jnp.where(first_kept, output, output_got), jnp.where(first_kept, output_got, output)]
-    ).reshape(halves, 2, seq, width)
+    outs = [
+        jnp.stack([jnp.where(first_kept, a, b), jnp.where(first_kept, b, a)])
+        for a, b in (outs[:2], outs[2:])
+    ]
     grad_ins = jnp.stack(
         [jnp.where(first_kept, grad_kept, grad_got), jnp.where(first_kept, grad_got, grad_kept)]
     ).reshape(halves, 2, seq, width // halves)
@@ -895,8 +893,8 @@
     grad_b_in = mine(small[ends[1] : ends[2]].reshape(halves, ffn))
     pairs = small[ends[2] :].reshape(3, 2, width)
     return (
-        outs[:, 0],
-        outs[:, 1],
+        outs[0],
+        outs[1],
         grad_ins[:, 0],
         grad_ins[:, 1],
         jnp.transpose(qkv_share.reshape(rows, 3, part), (1, 0, 2)),

time: 306 us -> 318 us (1.039)
  waiting for transfers between devices: 44.3 us -> 55.4 us
  other arithmetic: 31.4 us -> 36 us
  local copies, waits for them, and re-layouts: 23.9 us -> 27.7 us
  starting transfers between devices: 41.3 us -> 38 us
    ppermute x25 -> x26, waiting for transfers between devices: 35.9 us -> 46.7 us  [shifted(): lax.ppermute(value, axis, [(i, (i + step) % size) for i in range(size)])]
    another operation x0 -> x4, other arithmetic: none -> 3.9 us  [shards(): jnp.stack([jnp.where(first_kept, a, b), jnp.where(first_kept, b, a)])]
    pallas_call x12 -> x11, Pallas kernels: 148 us -> 145 us  [call(): pl.pallas_call(body, in_specs=in_specs + anywhere, **settings)]
    ppermute x25 -> x26, starting transfers between devices: 32.1 us -> 29.8 us  [shifted(): lax.ppermute(value, axis, [(i, (i + step) % size) for i in range(size)])]
    unnamed x70 -> x80, local copies, waits for them, and re-layouts: 9.33 us -> 11.6 us
  transfers between devices with their start and end apart: 32 -> 33, of which waited for: 13 -> 12; matrix products, arithmetic and copies ran while one was open for 15% -> 16% of each run, Pallas kernels for 40% -> 35%
where the time goes in v2:
time: 318 us; the launch traced here: 317 us
  Pallas kernels  145 us (46%)
  waiting for transfers between devices  55.4 us (17%)
  starting transfers between devices  38 us (12%)
  other arithmetic  36 us (11%)
  local copies, waits for them, and re-layouts  27.7 us (9%)
  between operations  14.8 us (5%)
    pallas_call x11, Pallas kernels, call(): pl.pallas_call(body, in_specs=in_specs + anywhere, **settings)  145 us
    ppermute x26, waiting for transfers between devices, shifted(): lax.ppermute(value, axis, [(i, (i + step) % size) for i in range(size)])  46.7 us
    ppermute x26, starting transfers between devices, shifted(): lax.ppermute(value, axis, [(i, (i + step) % size) for i in range(size)])  29.8 us
    unnamed x80, local copies, waits for them, and re-layouts  11.6 us
    convert_element_type x6, other arithmetic, start(): out = [total(at(lax.rem(me + k, size))).astype(BF) for k in range(1, size)]  10.1 us
    ppermute x5, starting transfers between devices, sum_pairs(): lax.ppermute(value, axis, [(i, i ^ step) for i in range(size)])  8.14 us
  transfers between devices with their start and end apart: 33, of which 12 were waited for; matrix products, arithmetic and copies ran while one was open for 16% of the time, Pallas kernels for 35%

profile of v2, /device:TPU:0, one launch (start us, length us, event | category | flops | bytes accessed | tf_op | source)
XLA Modules:
  0.0 316.5 jit_solution(5497853310893762459)
XLA Ops:
  7.2 1.9 pad_maximum_fusion.10
  10.0 1.4 pad_maximum_fusion.11
  11.4 5.0 %collective-permute-start = (bf16[48,1536]{1,0:T(8,128)(2,1)}, bf16[48,1536]{1,0:T(8,128)(2,1)S(1)}, u32[]{:S(2)}, u32[]{:S(2)}) collective-permute-start(bf16[48,1536]{1,0:T(8,128)(2,1)} %pad_maximum_fusion.11), channel_id=1, source_target_pairs={{0,24},{8,0},{16,8},{24,16},{1,25},{9,1},{17,9},{25,17},{2,26},{10... | collective-permute-start | bytes 442376 | tf_op jit(solution)/shard_map/ppermute | solution.py:685
  20.3 1.5 collective-permute-start.5
  26.0 7.8 %collective-permute-done.1 = bf16[48,1536]{1,0:T(8,128)(2,1)S(1)} collective-permute-done((bf16[48,1536]{1,0:T(8,128)(2,1)}, bf16[48,1536]{1,0:T(8,128)(2,1)S(1)}, u32[]{:S(2)}, u32[]{:S(2)}) %collective-permute-start.1) | collective-permute-done | bytes 147488 | tf_op jit(solution)/shard_map/ppermute | solution.py:685
  36.0 1.6 collective-permute-start.3
  37.6 1.7 collective-permute-start.4
  42.1 8.6 %shard_map.272.refs_3_ = bf16[12,512,1024]{2,1,0:T(8,128)(2,1)} custom-call(s32[1]{0:T(128)} %dynamic_slice.183.refs_0_, s32[512,512]{1,0:T(8,128)} %bitcast.190, s32[1,512]{1,0:T(1,128)} %constant_dynamic-slice_fusion.3.refs_2_, s32[512,1]{1,0:T(8,128)} %copy.45.refs_3_, f32[12,128]{1,0:T(8,128)} %pad.15.refs_4_), custom_call_target="tpu_custom_call" | custom-call | flops 90000000 | bytes 90000 | tf_op jit(solution)/shard_map/pallas_call | solution.py:272
  52.0 13.7 %collective-permute-done.7 = bf16[2,4,48,768]{3,2,1,0:T(8,128)(2,1)S(1)} collective-permute-done((bf16[2,4,48,768]{3,2,1,0:T(8,128)(2,1)S(1)}, bf16[2,4,48,768]{3,2,1,0:T(8,128)(2,1)S(1)}, u32[]{:S(2)}, u32[]{:S(2)}) %collective-permute-start.7) | collective-permute-done | bytes 589856 | tf_op jit(solution)/shard_map/ppermute | solution.py:685
  68.4 1.5 dynamic-slice_bitcast_fusion.2
  77.0 7.9 %shard_map.273 = (bf16[768,1024]{1,0:T(8,128)(2,1)}, bf16[768,512]{1,0:T(8,128)(2,1)}, bf16[768,512]{1,0:T(8,128)(2,1)}, bf16[2,8,2,48,1536]{4,3,2,1,0:T(8,128)(2,1)}) custom-call(s32[1]{0:T(128)} %bitcast.refs_0_, bf16[2,8,48,768]{3,2,1,0:T(8,128)(2,1)} %copy-done.9, bf16[2,8,48,768]{3,2,1,0:T(8,128)(2,1)} %bitcast.193, ...), custom_call_target="tpu_custom_call" | custom-call | flops 60000000 | bytes 60000 | tf_op jit(solution)/shard_map/pallas_call | solution.py:272
  84.9 16.4 %shard_map.274 = (bf16[12,512,1024]{2,1,0:T(8,128)(2,1)}, bf16[768,1024]{1,0:T(8,128)(2,1)}, f32[12,1,1024]{2,1,0:T(1,128)}) custom-call(bf16[768,1024]{1,0:T(8,128)(2,1)} %get-tuple-element.81.refs_0_, bf16[768,512]{1,0:T(8,128)(2,1)} %get-tuple-element.82.refs_1_, bf16[768,512]{1,0:T(8,128)(2,1)} %get-tuple-element.83.refs_2_, ...), custom_call_target="tpu_custom_call" | custom-call | flops 180000000 | bytes 180000 | tf_op jit(solution)/shard_map/pallas_call | solution.py:272
  101.3 3.5 %all-gather.3.cloned.1.call-done = bf16[1536,3072]{1,0:T(8,128)(2,1)} async-done(((bf16[48,3072]{1,0:T(8,128)(2,1)}), bf16[1536,3072]{1,0:T(8,128)(2,1)}) %all-gather.3.cloned.1.call-update) | async-done | bytes 9437200 | tf_op jit(solution)/shard_map/all_gather | solution.py:790
  104.8 25.4 %shard_map.275 = (bf16[1024,768]{1,0:T(8,128)(2,1)}, bf16[768,1024]{1,0:T(8,128)(2,1)}, bf16[2,1024,1536]{2,1,0:T(8,128)(2,1)}, bf16[2,1024,1536]{2,1,0:T(8,128)...) custom-call(bf16[768,1024]{1,0:T(8,128)(2,1)} %get-tuple-element.85., ...), custom_call_target="tpu_custom_call" | custom-call | flops 200000000 | bytes 200000 | tf_op jit(solution)/shard_map/pallas_call | solution.py:272
  130.2 1.5 fusion.31
  131.7 1.7 collective-permute-start.10
  133.4 22.5 %shard_map.276 = (bf16[2,1024,1536]{2,1,0:T(8,128)(2,1)}, f32[1024,768]{1,0:T(8,128)}, bf16[768,1024]{1,0:T(8,128)(2,1)}, bf16[768,1024]{1,0:T(8,128)(2,1)}, f32...) custom-call(bf16[1024,768]{1,0:T(8,128)(2,1)} %get-tuple-element.90.refs_0_, f32[1024,768]{1,0:T(8,128)} %get-tuple-element.91.refs_1_, ...), custom_call_target="tpu_custom_call" | custom-call | flops 180000000 | bytes 180000 | tf_op jit(solution)/shard_map/pallas_call | solution.py:272
  156.8 9.4 %shard_map.277 = (bf16[2,8,48,1536]{3,2,1,0:T(8,128)(2,1)}, bf16[2,8,48,1536]{3,2,1,0:T(8,128)(2,1)}) custom-call(s32[1]{0:T(128)} %bitcast.refs_0_, bf16[768,1024]{1,0:T(8,128)(2,1)} %get-tuple-element.87.refs_1_, bf16[2,1024,1536]{2,1,0:T(8,128)(2,1)} %get-tuple-element.88.refs_2_, bf16[768,1024]{1,0:T(8,128)(2,1)} %get-tuple-element.101.refs_3_.refs_2_), custom_call_target="tpu_custom_call" | custom-call | flops 50000000 | bytes 50000 | tf_op jit(solution)/shard_map/pallas_call | solution.py:272
  166.7 1.7 copy-done.2
  168.4 1.7 copy-done.6
  170.0 11.5 %shard_map.278 = bf16[16,2,48,1920]{3,2,1,0:T(8,128)(2,1)} custom-call(bf16[768,1024]{1,0:T(8,128)(2,1)} %get-tuple-element.104.refs_0_, bf16[2,1024,1536]{2,1,0:T(8,128)(2,1)} %get-tuple-element.105.refs_1_, bf16[768,1024]{1,0:T(8,128)(2,1)} %get-tuple-element.101.refs_3_.refs_2_, bf16[768,1024]{1,0:T(8,128)(2,1)} %get-tuple-element.85.refs_0_.refs_3_.refs_5_, ...), custom_call_target="tpu_custom_call" | custom-call | flops 60000000 | bytes 60000 | tf_op jit(solution)/shard_map/pallas_call | solution.py:272
  181.6 4.7 %collective-permute-done.12 = bf16[512,768]{1,0:T(8,128)(2,1)} collective-permute-done((bf16[512,768]{1,0:T(8,128)(2,1)S(1)}, bf16[512,768]{1,0:T(8,128)(2,1)}, u32[]{:S(2)}, u32[]{:S(2)}) %collective-permute-start.12) | collective-permute-done | bytes 786464 | tf_op jit(solution)/shard_map/ppermute | solution.py:685
  186.3 2.6 fusion.refs_7_
  189.5 18.4 %shard_map.279 = (bf16[768,1024]{1,0:T(8,128)(2,1)}, bf16[768,512]{1,0:T(8,128)(2,1)}, bf16[768,512]{1,0:T(8,128)(2,1)}, bf16[32,192,512]{2,1,0:T(8,128)(2,1)}) custom-call(bf16[768,1024]{1,0:T(8,128)(2,1)} %get-tuple-element.81.refs_0_, bf16[768,512]{1,0:T(8,128)(2,1)} %get-tuple-element.82.refs_1_, bf16[768,512]{1,0:T(8,128)(2,1)} %get-tuple-element.83.refs_2_, ...), custom_call_target="tpu_custom_call" | custom-call | flops 599999971328 | bytes 600000000 | tf_op jit(solution)/shard_map/pallas_call | solution.py:272
  208.0 7.9 %shard_map.280 = (bf16[2,8,48,1152]{3,2,1,0:T(8,128)(2,1)}, bf16[2,8,48,1152]{3,2,1,0:T(8,128)(2,1)}) custom-call(s32[1]{0:T(128)} %bitcast.refs_0_, bf16[1024,768]{1,0:T(8,128)(2,1)} %pad_maximum_fusion.refs_5_.refs_1_, bf16[768,1024]{1,0:T(8,128)(2,1)} %get-tuple-element.110.refs_2_.refs_3_, bf16[768,512]{1,0:T(8,128)(2,1)} %get-tuple-element.111.refs_3_.refs_4_, ...), custom_call_target="tpu_custom_call" | custom-call | flops 50000000 | bytes 50000 | tf_op jit(solution)/shard_map/pallas_call | solution.py:272
  216.9 1.5 fusion.1.refs_4_
  219.2 1.8 convert_reduce_fusion
  222.4 1.5 copy-done.7
  223.9 7.8 %shard_map.281 = f32[32,192]{1,0:T(8,128)S(1)} custom-call(s32[512,512]{1,0:T(8,128)} %bitcast.191, bf16[32,192,512]{2,1,0:T(8,128)(2,1)} %get-tuple-element.118.refs_1_, bf16[2,8,48,1152]{3,2,1,0:T(8,128)(2,1)S(1)} %copy-done.5, bf16[2,8,48,1152]{3,2,1,0:T(8,128)(2,1)S(1)} %copy-done.7, bf16[4,48,1536]{2,1,0:T(8,128)(2,1)S(1)} %fusion.1.refs_4_), custom_call_target="tpu_custom_call" | custom-call | flops 60000000 | bytes 60000 | tf_op jit(solution)/shard_map/pallas_call | solution.py:272
  231.6 9.5 %collective-permute-done.15 = bf16[4,48,1536]{2,1,0:T(8,128)(2,1)} collective-permute-done((bf16[4,48,1536]{2,1,0:T(8,128)(2,1)S(1)}, bf16[4,48,1536]{2,1,0:T(8,128)(2,1)}, u32[]{:S(2)}, u32[]{:S(2)}) %collective-permute-start.15) | collective-permute-done | bytes 589856 | tf_op jit(solution)/shard_map/ppermute | solution.py:685
  241.6 1.6 fusion.2.refs_6_
  243.2 1.5 collective-permute-start.16
  244.7 1.6 fusion.11
  246.4 1.6 collective-permute-start.28
  247.9 2.4 collective-permute-start.29
  250.4 1.4 collective-permute-start.30
  251.8 9.0 %shard_map.282 = (bf16[1024,384]{1,0:T(8,128)(2,1)}, bf16[1024,384]{1,0:T(8,128)(2,1)}) custom-call(s32[1]{0:T(128)} %bitcast.40.refs_0_, bf16[2,768,1536]{2,1,0:T(8,128)(2,1)} %bitcast.189, f32[1024,768]{1,0:T(8,128)} %get-tuple-element.120.refs_2_, bf16[768,1024]{1,0:T(8,128)(2,1)} %get-tuple-element.110.refs_2_.refs_3_, ...), custom_call_target="tpu_custom_call" | custom-call | flops 50000000 | bytes 50000 | tf_op jit(solution)/shard_map/pallas_call | solution.py:272
  260.8 2.0 fusion.10
  262.8 2.5 collective-permute-done.16
  265.3 6.5 %collective-permute-start.20 = (f32[75,128]{1,0:T(8,128)S(1)}, f32[75,128]{1,0:T(8,128)S(1)}, u32[]{:S(2)}, u32[]{:S(2)}) collective-permute-start(f32[75,128]{1,0:T(8,128)S(1)} %bitcast_add_fusion), channel_id=1, source_target_pairs={{0,8},{8,0},{16,24},{24,16},{1,9},{9,1},{17,25},{25,17},{2,10},{10... | collective-permute-start | bytes 115208 | tf_op jit(solution)/shard_map/ppermute | solution.py:751
  273.2 1.6 collective-permute-start.18
  278.7 2.7 collective-permute-done.21
  281.4 3.3 %collective-permute-done.19 = bf16[4,48,1152]{2,1,0:T(8,128)(2,1)S(1)} collective-permute-done((bf16[4,48,1152]{2,1,0:T(8,128)(2,1)S(1)}, bf16[4,48,1152]{2,1,0:T(8,128)(2,1)S(1)}, u32[]{:S(2)}, u32[]{:S(2)}) %collective-permute-start.19) | collective-permute-done | bytes 442400 | tf_op jit(solution)/shard_map/ppermute | solution.py:685
  286.3 2.4 collective-permute-done.25
  290.9 3.2 collective-permute-start.24
  297.8 1.9 collective-permute-done.23
  302.7 1.9 collective-permute-start.27
  306.0 2.2 collective-permute-done.27
  (199 shorter events, 49.0 us)
Async XLA Ops:
  7.2 14.6 %copy-start = (s32[2,512,512]{2,1,0:T(8,128)S(1)}, s32[2,512,512]{2,1,0:T(8,128)}, u32[]{:S(2)}) copy-start(s32[2,512,512]{2,1,0:T(8,128)} %param.21) | copy-start | bytes 6291460
  7.2 97.6 %all-gather.3.cloned.1.call-start = ((), (), s32[]{:S(2)}) async-start(), calls=%async_computation.2 | async-start | bytes 9732096 | tf_op jit(solution)/shard_map/all_gather | solution.py:790
  9.1 292.6 %reduce-scatter.2.cloned.1.call-start = ((), (), s32[]{:S(2)}) async-start(), calls=%async_computation.1 | async-start | bytes 6266880 | tf_op jit(solution)/shard_map/reduce_scatter | solution.py:841
  11.4 14.6 %collective-permute-start = (bf16[48,1536]{1,0:T(8,128)(2,1)}, bf16[48,1536]{1,0:T(8,128)(2,1)S(1)}, u32[]{:S(2)}, u32[]{:S(2)}) collective-permute-start(bf16[48,1536]{1,0:T(8,128)(2,1)} %pad_maximum_fusion.11), channel_id=1, source_target_pairs={{0,24},{8,0},{16,8},{24,16},{1,25},{9,1},{17,9},{25,17},{2,26},{10... | collective-permute-start | bytes 442376 | tf_op jit(solution)/shard_map/ppermute | solution.py:685
  16.5 17.3 %collective-permute-start.1 = (bf16[48,1536]{1,0:T(8,128)(2,1)}, bf16[48,1536]{1,0:T(8,128)(2,1)S(1)}, u32[]{:S(2)}, u32[]{:S(2)}) collective-permute-start(bf16[48,1536]{1,0:T(8,128)(2,1)} %pad_maximum_fusion.11), channel_id=1, source_target_pairs={{0,16},{8,24},{16,0},{24,8},{1,17},{9,25},{17,1},{25,9},{2,18},{10... | collective-permute-start | bytes 442376 | tf_op jit(solution)/shard_map/ppermute | solution.py:685
  16.5 17.3 %collective-permute-start.2 = (bf16[48,1536]{1,0:T(8,128)(2,1)}, bf16[48,1536]{1,0:T(8,128)(2,1)}, u32[]{:S(2)}, u32[]{:S(2)}) collective-permute-start(bf16[48,1536]{1,0:T(8,128)(2,1)} %pad_maximum_fusion.11), channel_id=1, source_target_pairs={{0,8},{8,16},{16,24},{24,0},{1,9},{9,17},{17,25},{25,1},{2,10},{10... | collective-permute-start | bytes 442376 | tf_op jit(solution)/shard_map/ppermute | solution.py:685
  20.3 19.0 %collective-permute-start.5 = (bf16[38,384]{1,0:T(8,128)(2,1)}, bf16[38,384]{1,0:T(8,128)(2,1)}, u32[]{:S(2)}, u32[]{:S(2)}) collective-permute-start(bf16[38,384]{1,0:T(8,128)(2,1)} %fusion.21), channel_id=1, source_target_pairs={{0,1},{1,0},{2,3},{3,2},{4,5},{5,4},{6,7},{7,6},{8,9},{9,8},{10,11... | collective-permute-start | bytes 87560 | tf_op jit(solution)/shard_map/ppermute | solution.py:685
  21.9 11.9 %copy-start.23 = (bf16[384,48]{0,1:T(8,128)(2,1)S(1)}, bf16[384,48]{0,1:T(8,128)(2,1)}, u32[]{:S(2)}) copy-start(bf16[384,48]{0,1:T(8,128)(2,1)} %param.24) | copy-start | bytes 110596
  34.9 4.4 %copy-start.27 = (bf16[32,6]{1,0:T(8,128)(2,1)S(1)}, bf16[32,6]{1,0:T(8,128)(2,1)}, u32[]{:S(2)}) copy-start(bf16[32,6]{1,0:T(8,128)(2,1)} %copy-done.26) | copy-start | bytes 1156
  34.9 4.4 %copy-start.28 = (bf16[2,384]{1,0:T(2,128)(2,1)S(1)}, bf16[2,384]{1,0:T(2,128)(2,1)}, u32[]{:S(2)}) copy-start(bf16[2,384]{1,0:T(2,128)(2,1)} %param.23) | copy-start | bytes 4612
  36.0 14.7 %collective-permute-start.3 = (bf16[4,48,768]{2,1,0:T(8,128)(2,1)S(1)}, bf16[4,48,768]{2,1,0:T(8,128)(2,1)S(1)}, u32[]{:S(2)}, u32[]{:S(2)}) collective-permute-start(bf16[4,48,768]{2,1,0:T(8,128)(2,1)S(1)} %get-tuple-element.78), channel_id=1, source_target_pairs={{0,4},{4,0},{1,5},{5,1},{2,6},{6,2},{3,7},{7,3},{8,12},{12,8},{9,1... | collective-permute-start | bytes 884744 | tf_op jit(solution)/shard_map/ppermute | solution.py:685
  37.6 13.1 %collective-permute-start.4 = (bf16[4,48,768]{2,1,0:T(8,128)(2,1)S(1)}, bf16[4,48,768]{2,1,0:T(8,128)(2,1)S(1)}, u32[]{:S(2)}, u32[]{:S(2)}) collective-permute-start(bf16[4,48,768]{2,1,0:T(8,128)(2,1)S(1)} %get-tuple-element.80), channel_id=1, source_target_pairs={{0,1},{1,0},{2,3},{3,2},{4,5},{5,4},{6,7},{7,6},{8,9},{9,8},{10,11... | collective-permute-start | bytes 884744 | tf_op jit(solution)/shard_map/ppermute | solution.py:685
  50.9 14.8 %collective-permute-start.7 = (bf16[2,4,48,768]{3,2,1,0:T(8,128)(2,1)S(1)}, bf16[2,4,48,768]{3,2,1,0:T(8,128)(2,1)S(1)}, u32[]{:S(2)}, u32[]{:S(2)}) collective-permute-start(bf16[2,4,48,768]{3,2,1,0:T(8,128)(2,1)S(1)} %pad_maximum_fusion.9), channel_id=1, source_target_pairs={{0,4},{4,0},{1,5},{5,1},{2,6},{6,2},{3,7},{7,3},{8,12},{12,8},{9,1... | collective-permute-start | bytes 1769480 | tf_op jit(solution)/shard_map/ppermute | solution.py:685
  51.4 14.7 %collective-permute-start.6 = (bf16[4,2,48,768]{3,2,0,1:T(8,128)(2,1)S(1)}, bf16[4,2,48,768]{3,2,0,1:T(8,128)(2,1)S(1)}, u32[]{:S(2)}, u32[]{:S(2)}) collective-permute-start(bf16[4,2,48,768]{3,2,0,1:T(8,128)(2,1)S(1)} %pad_maximum_fusion.8), channel_id=1, source_target_pairs={{0,1},{1,0},{2,3},{3,2},{4,5},{5,4},{6,7},{7,6},{8,9},{9,8},{10,11... | collective-permute-start | bytes 1769480 | tf_op jit(solution)/shard_map/ppermute | solution.py:685
  66.0 10.0 %collective-permute-start.9 = (bf16[2,8,48,768]{3,2,1,0:T(8,128)(2,1)S(1)}, bf16[2,8,48,768]{3,2,1,0:T(8,128)(2,1)S(1)}, u32[]{:S(2)}, u32[]{:S(2)}) collective-permute-start(bf16[2,8,48,768]{3,2,1,0:T(8,128)(2,1)S(1)} %bitcast.192), channel_id=1, source_target_pairs={{0,2},{2,0},{1,3},{3,1},{4,6},{6,4},{5,7},{7,5},{8,10},{10,8},{9,1... | collective-permute-start | bytes 3538952 | tf_op jit(solution)/shard_map/ppermute | solution.py:685
  67.3 8.8 %collective-permute-start.8 = (bf16[2,8,48,768]{3,2,1,0:T(8,128)(2,1)S(1)}, bf16[2,8,48,768]{3,2,1,0:T(8,128)(2,1)}, u32[]{:S(2)}, u32[]{:S(2)}) collective-permute-start(bf16[2,8,48,768]{3,2,1,0:T(8,128)(2,1)S(1)} %pad_maximum_fusion.4.refs_1_), channel_id=1, source_target_pairs={{0,2},{2,0},{1,3},{3,1},{4,6},{6,4},{5,7},{7,5},{8,10},{10,8},{9,1... | collective-permute-start | bytes 3538952 | tf_op jit(solution)/shard_map/ppermute | solution.py:685
  131.7 24.2 %copy-start.10 = (bf16[512,768]{1,0:T(8,128)(2,1)}, bf16[512,768]{1,0:T(8,128)(2,1)S(1)}, u32[]{:S(2)}) copy-start(bf16[512,768]{1,0:T(8,128)(2,1)S(1)} %get-tuple-element.130) | copy-start | bytes 2359300
  131.7 34.5 %copy-start.12 = (bf16[512,768]{1,0:T(8,128)(2,1)}, bf16[512,768]{1,0:T(8,128)(2,1)S(1)}, u32[]{:S(2)}) copy-start(bf16[512,768]{1,0:T(8,128)(2,1)S(1)} %get-tuple-element.132) | copy-start | bytes 2359300
  131.7 24.2 %collective-permute-start.10 = (bf16[512,768]{1,0:T(8,128)(2,1)S(1)}, bf16[512,768]{1,0:T(8,128)(2,1)S(1)}, u32[]{:S(2)}, u32[]{:S(2)}) collective-permute-start(bf16[512,768]{1,0:T(8,128)(2,1)S(1)} %get-tuple-element.130), channel_id=1, source_target_pairs={{0,1},{1,0},{2,3},{3,2},{4,5},{5,4},{6,7},{7,6},{8,9},{9,8},{10,11... | collective-permute-start | bytes 2359304 | tf_op jit(solution)/shard_map/ppermute | solution.py:685
  166.2 20.1 %collective-permute-start.11 = (bf16[2,8,48,1536]{3,2,1,0:T(8,128)(2,1)}, bf16[2,8,48,1536]{3,2,1,0:T(8,128)(2,1)}, u32[]{:S(2)}, u32[]{:S(2)}) collective-permute-start(bf16[2,8,48,1536]{3,2,1,0:T(8,128)(2,1)} %get-tuple-element.103.refs_5_), channel_id=1, source_target_pairs={{0,2},{2,0},{1,3},{3,1},{4,6},{6,4},{5,7},{7,5},{8,10},{10,8},{9,1... | collective-permute-start | bytes 7077896 | tf_op jit(solution)/shard_map/ppermute | solution.py:685
  166.2 20.1 %collective-permute-start.12 = (bf16[512,768]{1,0:T(8,128)(2,1)S(1)}, bf16[512,768]{1,0:T(8,128)(2,1)}, u32[]{:S(2)}, u32[]{:S(2)}) collective-permute-start(bf16[512,768]{1,0:T(8,128)(2,1)S(1)} %get-tuple-element.132), channel_id=1, source_target_pairs={{0,1},{1,0},{2,3},{3,2},{4,5},{5,4},{6,7},{7,6},{8,9},{9,8},{10,11... | collective-permute-start | bytes 2359304 | tf_op jit(solution)/shard_map/ppermute | solution.py:685
  181.5 4.8 %copy-start.3 = (bf16[2,8,48,1536]{3,2,1,0:T(8,128)(2,1)S(1)}, bf16[2,8,48,1536]{3,2,1,0:T(8,128)(2,1)}, u32[]{:S(2)}) copy-start(bf16[2,8,48,1536]{3,2,1,0:T(8,128)(2,1)} %get-tuple-element.102.refs_4_) | copy-start | bytes 7077892
  188.9 27.8 %collective-permute-start.13 = (bf16[4,2,48,1536]{3,2,1,0:T(8,128)(2,1)}, bf16[4,2,48,1536]{3,2,1,0:T(8,128)(2,1)}, u32[]{:S(2)}, u32[]{:S(2)}) collective-permute-start(bf16[4,2,48,1536]{3,2,1,0:T(8,128)(2,1)} %fusion.refs_7_), channel_id=1, source_target_pairs={{0,1},{1,0},{2,3},{3,2},{4,5},{5,4},{6,7},{7,6},{8,9},{9,8},{10,11... | collective-permute-start | bytes 3538952 | tf_op jit(solution)/shard_map/ppermute | solution.py:685
  207.9 8.8 %copy-start.24 = (f32[4,3,8,768]{3,2,1,0:T(8,128)S(1)}, f32[4,3,8,768]{3,2,1,0:T(8,128)}, u32[]{:S(2)}) copy-start(f32[4,3,8,768]{3,2,1,0:T(8,128)} %get-tuple-element.127) | copy-start | bytes 884740
  207.9 8.9 %copy-start.25 = (f32[4,3,8,768]{3,2,1,0:T(8,128)S(1)}, f32[4,3,8,768]{3,2,1,0:T(8,128)}, u32[]{:S(2)}) copy-start(f32[4,3,8,768]{3,2,1,0:T(8,128)} %get-tuple-element.126) | copy-start | bytes 884740
  207.9 8.9 %copy-start.4 = (bf16[2,8,48,1536]{3,2,1,0:T(8,128)(2,1)S(1)}, bf16[2,8,48,1536]{3,2,1,0:T(8,128)(2,1)}, u32[]{:S(2)}) copy-start(bf16[2,8,48,1536]{3,2,1,0:T(8,128)(2,1)} %get-tuple-element.102.refs_4_) | copy-start | bytes 7077892
  216.7 24.4 %collective-permute-start.14 = (bf16[2,8,48,1152]{3,2,1,0:T(8,128)(2,1)}, bf16[2,8,48,1152]{3,2,1,0:T(8,128)(2,1)}, u32[]{:S(2)}, u32[]{:S(2)}) collective-permute-start(bf16[2,8,48,1152]{3,2,1,0:T(8,128)(2,1)} %get-tuple-element.116.refs_3_), channel_id=1, source_target_pairs={{0,2},{2,0},{1,3},{3,1},{4,6},{6,4},{5,7},{7,5},{8,10},{10,8},{9,1... | collective-permute-start | bytes 5308424 | tf_op jit(solution)/shard_map/ppermute | solution.py:685
  218.4 22.8 %collective-permute-start.15 = (bf16[4,48,1536]{2,1,0:T(8,128)(2,1)S(1)}, bf16[4,48,1536]{2,1,0:T(8,128)(2,1)}, u32[]{:S(2)}, u32[]{:S(2)}) collective-permute-start(bf16[4,48,1536]{2,1,0:T(8,128)(2,1)S(1)} %fusion.1.refs_4_), channel_id=1, source_target_pairs={{0,4},{4,0},{1,5},{5,1},{2,6},{6,2},{3,7},{7,3},{8,12},{12,8},{9,1... | collective-permute-start | bytes 1769480 | tf_op jit(solution)/shard_map/ppermute | solution.py:685
  241.5 19.3 %collective-permute-start.17 = (f32[75,128]{1,0:T(8,128)S(1)}, f32[75,128]{1,0:T(8,128)S(1)}, u32[]{:S(2)}, u32[]{:S(2)}) collective-permute-start(f32[75,128]{1,0:T(8,128)S(1)} %bitcast.204), channel_id=1, source_target_pairs={{0,2},{2,0},{1,3},{3,1},{4,6},{6,4},{5,7},{7,5},{8,10},{10,8},{9,1... | collective-permute-start | bytes 115208 | tf_op jit(solution)/shard_map/ppermute | solution.py:751
  243.2 22.1 %collective-permute-start.16 = (bf16[4,2,48,1152]{3,2,1,0:T(8,128)(2,1)S(1)}, bf16[4,2,48,1152]{3,2,1,0:T(8,128)(2,1)S(1)}, u32[]{:S(2)}, u32[]{:S(2)}) collective-permute-start(bf16[4,2,48,1152]{3,2,1,0:T(8,128)(2,1)S(1)} %fusion.2.refs_6_), channel_id=1, source_target_pairs={{0,1},{1,0},{2,3},{3,2},{4,5},{5,4},{6,7},{7,6},{8,9},{9,8},{10,11... | collective-permute-start | bytes 2654216 | tf_op jit(solution)/shard_map/ppermute | solution.py:685
  246.4 14.4 %collective-permute-start.28 = (bf16[48,1536]{1,0:T(8,128)(2,1)S(1)}, bf16[48,1536]{1,0:T(8,128)(2,1)S(1)}, u32[]{:S(2)}, u32[]{:S(2)}) collective-permute-start(bf16[48,1536]{1,0:T(8,128)(2,1)S(1)} %get-tuple-element.162.refs_7_), channel_id=1, source_target_pairs={{0,8},{8,16},{16,24},{24,0},{1,9},{9,17},{17,25},{25,1},{2,10},{10... | collective-permute-start | bytes 442376 | tf_op jit(solution)/shard_map/ppermute | solution.py:685
  247.9 12.9 %collective-permute-start.29 = (bf16[48,1536]{1,0:T(8,128)(2,1)S(1)}, bf16[48,1536]{1,0:T(8,128)(2,1)S(1)}, u32[]{:S(2)}, u32[]{:S(2)}) collective-permute-start(bf16[48,1536]{1,0:T(8,128)(2,1)S(1)} %get-tuple-element.161.refs_8_), channel_id=1, source_target_pairs={{0,16},{8,24},{16,0},{24,8},{1,17},{9,25},{17,1},{25,9},{2,18},{10... | collective-permute-start | bytes 442376 | tf_op jit(solution)/shard_map/ppermute | solution.py:685
  250.4 10.5 %collective-permute-start.30 = (bf16[48,1536]{1,0:T(8,128)(2,1)S(1)}, bf16[48,1536]{1,0:T(8,128)(2,1)S(1)}, u32[]{:S(2)}, u32[]{:S(2)}) collective-permute-start(bf16[48,1536]{1,0:T(8,128)(2,1)S(1)} %get-tuple-element.160.refs_9_), channel_id=1, source_target_pairs={{0,24},{8,0},{16,8},{24,16},{1,25},{9,1},{17,9},{25,17},{2,26},{10... | collective-permute-start | bytes 442376 | tf_op jit(solution)/shard_map/ppermute | solution.py:685
  260.8 14.0 %copy-start.13 = (bf16[512,768]{1,0:T(8,128)(2,1)S(1)}, bf16[512,768]{1,0:T(8,128)(2,1)}, u32[]{:S(2)}) copy-start(bf16[512,768]{1,0:T(8,128)(2,1)} %copy-done.12) | copy-start | bytes 2359300
  265.3 10.9 %collective-permute-start.20 = (f32[75,128]{1,0:T(8,128)S(1)}, f32[75,128]{1,0:T(8,128)S(1)}, u32[]{:S(2)}, u32[]{:S(2)}) collective-permute-start(f32[75,128]{1,0:T(8,128)S(1)} %bitcast_add_fusion), channel_id=1, source_target_pairs={{0,8},{8,0},{16,24},{24,16},{1,9},{9,1},{17,25},{25,17},{2,10},{10... | collective-permute-start | bytes 115208 | tf_op jit(solution)/shard_map/ppermute | solution.py:751
  273.1 11.5 %collective-permute-start.19 = (bf16[4,48,1152]{2,1,0:T(8,128)(2,1)S(1)}, bf16[4,48,1152]{2,1,0:T(8,128)(2,1)S(1)}, u32[]{:S(2)}, u32[]{:S(2)}) collective-permute-start(bf16[4,48,1152]{2,1,0:T(8,128)(2,1)S(1)} %fusion.3), channel_id=1, source_target_pairs={{0,4},{4,0},{1,5},{5,1},{2,6},{6,2},{3,7},{7,3},{8,12},{12,8},{9,1... | collective-permute-start | bytes 1327112 | tf_op jit(solution)/shard_map/ppermute | solution.py:685
  273.2 31.3 %collective-permute-start.18 = (bf16[1024,384]{1,0:T(8,128)(2,1)}, bf16[1024,384]{1,0:T(8,128)(2,1)S(1)}, u32[]{:S(2)}, u32[]{:S(2)}) collective-permute-start(bf16[1024,384]{1,0:T(8,128)(2,1)} %get-tuple-element.135), channel_id=1, source_target_pairs={{0,1},{1,0},{2,3},{3,2},{4,5},{5,4},{6,7},{7,6},{8,9},{9,8},{10,11... | collective-permute-start | bytes 2359304 | tf_op jit(solution)/shard_map/ppermute | solution.py:685
  276.2 5.2 %collective-permute-start.21 = (f32[75,128]{1,0:T(8,128)S(1)}, f32[75,128]{1,0:T(8,128)S(1)}, u32[]{:S(2)}, u32[]{:S(2)}) collective-permute-start(f32[75,128]{1,0:T(8,128)S(1)} %add.498), channel_id=1, source_target_pairs={{0,16},{8,24},{16,0},{24,8},{1,17},{9,25},{17,1},{25,9},{2,18},{10... | collective-permute-start | bytes 115208 | tf_op jit(solution)/shard_map/ppermute | solution.py:751
  284.7 4.1 %copy-start.18 = (bf16[4,48,1152]{2,1,0:T(8,128)(2,1)}, bf16[4,48,1152]{2,1,0:T(8,128)(2,1)S(1)}, u32[]{:S(2)}) copy-start(bf16[4,48,1152]{2,1,0:T(8,128)(2,1)S(1)} %collective-permute-done.19) | copy-start | bytes 1327108
  284.7 4.0 %collective-permute-start.25 = (f32[75,128]{1,0:T(8,128)S(1)}, f32[75,128]{1,0:T(8,128)S(1)}, u32[]{:S(2)}, u32[]{:S(2)}) collective-permute-start(f32[75,128]{1,0:T(8,128)S(1)} %add.499), channel_id=1, source_target_pairs={{0,4},{4,0},{1,5},{5,1},{2,6},{6,2},{3,7},{7,3},{8,12},{12,8},{9,1... | collective-permute-start | bytes 115208 | tf_op jit(solution)/shard_map/ppermute | solution.py:751
  288.7 5.4 %collective-permute-start.26 = (f32[75,128]{1,0:T(8,128)S(1)}, f32[75,128]{1,0:T(8,128)S(1)}, u32[]{:S(2)}, u32[]{:S(2)}) collective-permute-start(f32[75,128]{1,0:T(8,128)S(1)} %add.516), channel_id=1, source_target_pairs={{0,1},{1,0},{2,3},{3,2},{4,5},{5,4},{6,7},{7,6},{8,9},{9,8},{10,11... | collective-permute-start | bytes 115208 | tf_op jit(solution)/shard_map/ppermute | solution.py:751
  290.2 14.4 %copy-start.17 = (bf16[1024,384]{1,0:T(8,128)(2,1)S(1)}, bf16[1024,384]{1,0:T(8,128)(2,1)}, u32[]{:S(2)}) copy-start(bf16[1024,384]{1,0:T(8,128)(2,1)} %get-tuple-element.134) | copy-start | bytes 2359300
  290.2 7.7 %collective-permute-start.22 = (bf16[48,1152]{1,0:T(8,128)(2,1)S(1)}, bf16[48,1152]{1,0:T(8,128)(2,1)S(1)}, u32[]{:S(2)}, u32[]{:S(2)}) collective-permute-start(bf16[48,1152]{1,0:T(8,128)(2,1)S(1)} %get-tuple-element.163), channel_id=1, source_target_pairs={{0,8},{8,16},{16,24},{24,0},{1,9},{9,17},{17,25},{25,1},{2,10},{10... | collective-permute-start | bytes 331784 | tf_op jit(solution)/shard_map/ppermute | solution.py:685
  290.5 9.3 %collective-permute-start.23 = (bf16[48,1152]{1,0:T(8,128)(2,1)S(1)}, bf16[48,1152]{1,0:T(8,128)(2,1)S(1)}, u32[]{:S(2)}, u32[]{:S(2)}) collective-permute-start(bf16[48,1152]{1,0:T(8,128)(2,1)S(1)} %get-tuple-element.165), channel_id=1, source_target_pairs={{0,16},{8,24},{16,0},{24,8},{1,17},{9,25},{17,1},{25,9},{2,18},{10... | collective-permute-start | bytes 331784 | tf_op jit(solution)/shard_map/ppermute | solution.py:685
  290.9 8.9 %collective-permute-start.24 = (bf16[48,1152]{1,0:T(8,128)(2,1)S(1)}, bf16[48,1152]{1,0:T(8,128)(2,1)}, u32[]{:S(2)}, u32[]{:S(2)}) collective-permute-start(bf16[48,1152]{1,0:T(8,128)(2,1)S(1)} %get-tuple-element.164), channel_id=1, source_target_pairs={{0,24},{8,0},{16,8},{24,16},{1,25},{9,1},{17,9},{25,17},{2,26},{10... | collective-permute-start | bytes 331784 | tf_op jit(solution)/shard_map/ppermute | solution.py:685
  302.7 5.6 %collective-permute-start.27 = (bf16[48,1920]{1,0:T(8,128)(2,1)S(1)}, bf16[48,1920]{1,0:T(8,128)(2,1)S(1)}, u32[]{:S(2)}, u32[]{:S(2)}) collective-permute-start(bf16[48,1920]{1,0:T(8,128)(2,1)S(1)} %dynamic-slice_bitcast_fusion.4), channel_id=1, source_target_pairs={{0,1},{1,0},{2,3},{3,2},{4,5},{5,4},{6,7},{7,6},{8,9},{9,8},{10,11... | collective-permute-start | bytes 552968 | tf_op jit(solution)/shard_map/ppermute | solution.py:685
  304.7 5.0 %copy-start.1 = (s32[2,512,512]{2,1,0:T(8,128)S(1)}, s32[2,512,512]{2,1,0:T(8,128)}, u32[]{:S(2)}) copy-start(s32[2,512,512]{2,1,0:T(8,128)} %param.21) | copy-start | bytes 6291460
  304.7 3.5 %copy-start.22 = (bf16[1,2,48,1920]{3,2,1,0:T(8,128)(2,1)S(1)}, bf16[1,2,48,1920]{3,2,1,0:T(8,128)(2,1)}, u32[]{:S(2)}) copy-start(bf16[1,2,48,1920]{3,2,1,0:T(8,128)(2,1)} %reduce-scatter.2.cloned.1.call-done) | copy-start | bytes 1105924
  (19 other events, 39.5 us)
Sparse Core Ops, SparseCore 0:
  11.5 93.2 all-gather.2
  181.7 95.0 reduce-scatter.1

commit v3 on v1

--- a/solution.py
+++ b/solution.py
@@ -113,9 +113,9 @@
         in_specs=[wide, thin, thin, square] + [pl.BlockSpec(memory_space=pl.ANY)] * len(before),
         out_specs=[square, wide, pl.BlockSpec((count, 1, both), lambda h: (h + begin, 0, 0))],
         out_shape=[
-            jax.ShapeDtypeStruct((heads, seq, both), BF),
-            jax.ShapeDtypeStruct((width, both), BF),
-            jax.ShapeDtypeStruct((heads, 1, both), F32),
+            pltpu.HBM((heads, seq, both), BF),
+            pltpu.HBM((width, both), BF),
+            pltpu.HBM((heads, 1, both), F32),
         ],
         input_output_aliases={4 + i: i for i in range(len(before))},
         compiler_params=pltpu.CompilerParams(vmem_limit_bytes=48 * 1024 * 1024),
@@ -238,7 +238,7 @@
         out_ref[...] = jnp.sum(kept.reshape(buckets, group, value.shape[1]), axis=1)
 
 
-def table_back(buckets_t, held, buckets, group=16, parts=4, after=()):
+def table_back(buckets_t, held, buckets, group=16, parts=8, after=()):
     seq = buckets_t.shape[0]
     cols = held.shape[1]
     return call(
@@ -532,7 +532,7 @@
             pl.BlockSpec((part, tokens), lambda y: (y, 0)),
         ],
         out_specs=pl.BlockSpec((owners, 1, rows, ffn + part), lambda y: (0, y, 0, 0)),
-        out_shape=jax.ShapeDtypeStruct((owners, halves, rows, ffn + part), BF),
+        out_shape=pltpu.HBM((owners, halves, rows, ffn + part), BF),
         compiler_params=pltpu.CompilerParams(vmem_limit_bytes=48 * 1024 * 1024),
         cost_estimate=cost(6),
     )
@@ -607,7 +607,7 @@
     chips = width // (2 * rows)
     part = width // halves
     block = pl.BlockSpec((1, chips, rows, 3 * part), lambda y: (y, 0, 0, 0))
-    shape = jax.ShapeDtypeStruct((halves, chips, rows, 3 * part), BF)
+    shape = pltpu.HBM((halves, chips, rows, 3 * part), BF)
     return call(
         project_back_kernel,
         after,
@@ -673,7 +673,7 @@
             thin,
         ],
         out_specs=[out, out],
-        out_shape=[jax.ShapeDtypeStruct((tokens, width // 2), BF)] * 2,
+        out_shape=[pltpu.HBM((tokens, width // 2), BF)] * 2,
         scratch_shapes=[pltpu.VMEM((tile, width), F32)],
         compiler_params=pltpu.CompilerParams(vmem_limit_bytes=40 * 1024 * 1024),
         cost_estimate=cost(5),

time: 306 us -> 304 us (level)
    unnamed x70 -> x64, local copies, waits for them, and re-layouts: 9.33 us -> 6.46 us
  transfers between devices with their start and end apart: 32 -> 32, of which waited for: 13 -> 12; matrix products, arithmetic and copies ran while one was open for 15% -> 15% of each run, Pallas kernels for 40% -> 41%
where the time goes in v3:
time: 304 us; the launch traced here: 302 us
  Pallas kernels  149 us (49%)
  waiting for transfers between devices  46.9 us (15%)
  starting transfers between devices  38.7 us (13%)
  other arithmetic  31.3 us (10%)
  local copies, waits for them, and re-layouts  21 us (7%)
  between operations  14.6 us (5%)
    pallas_call x12, Pallas kernels, call(): pl.pallas_call(body, in_specs=in_specs + anywhere, **settings)  149 us
    ppermute x25, waiting for transfers between devices, shifted(): lax.ppermute(value, axis, [(i, (i + step) % size) for i in range(size)])  36.2 us
    ppermute x25, starting transfers between devices, shifted(): lax.ppermute(value, axis, [(i, (i + step) % size) for i in range(size)])  30.7 us
    convert_element_type x6, other arithmetic, start(): out = [total(at(lax.rem(me + k, size))).astype(BF) for k in range(1, size)]  8.8 us
    ppermute x5, starting transfers between devices, sum_pairs(): lax.ppermute(value, axis, [(i, i ^ step) for i in range(size)])  7.96 us
    all_gather x1, waiting for transfers between devices, shards(): lax.all_gather(jnp.concatenate([w_in, w_down.T], axis=1), ('y', 'z', 'x',...  6.78 us
    unnamed x64, local copies, waits for them, and re-layouts  6.46 us
  transfers between devices with their start and end apart: 32, of which 12 were waited for; matrix products, arithmetic and copies ran while one was open for 15% of the time, Pallas kernels for 41%

profile of v3, /device:TPU:0, one launch (start us, length us, event | category | flops | bytes accessed | tf_op | source)
XLA Modules:
  0.0 301.6 jit_solution(4803917877269697380)
XLA Ops:
  7.2 1.9 pad_maximum_fusion.9
  10.0 1.4 pad_maximum_fusion.10
  11.4 5.0 %collective-permute-start = (bf16[48,1536]{1,0:T(8,128)(2,1)}, bf16[48,1536]{1,0:T(8,128)(2,1)S(1)}, u32[]{:S(2)}, u32[]{:S(2)}) collective-permute-start(bf16[48,1536]{1,0:T(8,128)(2,1)} %pad_maximum_fusion.10), channel_id=1, source_target_pairs={{0,24},{8,0},{16,8},{24,16},{1,25},{9,1},{17,9},{25,17},{2,26},{10... | collective-permute-start | bytes 442376 | tf_op jit(solution)/shard_map/ppermute | solution.py:685
  20.3 1.5 collective-permute-start.5
  26.0 7.8 %collective-permute-done.1 = bf16[48,1536]{1,0:T(8,128)(2,1)S(1)} collective-permute-done((bf16[48,1536]{1,0:T(8,128)(2,1)}, bf16[48,1536]{1,0:T(8,128)(2,1)S(1)}, u32[]{:S(2)}, u32[]{:S(2)}) %collective-permute-start.1) | collective-permute-done | bytes 147488 | tf_op jit(solution)/shard_map/ppermute | solution.py:685
  36.0 1.6 collective-permute-start.3
  37.6 1.7 collective-permute-start.4
  40.8 8.6 %shard_map.272.refs_3_ = bf16[12,512,1024]{2,1,0:T(8,128)(2,1)} custom-call(s32[1]{0:T(128)} %dynamic_slice.183.refs_0_, s32[512,512]{1,0:T(8,128)} %bitcast.188, s32[1,512]{1,0:T(1,128)} %constant_dynamic-slice_fusion.3.refs_2_, s32[512,1]{1,0:T(8,128)} %copy.51.refs_3_, f32[12,128]{1,0:T(8,128)} %pad.15.refs_4_), custom_call_target="tpu_custom_call" | custom-call | flops 90000000 | bytes 90000 | tf_op jit(solution)/shard_map/pallas_call | solution.py:272
  50.7 15.1 %collective-permute-done.7 = bf16[2,4,48,768]{3,2,1,0:T(8,128)(2,1)S(1)} collective-permute-done((bf16[2,4,48,768]{3,2,1,0:T(8,128)(2,1)S(1)}, bf16[2,4,48,768]{3,2,1,0:T(8,128)(2,1)S(1)}, u32[]{:S(2)}, u32[]{:S(2)}) %collective-permute-start.7) | collective-permute-done | bytes 589856 | tf_op jit(solution)/shard_map/ppermute | solution.py:685
  68.4 1.5 dynamic-slice_bitcast_fusion.2
  74.4 7.8 %shard_map.273 = (bf16[768,1024]{1,0:T(8,128)(2,1)}, bf16[768,512]{1,0:T(8,128)(2,1)}, bf16[768,512]{1,0:T(8,128)(2,1)}, bf16[2,8,2,48,1536]{4,3,2,1,0:T(8,128)(2,1)}) custom-call(s32[1]{0:T(128)} %bitcast.refs_0_, bf16[2,8,48,768]{3,2,1,0:T(8,128)(2,1)} %copy-done.6, bf16[2,8,48,768]{3,2,1,0:T(8,128)(2,1)} %bitcast.193, ...), custom_call_target="tpu_custom_call" | custom-call | flops 60000000 | bytes 60000 | tf_op jit(solution)/shard_map/pallas_call | solution.py:272
  82.2 16.3 %shard_map.274 = (bf16[12,512,1024]{2,1,0:T(8,128)(2,1)}, bf16[768,1024]{1,0:T(8,128)(2,1)}, f32[12,1,1024]{2,1,0:T(1,128)}) custom-call(bf16[768,1024]{1,0:T(8,128)(2,1)} %get-tuple-element.81.refs_0_, bf16[768,512]{1,0:T(8,128)(2,1)} %get-tuple-element.82.refs_1_, bf16[768,512]{1,0:T(8,128)(2,1)} %get-tuple-element.83.refs_2_, ...), custom_call_target="tpu_custom_call" | custom-call | flops 180000000 | bytes 180000 | tf_op jit(solution)/shard_map/pallas_call | solution.py:272
  98.5 6.8 %all-gather.3.cloned.1.call-done = bf16[1536,3072]{1,0:T(8,128)(2,1)} async-done(((bf16[48,3072]{1,0:T(8,128)(2,1)}), bf16[1536,3072]{1,0:T(8,128)(2,1)}) %all-gather.3.cloned.1.call-update) | async-done | bytes 9437200 | tf_op jit(solution)/shard_map/all_gather | solution.py:790
  105.3 25.5 %shard_map.275 = (bf16[1024,768]{1,0:T(8,128)(2,1)}, bf16[768,1024]{1,0:T(8,128)(2,1)}, bf16[2,1024,1536]{2,1,0:T(8,128)(2,1)}, bf16[2,1024,1536]{2,1,0:T(8,128)...) custom-call(bf16[768,1024]{1,0:T(8,128)(2,1)} %get-tuple-element.85., ...), custom_call_target="tpu_custom_call" | custom-call | flops 200000000 | bytes 200000 | tf_op jit(solution)/shard_map/pallas_call | solution.py:272
  130.8 1.5 collective-permute-start.10
  132.3 22.4 %shard_map.276 = (bf16[2,1024,1536]{2,1,0:T(8,128)(2,1)}, f32[1024,768]{1,0:T(8,128)}, bf16[768,1024]{1,0:T(8,128)(2,1)}, bf16[768,1024]{1,0:T(8,128)(2,1)}, f32...) custom-call(bf16[1024,768]{1,0:T(8,128)(2,1)} %get-tuple-element.91.refs_0_, f32[1024,768]{1,0:T(8,128)} %get-tuple-element.92.refs_1_, ...), custom_call_target="tpu_custom_call" | custom-call | flops 180000000 | bytes 180000 | tf_op jit(solution)/shard_map/pallas_call | solution.py:272
  154.7 11.6 %shard_map.277.refs_3_ = bf16[16,2,48,1920]{3,2,1,0:T(8,128)(2,1)} custom-call(bf16[768,1024]{1,0:T(8,128)(2,1)} %get-tuple-element.90.refs_0_, bf16[2,1024,1536]{2,1,0:T(8,128)(2,1)} %get-tuple-element.96.refs_1_, bf16[768,1024]{1,0:T(8,128)(2,1)} %get-tuple-element.97.refs_2_, bf16[768,1024]{1,0:T(8,128)(2,1)} %get-tuple-element.85.refs_0_.refs_3_.refs_5_), custom_call_target="tpu_custom_call" | custom-call | flops 60000000 | bytes 60000 | tf_op jit(solution)/shard_map/pallas_call | solution.py:272
  167.6 10.1 %shard_map.278 = (bf16[2,8,48,1536]{3,2,1,0:T(8,128)(2,1)}, bf16[2,8,48,1536]{3,2,1,0:T(8,128)(2,1)}) custom-call(s32[1]{0:T(128)} %bitcast.refs_0_, bf16[768,1024]{1,0:T(8,128)(2,1)} %get-tuple-element.87.refs_1_, bf16[2,1024,1536]{2,1,0:T(8,128)(2,1)} %get-tuple-element.88.refs_2_, bf16[16,2,48,1920]{3,2,1,0:T(8,128)(2,1)} %shard_map.277.refs_3_), custom_call_target="tpu_custom_call" | custom-call | flops 50000000 | bytes 50000 | tf_op jit(solution)/shard_map/pallas_call | solution.py:272
  177.7 5.8 %shard_map.279 = (bf16[768,1024]{1,0:T(8,128)(2,1)}, bf16[768,512]{1,0:T(8,128)(2,1)}, bf16[768,512]{1,0:T(8,128)(2,1)}, bf16[32,192,512]{2,1,0:T(8,128)(2,1)}) custom-call(bf16[768,1024]{1,0:T(8,128)(2,1)} %get-tuple-element.81.refs_0_, bf16[768,512]{1,0:T(8,128)(2,1)} %get-tuple-element.82.refs_1_, bf16[768,512]{1,0:T(8,128)(2,1)} %get-tuple-element.83.refs_2_, ...), custom_call_target="tpu_custom_call" | custom-call | flops 99999997952 | bytes 100000000 | tf_op jit(solution)/shard_map/pallas_call | solution.py:272
  183.6 1.6 fusion.3.refs_11_
  185.4 1.5 collective-permute-start.12
  187.0 16.1 %shard_map.280 = (bf16[768,1024]{1,0:T(8,128)(2,1)}, bf16[768,512]{1,0:T(8,128)(2,1)}, bf16[768,512]{1,0:T(8,128)(2,1)}, bf16[32,192,512]{2,1,0:T(8,128)(2,1)}) custom-call(bf16[768,1024]{1,0:T(8,128)(2,1)} %get-tuple-element.81.refs_0_, ...), custom_call_target="tpu_custom_call", output_to_operand_aliasing={{0}: (7, {}), {1}: (8, {}), {2}: (9, {}), {3}: (10, {})} | custom-call | flops 499999997952 | bytes 500000000 | tf_op jit(solution)/shard_map/pallas_call | solution.py:272
  203.1 8.0 %shard_map.281 = (bf16[2,8,48,1152]{3,2,1,0:T(8,128)(2,1)}, bf16[2,8,48,1152]{3,2,1,0:T(8,128)(2,1)}) custom-call(s32[1]{0:T(128)} %bitcast.refs_0_, bf16[1024,768]{1,0:T(8,128)(2,1)} %pad_maximum_fusion.1.refs_5_.refs_1_, bf16[768,1024]{1,0:T(8,128)(2,1)} %get-tuple-element.113.refs_2_.refs_3_, bf16[768,512]{1,0:T(8,128)(2,1)} %get-tuple-element.114.refs_3_.refs_4_, ...), custom_call_target="tpu_custom_call" | custom-call | flops 50000000 | bytes 50000 | tf_op jit(solution)/shard_map/pallas_call | solution.py:272
  211.1 3.0 collective-permute-done.12
  214.3 1.7 fusion.4.refs_4_
  216.0 1.5 collective-permute-start.14
  218.6 1.7 convert_reduce_fusion
  220.5 1.5 copy-done.3
  222.0 7.7 %shard_map.282 = f32[32,192]{1,0:T(8,128)S(1)} custom-call(s32[512,512]{1,0:T(8,128)} %bitcast.189, bf16[32,192,512]{2,1,0:T(8,128)(2,1)} %get-tuple-element.121.refs_1_, bf16[2,8,48,1152]{3,2,1,0:T(8,128)(2,1)S(1)} %copy-done.2, bf16[2,8,48,1152]{3,2,1,0:T(8,128)(2,1)S(1)} %copy-done.3, bf16[4,48,1536]{2,1,0:T(8,128)(2,1)S(1)} %fusion.4.refs_4_), custom_call_target="tpu_custom_call" | custom-call | flops 60000000 | bytes 60000 | tf_op jit(solution)/shard_map/pallas_call | solution.py:272
  229.8 2.2 collective-permute-done.14
  233.5 1.5 collective-permute-start.15
  235.2 1.8 fusion.14
  237.0 1.5 collective-permute-start.27
  239.6 2.3 collective-permute-start.29
  241.9 9.0 %shard_map.283 = (bf16[1024,384]{1,0:T(8,128)(2,1)}, bf16[1024,384]{1,0:T(8,128)(2,1)}) custom-call(s32[1]{0:T(128)} %bitcast.40.refs_0_, bf16[2,768,1536]{2,1,0:T(8,128)(2,1)} %bitcast.187, f32[1024,768]{1,0:T(8,128)} %get-tuple-element.123.refs_2_, bf16[768,1024]{1,0:T(8,128)(2,1)} %get-tuple-element.113.refs_2_.refs_3_, ...), custom_call_target="tpu_custom_call" | custom-call | flops 50000000 | bytes 50000 | tf_op jit(solution)/shard_map/pallas_call | solution.py:272
  250.9 4.0 %collective-permute-done.15 = bf16[4,2,48,1152]{3,2,1,0:T(8,128)(2,1)S(1)} collective-permute-done((bf16[4,2,48,1152]{3,2,1,0:T(8,128)(2,1)S(1)}, bf16[4,2,48,1152]{3,2,1,0:T(8,128)(2,1)S(1)}, u32[]{:S(2)}, u32[]{:S(2)}) %collective-permute-start.15) | collective-permute-done | bytes 884768 | tf_op jit(solution)/shard_map/ppermute | solution.py:685
  254.9 1.5 collective-permute-start.19
  257.5 1.5 collective-permute-start.18
  259.1 2.0 fusion.13
  261.6 3.3 %collective-permute-start.20 = (f32[75,128]{1,0:T(8,128)S(1)}, f32[75,128]{1,0:T(8,128)S(1)}, u32[]{:S(2)}, u32[]{:S(2)}) collective-permute-start(f32[75,128]{1,0:T(8,128)S(1)} %add.498), channel_id=1, source_target_pairs={{0,16},{8,24},{16,0},{24,8},{1,17},{9,25},{17,1},{25,9},{2,18},{10... | collective-permute-start | bytes 115208 | tf_op jit(solution)/shard_map/ppermute | solution.py:751
  265.1 1.8 collective-permute-done.20
  268.2 1.6 collective-permute-start.24
  269.8 1.9 fusion.2
  272.2 1.6 collective-permute-start.25
  275.0 1.9 collective-permute-start.21
  279.4 1.6 collective-permute-done.25
  289.0 1.5 broadcast_select_fusion.2
  291.9 1.4 collective-permute-done.26
  (179 shorter events, 45.0 us)
Async XLA Ops:
  7.2 14.6 %copy-start = (s32[2,512,512]{2,1,0:T(8,128)S(1)}, s32[2,512,512]{2,1,0:T(8,128)}, u32[]{:S(2)}) copy-start(s32[2,512,512]{2,1,0:T(8,128)} %param.21) | copy-start | bytes 6291460
  7.2 98.1 %all-gather.3.cloned.1.call-start = ((), (), s32[]{:S(2)}) async-start(), calls=%async_computation.2 | async-start | bytes 9732096 | tf_op jit(solution)/shard_map/all_gather | solution.py:790
  9.1 277.6 %reduce-scatter.2.cloned.1.call-start = ((), (), s32[]{:S(2)}) async-start(), calls=%async_computation.1 | async-start | bytes 6266880 | tf_op jit(solution)/shard_map/reduce_scatter | solution.py:839
  11.4 14.6 %collective-permute-start = (bf16[48,1536]{1,0:T(8,128)(2,1)}, bf16[48,1536]{1,0:T(8,128)(2,1)S(1)}, u32[]{:S(2)}, u32[]{:S(2)}) collective-permute-start(bf16[48,1536]{1,0:T(8,128)(2,1)} %pad_maximum_fusion.10), channel_id=1, source_target_pairs={{0,24},{8,0},{16,8},{24,16},{1,25},{9,1},{17,9},{25,17},{2,26},{10... | collective-permute-start | bytes 442376 | tf_op jit(solution)/shard_map/ppermute | solution.py:685
  16.5 17.3 %collective-permute-start.1 = (bf16[48,1536]{1,0:T(8,128)(2,1)}, bf16[48,1536]{1,0:T(8,128)(2,1)S(1)}, u32[]{:S(2)}, u32[]{:S(2)}) collective-permute-start(bf16[48,1536]{1,0:T(8,128)(2,1)} %pad_maximum_fusion.10), channel_id=1, source_target_pairs={{0,16},{8,24},{16,0},{24,8},{1,17},{9,25},{17,1},{25,9},{2,18},{10... | collective-permute-start | bytes 442376 | tf_op jit(solution)/shard_map/ppermute | solution.py:685
  16.5 17.3 %collective-permute-start.2 = (bf16[48,1536]{1,0:T(8,128)(2,1)}, bf16[48,1536]{1,0:T(8,128)(2,1)}, u32[]{:S(2)}, u32[]{:S(2)}) collective-permute-start(bf16[48,1536]{1,0:T(8,128)(2,1)} %pad_maximum_fusion.10), channel_id=1, source_target_pairs={{0,8},{8,16},{16,24},{24,0},{1,9},{9,17},{17,25},{25,1},{2,10},{10... | collective-permute-start | bytes 442376 | tf_op jit(solution)/shard_map/ppermute | solution.py:685
  18.3 3.5 %copy-start.18 = (bf16[32,6]{1,0:T(8,128)(2,1)}, bf16[32,6]{1,0:T(8,128)(2,1)S(1)}, u32[]{:S(2)}) copy-start(bf16[32,6]{1,0:T(8,128)(2,1)S(1)} %copy.49) | copy-start | bytes 1156
  20.3 19.0 %collective-permute-start.5 = (bf16[38,384]{1,0:T(8,128)(2,1)}, bf16[38,384]{1,0:T(8,128)(2,1)}, u32[]{:S(2)}, u32[]{:S(2)}) collective-permute-start(bf16[38,384]{1,0:T(8,128)(2,1)} %fusion.24), channel_id=1, source_target_pairs={{0,1},{1,0},{2,3},{3,2},{4,5},{5,4},{6,7},{7,6},{8,9},{9,8},{10,11... | collective-permute-start | bytes 87560 | tf_op jit(solution)/shard_map/ppermute | solution.py:685
  21.9 2.9 copy-start.25
  21.9 3.5 %copy-start.21 = (s32[2,512]{1,0:T(2,128)S(1)}, s32[2,512]{1,0:T(2,128)}, u32[]{:S(2)}) copy-start(s32[2,512]{1,0:T(2,128)} %param.20) | copy-start | bytes 12292
  21.9 11.9 %copy-start.15 = (bf16[384,48]{0,1:T(8,128)(2,1)S(1)}, bf16[384,48]{0,1:T(8,128)(2,1)}, u32[]{:S(2)}) copy-start(bf16[384,48]{0,1:T(8,128)(2,1)} %param.24) | copy-start | bytes 110596
  34.9 4.4 %copy-start.19 = (bf16[32,6]{1,0:T(8,128)(2,1)S(1)}, bf16[32,6]{1,0:T(8,128)(2,1)}, u32[]{:S(2)}) copy-start(bf16[32,6]{1,0:T(8,128)(2,1)} %copy-done.18) | copy-start | bytes 1156
  34.9 4.4 %copy-start.20 = (bf16[2,384]{1,0:T(2,128)(2,1)S(1)}, bf16[2,384]{1,0:T(2,128)(2,1)}, u32[]{:S(2)}) copy-start(bf16[2,384]{1,0:T(2,128)(2,1)} %param.23) | copy-start | bytes 4612
  36.0 13.4 %collective-permute-start.3 = (bf16[4,48,768]{2,1,0:T(8,128)(2,1)S(1)}, bf16[4,48,768]{2,1,0:T(8,128)(2,1)S(1)}, u32[]{:S(2)}, u32[]{:S(2)}) collective-permute-start(bf16[4,48,768]{2,1,0:T(8,128)(2,1)S(1)} %get-tuple-element.78), channel_id=1, source_target_pairs={{0,4},{4,0},{1,5},{5,1},{2,6},{6,2},{3,7},{7,3},{8,12},{12,8},{9,1... | collective-permute-start | bytes 884744 | tf_op jit(solution)/shard_map/ppermute | solution.py:685
  37.6 11.8 %collective-permute-start.4 = (bf16[4,48,768]{2,1,0:T(8,128)(2,1)S(1)}, bf16[4,48,768]{2,1,0:T(8,128)(2,1)S(1)}, u32[]{:S(2)}, u32[]{:S(2)}) collective-permute-start(bf16[4,48,768]{2,1,0:T(8,128)(2,1)S(1)} %get-tuple-element.80), channel_id=1, source_target_pairs={{0,1},{1,0},{2,3},{3,2},{4,5},{5,4},{6,7},{7,6},{8,9},{9,8},{10,11... | collective-permute-start | bytes 884744 | tf_op jit(solution)/shard_map/ppermute | solution.py:685
  49.6 16.1 %collective-permute-start.7 = (bf16[2,4,48,768]{3,2,1,0:T(8,128)(2,1)S(1)}, bf16[2,4,48,768]{3,2,1,0:T(8,128)(2,1)S(1)}, u32[]{:S(2)}, u32[]{:S(2)}) collective-permute-start(bf16[2,4,48,768]{3,2,1,0:T(8,128)(2,1)S(1)} %pad_maximum_fusion.8), channel_id=1, source_target_pairs={{0,4},{4,0},{1,5},{5,1},{2,6},{6,2},{3,7},{7,3},{8,12},{12,8},{9,1... | collective-permute-start | bytes 1769480 | tf_op jit(solution)/shard_map/ppermute | solution.py:685
  50.1 16.0 %collective-permute-start.6 = (bf16[4,2,48,768]{3,2,0,1:T(8,128)(2,1)S(1)}, bf16[4,2,48,768]{3,2,0,1:T(8,128)(2,1)S(1)}, u32[]{:S(2)}, u32[]{:S(2)}) collective-permute-start(bf16[4,2,48,768]{3,2,0,1:T(8,128)(2,1)S(1)} %pad_maximum_fusion.7), channel_id=1, source_target_pairs={{0,1},{1,0},{2,3},{3,2},{4,5},{5,4},{6,7},{7,6},{8,9},{9,8},{10,11... | collective-permute-start | bytes 1769480 | tf_op jit(solution)/shard_map/ppermute | solution.py:685
  66.0 8.3 %collective-permute-start.9 = (bf16[2,8,48,768]{3,2,1,0:T(8,128)(2,1)S(1)}, bf16[2,8,48,768]{3,2,1,0:T(8,128)(2,1)}, u32[]{:S(2)}, u32[]{:S(2)}) collective-permute-start(bf16[2,8,48,768]{3,2,1,0:T(8,128)(2,1)S(1)} %bitcast.192), channel_id=1, source_target_pairs={{0,2},{2,0},{1,3},{3,1},{4,6},{6,4},{5,7},{7,5},{8,10},{10,8},{9,1... | collective-permute-start | bytes 3538952 | tf_op jit(solution)/shard_map/ppermute | solution.py:685
  67.3 7.1 %collective-permute-start.8 = (bf16[2,8,48,768]{3,2,1,0:T(8,128)(2,1)S(1)}, bf16[2,8,48,768]{3,2,1,0:T(8,128)(2,1)}, u32[]{:S(2)}, u32[]{:S(2)}) collective-permute-start(bf16[2,8,48,768]{3,2,1,0:T(8,128)(2,1)S(1)} %pad_maximum_fusion.3.refs_1_), channel_id=1, source_target_pairs={{0,2},{2,0},{1,3},{3,1},{4,6},{6,4},{5,7},{7,5},{8,10},{10,8},{9,1... | collective-permute-start | bytes 3538952 | tf_op jit(solution)/shard_map/ppermute | solution.py:685
  130.8 36.8 %collective-permute-start.10 = (bf16[1024,768]{1,0:T(8,128)(2,1)}, bf16[1024,768]{1,0:T(8,128)(2,1)S(1)}, u32[]{:S(2)}, u32[]{:S(2)}) collective-permute-start(bf16[1024,768]{1,0:T(8,128)(2,1)} %get-tuple-element.132), channel_id=1, source_target_pairs={{0,1},{1,0},{2,3},{3,2},{4,5},{5,4},{6,7},{7,6},{8,9},{9,8},{10,11... | collective-permute-start | bytes 4718600 | tf_op jit(solution)/shard_map/ppermute | solution.py:685
  167.6 10.1 %copy-start.10 = (bf16[1024,768]{1,0:T(8,128)(2,1)}, bf16[1024,768]{1,0:T(8,128)(2,1)S(1)}, u32[]{:S(2)}) copy-start(bf16[1024,768]{1,0:T(8,128)(2,1)S(1)} %collective-permute-done.10) | copy-start | bytes 4718596
  177.7 5.8 %collective-permute-start.11 = (bf16[2,8,48,1536]{3,2,1,0:T(8,128)(2,1)}, bf16[2,8,48,1536]{3,2,1,0:T(8,128)(2,1)S(1)}, u32[]{:S(2)}, u32[]{:S(2)}) collective-permute-start(bf16[2,8,48,1536]{3,2,1,0:T(8,128)(2,1)} %get-tuple-element.100.refs_8_), channel_id=1, source_target_pairs={{0,2},{2,0},{1,3},{3,1},{4,6},{6,4},{5,7},{7,5},{8,10},{10,8},{9,1... | collective-permute-start | bytes 7077896 | tf_op jit(solution)/shard_map/ppermute | solution.py:685
  177.7 5.8 %copy-start.7 = (bf16[2,8,48,1536]{3,2,1,0:T(8,128)(2,1)S(1)}, bf16[2,8,48,1536]{3,2,1,0:T(8,128)(2,1)}, u32[]{:S(2)}) copy-start(bf16[2,8,48,1536]{3,2,1,0:T(8,128)(2,1)} %get-tuple-element.99.refs_7_) | copy-start | bytes 7077892
  185.4 28.7 %collective-permute-start.12 = (bf16[4,2,48,1536]{3,2,1,0:T(8,128)(2,1)}, bf16[4,2,48,1536]{3,2,1,0:T(8,128)(2,1)}, u32[]{:S(2)}, u32[]{:S(2)}) collective-permute-start(bf16[4,2,48,1536]{3,2,1,0:T(8,128)(2,1)} %fusion.3.refs_11_), channel_id=1, source_target_pairs={{0,1},{1,0},{2,3},{3,2},{4,5},{5,4},{6,7},{7,6},{8,9},{9,8},{10,11... | collective-permute-start | bytes 3538952 | tf_op jit(solution)/shard_map/ppermute | solution.py:685
  203.1 11.1 %copy-start.17 = (f32[4,3,8,768]{3,2,1,0:T(8,128)S(1)}, f32[4,3,8,768]{3,2,1,0:T(8,128)}, u32[]{:S(2)}) copy-start(f32[4,3,8,768]{3,2,1,0:T(8,128)} %get-tuple-element.129) | copy-start | bytes 884740
  203.1 11.1 %copy-start.16 = (f32[4,3,8,768]{3,2,1,0:T(8,128)S(1)}, f32[4,3,8,768]{3,2,1,0:T(8,128)}, u32[]{:S(2)}) copy-start(f32[4,3,8,768]{3,2,1,0:T(8,128)} %get-tuple-element.130) | copy-start | bytes 884740
  214.2 17.8 %collective-permute-start.13 = (bf16[2,8,48,1152]{3,2,1,0:T(8,128)(2,1)}, bf16[2,8,48,1152]{3,2,1,0:T(8,128)(2,1)}, u32[]{:S(2)}, u32[]{:S(2)}) collective-permute-start(bf16[2,8,48,1152]{3,2,1,0:T(8,128)(2,1)} %get-tuple-element.119.refs_3_), channel_id=1, source_target_pairs={{0,2},{2,0},{1,3},{3,1},{4,6},{6,4},{5,7},{7,5},{8,10},{10,8},{9,1... | collective-permute-start | bytes 5308424 | tf_op jit(solution)/shard_map/ppermute | solution.py:685
  214.3 6.0 %copy-start.4 = (bf16[768,512]{1,0:T(8,128)(2,1)S(1)}, bf16[768,512]{1,0:T(8,128)(2,1)}, u32[]{:S(2)}) copy-start(bf16[768,512]{1,0:T(8,128)(2,1)} %get-tuple-element.115.refs_4_.refs_5_) | copy-start | bytes 2359300
  216.0 4.5 %copy-start.2 = (bf16[2,8,48,1152]{3,2,1,0:T(8,128)(2,1)S(1)}, bf16[2,8,48,1152]{3,2,1,0:T(8,128)(2,1)}, u32[]{:S(2)}) copy-start(bf16[2,8,48,1152]{3,2,1,0:T(8,128)(2,1)} %get-tuple-element.118.refs_2_) | copy-start | bytes 5308420
  216.0 15.9 %collective-permute-start.14 = (bf16[4,48,1536]{2,1,0:T(8,128)(2,1)S(1)}, bf16[4,48,1536]{2,1,0:T(8,128)(2,1)}, u32[]{:S(2)}, u32[]{:S(2)}) collective-permute-start(bf16[4,48,1536]{2,1,0:T(8,128)(2,1)S(1)} %fusion.4.refs_4_), channel_id=1, source_target_pairs={{0,4},{4,0},{1,5},{5,1},{2,6},{6,2},{3,7},{7,3},{8,12},{12,8},{9,1... | collective-permute-start | bytes 1769480 | tf_op jit(solution)/shard_map/ppermute | solution.py:685
  233.5 21.3 %collective-permute-start.15 = (bf16[4,2,48,1152]{3,2,1,0:T(8,128)(2,1)S(1)}, bf16[4,2,48,1152]{3,2,1,0:T(8,128)(2,1)S(1)}, u32[]{:S(2)}, u32[]{:S(2)}) collective-permute-start(bf16[4,2,48,1152]{3,2,1,0:T(8,128)(2,1)S(1)} %fusion.5.refs_6_), channel_id=1, source_target_pairs={{0,1},{1,0},{2,3},{3,2},{4,5},{5,4},{6,7},{7,6},{8,9},{9,8},{10,11... | collective-permute-start | bytes 2654216 | tf_op jit(solution)/shard_map/ppermute | solution.py:685
  235.1 15.8 %collective-permute-start.16 = (f32[75,128]{1,0:T(8,128)S(1)}, f32[75,128]{1,0:T(8,128)S(1)}, u32[]{:S(2)}, u32[]{:S(2)}) collective-permute-start(f32[75,128]{1,0:T(8,128)S(1)} %bitcast.212), channel_id=1, source_target_pairs={{0,2},{2,0},{1,3},{3,1},{4,6},{6,4},{5,7},{7,5},{8,10},{10,8},{9,1... | collective-permute-start | bytes 115208 | tf_op jit(solution)/shard_map/ppermute | solution.py:751
  237.0 22.1 %collective-permute-start.27 = (bf16[48,1536]{1,0:T(8,128)(2,1)S(1)}, bf16[48,1536]{1,0:T(8,128)(2,1)S(1)}, u32[]{:S(2)}, u32[]{:S(2)}) collective-permute-start(bf16[48,1536]{1,0:T(8,128)(2,1)S(1)} %get-tuple-element.162.refs_7_), channel_id=1, source_target_pairs={{0,8},{8,16},{16,24},{24,0},{1,9},{9,17},{17,25},{25,1},{2,10},{10... | collective-permute-start | bytes 442376 | tf_op jit(solution)/shard_map/ppermute | solution.py:685
  238.5 20.5 %collective-permute-start.28 = (bf16[48,1536]{1,0:T(8,128)(2,1)S(1)}, bf16[48,1536]{1,0:T(8,128)(2,1)S(1)}, u32[]{:S(2)}, u32[]{:S(2)}) collective-permute-start(bf16[48,1536]{1,0:T(8,128)(2,1)S(1)} %get-tuple-element.161.refs_8_), channel_id=1, source_target_pairs={{0,16},{8,24},{16,0},{24,8},{1,17},{9,25},{17,1},{25,9},{2,18},{10... | collective-permute-start | bytes 442376 | tf_op jit(solution)/shard_map/ppermute | solution.py:685
  239.6 19.4 %collective-permute-start.29 = (bf16[48,1536]{1,0:T(8,128)(2,1)S(1)}, bf16[48,1536]{1,0:T(8,128)(2,1)S(1)}, u32[]{:S(2)}, u32[]{:S(2)}) collective-permute-start(bf16[48,1536]{1,0:T(8,128)(2,1)S(1)} %get-tuple-element.160.refs_9_), channel_id=1, source_target_pairs={{0,24},{8,0},{16,8},{24,16},{1,25},{9,1},{17,9},{25,17},{2,26},{10... | collective-permute-start | bytes 442376 | tf_op jit(solution)/shard_map/ppermute | solution.py:685
  254.9 10.0 %copy-start.9 = (bf16[1024,768]{1,0:T(8,128)(2,1)S(1)}, bf16[1024,768]{1,0:T(8,128)(2,1)}, u32[]{:S(2)}) copy-start(bf16[1024,768]{1,0:T(8,128)(2,1)} %get-tuple-element.132) | copy-start | bytes 4718596
  254.9 10.0 %copy-start.11 = (bf16[1024,768]{1,0:T(8,128)(2,1)S(1)}, bf16[1024,768]{1,0:T(8,128)(2,1)}, u32[]{:S(2)}) copy-start(bf16[1024,768]{1,0:T(8,128)(2,1)} %copy-done.10) | copy-start | bytes 4718596
  254.9 6.7 %collective-permute-start.19 = (f32[75,128]{1,0:T(8,128)S(1)}, f32[75,128]{1,0:T(8,128)S(1)}, u32[]{:S(2)}, u32[]{:S(2)}) collective-permute-start(f32[75,128]{1,0:T(8,128)S(1)} %bitcast_add_fusion), channel_id=1, source_target_pairs={{0,8},{8,0},{16,24},{24,16},{1,9},{9,1},{17,25},{25,17},{2,10},{10... | collective-permute-start | bytes 115208 | tf_op jit(solution)/shard_map/ppermute | solution.py:751
  257.5 10.7 %collective-permute-start.18 = (bf16[4,48,1152]{2,1,0:T(8,128)(2,1)S(1)}, bf16[4,48,1152]{2,1,0:T(8,128)(2,1)S(1)}, u32[]{:S(2)}, u32[]{:S(2)}) collective-permute-start(bf16[4,48,1152]{2,1,0:T(8,128)(2,1)S(1)} %fusion.6), channel_id=1, source_target_pairs={{0,4},{4,0},{1,5},{5,1},{2,6},{6,2},{3,7},{7,3},{8,12},{12,8},{9,1... | collective-permute-start | bytes 1327112 | tf_op jit(solution)/shard_map/ppermute | solution.py:685
  261.0 28.0 %collective-permute-start.17 = (bf16[1024,384]{1,0:T(8,128)(2,1)}, bf16[1024,384]{1,0:T(8,128)(2,1)}, u32[]{:S(2)}, u32[]{:S(2)}) collective-permute-start(bf16[1024,384]{1,0:T(8,128)(2,1)} %get-tuple-element.135), channel_id=1, source_target_pairs={{0,1},{1,0},{2,3},{3,2},{4,5},{5,4},{6,7},{7,6},{8,9},{9,8},{10,11... | collective-permute-start | bytes 2359304 | tf_op jit(solution)/shard_map/ppermute | solution.py:685
  261.6 5.3 %collective-permute-start.20 = (f32[75,128]{1,0:T(8,128)S(1)}, f32[75,128]{1,0:T(8,128)S(1)}, u32[]{:S(2)}, u32[]{:S(2)}) collective-permute-start(f32[75,128]{1,0:T(8,128)S(1)} %add.498), channel_id=1, source_target_pairs={{0,16},{8,24},{16,0},{24,8},{1,17},{9,25},{17,1},{25,9},{2,18},{10... | collective-permute-start | bytes 115208 | tf_op jit(solution)/shard_map/ppermute | solution.py:751
  268.2 4.0 %collective-permute-start.24 = (f32[75,128]{1,0:T(8,128)S(1)}, f32[75,128]{1,0:T(8,128)S(1)}, u32[]{:S(2)}, u32[]{:S(2)}) collective-permute-start(f32[75,128]{1,0:T(8,128)S(1)} %add.499), channel_id=1, source_target_pairs={{0,4},{4,0},{1,5},{5,1},{2,6},{6,2},{3,7},{7,3},{8,12},{12,8},{9,1... | collective-permute-start | bytes 115208 | tf_op jit(solution)/shard_map/ppermute | solution.py:751
  272.2 8.8 %collective-permute-start.25 = (f32[75,128]{1,0:T(8,128)S(1)}, f32[75,128]{1,0:T(8,128)S(1)}, u32[]{:S(2)}, u32[]{:S(2)}) collective-permute-start(f32[75,128]{1,0:T(8,128)S(1)} %add.516), channel_id=1, source_target_pairs={{0,1},{1,0},{2,3},{3,2},{4,5},{5,4},{6,7},{7,6},{8,9},{9,8},{10,11... | collective-permute-start | bytes 115208 | tf_op jit(solution)/shard_map/ppermute | solution.py:751
  275.0 9.7 %collective-permute-start.21 = (bf16[48,1152]{1,0:T(8,128)(2,1)S(1)}, bf16[48,1152]{1,0:T(8,128)(2,1)}, u32[]{:S(2)}, u32[]{:S(2)}) collective-permute-start(bf16[48,1152]{1,0:T(8,128)(2,1)S(1)} %get-tuple-element.163), channel_id=1, source_target_pairs={{0,8},{8,16},{16,24},{24,0},{1,9},{9,17},{17,25},{25,1},{2,10},{10... | collective-permute-start | bytes 331784 | tf_op jit(solution)/shard_map/ppermute | solution.py:685
  276.9 7.8 %collective-permute-start.22 = (bf16[48,1152]{1,0:T(8,128)(2,1)S(1)}, bf16[48,1152]{1,0:T(8,128)(2,1)}, u32[]{:S(2)}, u32[]{:S(2)}) collective-permute-start(bf16[48,1152]{1,0:T(8,128)(2,1)S(1)} %get-tuple-element.165), channel_id=1, source_target_pairs={{0,16},{8,24},{16,0},{24,8},{1,17},{9,25},{17,1},{25,9},{2,18},{10... | collective-permute-start | bytes 331784 | tf_op jit(solution)/shard_map/ppermute | solution.py:685
  278.1 6.7 %collective-permute-start.23 = (bf16[48,1152]{1,0:T(8,128)(2,1)S(1)}, bf16[48,1152]{1,0:T(8,128)(2,1)}, u32[]{:S(2)}, u32[]{:S(2)}) collective-permute-start(bf16[48,1152]{1,0:T(8,128)(2,1)S(1)} %get-tuple-element.164), channel_id=1, source_target_pairs={{0,24},{8,0},{16,8},{24,16},{1,25},{9,1},{17,9},{25,17},{2,26},{10... | collective-permute-start | bytes 331784 | tf_op jit(solution)/shard_map/ppermute | solution.py:685
  287.7 5.6 %collective-permute-start.26 = (bf16[48,1920]{1,0:T(8,128)(2,1)S(1)}, bf16[48,1920]{1,0:T(8,128)(2,1)S(1)}, u32[]{:S(2)}, u32[]{:S(2)}) collective-permute-start(bf16[48,1920]{1,0:T(8,128)(2,1)S(1)} %dynamic-slice_bitcast_fusion.4), channel_id=1, source_target_pairs={{0,1},{1,0},{2,3},{3,2},{4,5},{5,4},{6,7},{7,6},{8,9},{9,8},{10,11... | collective-permute-start | bytes 552968 | tf_op jit(solution)/shard_map/ppermute | solution.py:685
  290.6 4.2 %copy-start.1 = (s32[2,512,512]{2,1,0:T(8,128)S(1)}, s32[2,512,512]{2,1,0:T(8,128)}, u32[]{:S(2)}) copy-start(s32[2,512,512]{2,1,0:T(8,128)} %param.21) | copy-start | bytes 6291460
  (10 other events, 16.3 us)
Sparse Core Ops, SparseCore 0:
  11.5 93.7 all-gather.2
  166.4 94.1 reduce-scatter.1
